TPU v7x, 128 devices: a whole 4x4x4 slice. The times are simulated.
128 devices in a mesh: tm: 16 (over x, z), chan: 8 (over y, core).
Axes of the slice: x: 4, y: 4, z: 4, core: 2. Of those that a mesh axis runs over, the one named last changes fastest.
Arguments:
- samples: float32 [8192, 65536], P('chan', 'tm'), as said below
- omega: float32 [4, 8192, 128], P(None, 'chan'), may hold values from -0.03125 to 0.03125
Outputs:
- basis: float32 [128, 65536], P(None, ('tm', 'chan'))
- projection: float32 [4, 8192, 128], P(None, 'chan')
Inputs may be any that keep to these rules, and one draw needn't show every extreme that they name: The samples are real-valued (magnitude and angle channels of the phasor stream).
All inputs are finite; a program needn't handle non-finite values.
Results may differ from a plain program's by a relative error of at most 0.0001.
Values sent between devices are 32-bit elements; how exact they have to be, the bound alone decides.
No kernel may reach another device: no remote copies, remote signals or barrier semaphores. Data moves between devices by JAX's collectives and lax.ppermute only.
A program may use at most 128 MiB of HBM per device.

v0:
```python
import math

import jax
import jax.numpy as jnp
from jax import lax
from jax.sharding import PartitionSpec as P

LAG = 512


def passed_along(value, axis, steps):
    count = lax.axis_size(axis)
    initial, last = (max(0, -steps), min(count, count - steps))
    return lax.ppermute(value, axis, [(source, source + steps) for source in range(initial, last)])


def shards(samples, omega):
    chan_rows, block = samples.shape
    delays = omega.shape[0]
    total = block * lax.axis_size("tm")
    margin = (delays - 1) * LAG
    rim = passed_along(samples[:, :margin], "tm", -1)
    extended = jnp.concatenate([samples, rim], 1)
    windows = [lax.slice_in_dim(extended, d * LAG, d * LAG + block, axis=1) for d in range(delays)]
    partial_value = None
    for d in range(delays):
        term = lax.dot_general(
            omega[d],
            windows[d],
            (((0,), (0,)), ((), ())),
            precision=lax.Precision.HIGHEST,
            preferred_element_type=jnp.float32,
        )
        partial_value = term if partial_value is None else partial_value + term
    share_width = block // lax.axis_size("chan")
    sketch = lax.psum(partial_value, "chan")
    gram = lax.psum(
        jnp.dot(
            sketch, sketch.T, precision=lax.Precision.HIGHEST, preferred_element_type=jnp.float32
        ),
        "tm",
    )
    lower = jnp.linalg.cholesky(gram)
    rows = lax.linalg.triangular_solve(lower, sketch, left_side=True, lower=True)
    mine = lax.dynamic_slice_in_dim(rows, lax.axis_index("chan") * share_width, share_width, 1)
    local = jnp.stack(
        [
            lax.dot_general(
                windows[d],
                rows,
                (((1,), (1,)), ((), ())),
                precision=lax.Precision.HIGHEST,
                preferred_element_type=jnp.float32,
            )
            for d in range(delays)
        ],
        0,
    )
    projection = lax.psum(local, "tm")
    return (mine * math.sqrt(total), projection)


def solution(mesh):
    return jax.shard_map(
        shards,
        mesh=mesh,
        in_specs=(P("chan", "tm"), P(None, "chan", None)),
        out_specs=(P(None, ("tm", "chan")), P(None, "chan", None)),
        check_vma=False,
    )
```

profile of v0, /device:TPU:0, one launch (start us, length us, event | category | flops | bytes accessed | tf_op | source)
XLA Modules:
  0.0 555.7 jit_solution(16777351636337844287)
XLA Ops:
  7.2 0.0 all-reduce.4.cloned.1.call-start
  7.2 5.9 %slice.35 = f32[1024,1536]{1,0:T(8,128)} slice(f32[1024,4096]{1,0:T(8,128)} %param.2), slice={[0:1024], [0:1536]} | slice | bytes 12582912 | tf_op jit(solution)/shard_map/slice | solution.py:22
  13.1 1.3 collective-permute-start
  14.4 13.5 %fusion.42 = f32[128,4096]{1,0:T(8,128)} fusion(f32[1024,4096]{1,0:T(8,128)} %param.2, f32[4,1024,128]{2,1,0:T(8,128)} %param.3), kind=kOutput, calls=%fused_computation.26 | convolution fusion | flops 6442450944 | bytes 19398656 | tf_op jit(solution)/shard_map/dot_general | solution.py:27
  27.8 6.9 %constant_dynamic-update-slice_fusion.1 = f32[1024,5632]{1,0:T(8,128)S(1)} fusion(f32[1024,4096]{1,0:T(8,128)} %param.2), kind=kLoop, calls=%fused_computation.43 | loop fusion | bytes 33554432
  34.7 118.1 %collective-permute-done = f32[1024,1536]{1,0:T(8,128)} collective-permute-done((f32[1024,1536]{1,0:T(8,128)}, f32[1024,1536]{1,0:T(8,128)}, u32[]{:S(2)}, u32[]{:S(2)}) %collective-permute-start) | collective-permute-done | bytes 6291488 | tf_op jit(solution)/shard_map/ppermute | solution.py:14
  152.8 3.2 constant_dynamic-update-slice_fusion
  156.0 0.0 copy-start
  156.1 12.3 %fusion.18 = f32[128,4096]{1,0:T(8,128)} fusion(f32[1024,5632]{1,0:T(8,128)S(1)} %constant_dynamic-update-slice_fusion, f32[4,1024,128]{2,1,0:T(8,128)} %param.3), kind=kOutput, calls=%fused_computation.14 | convolution fusion | flops 6442450944 | bytes 19398656 | tf_op jit(solution)/shard_map/dot_general | solution.py:27
  168.3 12.5 %fusion.24 = f32[128,4096]{1,0:T(8,128)} fusion(f32[128,4096]{1,0:T(8,128)} %fusion.42, f32[1024,5632]{1,0:T(8,128)S(1)} %constant_dynamic-update-slice_fusion, f32[4,1024,128]{2,1,0:T(8,128)} %param.3), kind=kOutput, calls=%fused_computation.16 | convolution fusion | flops 6442975232 | bytes 21495808 | tf_op jit(solution)/shard_map/dot_general | solution.py:27
  180.8 0.0 copy-done
  180.8 12.4 %fusion.27 = f32[128,4096]{1,0:T(8,128)} fusion(f32[128,4096]{1,0:T(8,128)} %fusion.18, f32[128,4096]{1,0:T(8,128)} %fusion.24, f32[1024,5632]{1,0:T(8,128)S(1)} %constant_dynamic-update-slice_fusion, f32[4,1024,128]{2,1,0:T(8,128)} %param.3), kind=kOutput, calls=%fused_computation.17 | convolution fusion | flops 6443499520 | bytes 23592960 | tf_op jit(solution)/shard_map/dot_general | solution.py:27
  193.3 0.0 all-reduce.4.cloned.1.call-update
  193.3 0.0 all-reduce.6.cloned.1.call-start
  193.4 70.1 %all-reduce.4.cloned.1.call-done = f32[128,4096]{1,0:T(8,128)} async-done(((f32[128,4096]{1,0:T(8,128)}), f32[128,4096]{1,0:T(8,128)}) %all-reduce.4.cloned.1.call-update) | async-done | bytes 2097168 | tf_op jit(solution)/shard_map/psum | solution.py:36
  263.5 4.7 fusion.52
  268.1 0.0 all-reduce.6.cloned.1.call-update
  268.2 0.2 all-reduce.8.cloned.1.call-start
  268.4 80.4 %all-reduce.6.cloned.1.call-done = f32[128,128]{0,1:T(8,128)} async-done(((f32[128,128]{0,1:T(8,128)}), f32[128,128]{0,1:T(8,128)}) %all-reduce.6.cloned.1.call-update) | async-done | bytes 65552 | tf_op jit(solution)/shard_map/psum | solution.py:37
  348.8 0.9 copy.8
  349.8 0.9 fusion.51
  350.6 11.7 %cholesky.16 = f32[128,128]{1,0:T(8,128)S(1)} custom-call(f32[128,128]{1,0:T(8,128)S(1)} %fusion.51), custom_call_target="Cholesky" | custom-call | tf_op jit(solution)/shard_map/jit(cholesky)/cholesky | solution.py:43
  362.4 0.6 compare_reduce_fusion
  363.0 0.7 fusion.48
  363.7 9.8 %custom-call.6 = f32[1,128,128]{1,2,0:T(8,128)S(1)} custom-call(f32[1,128,128]{2,1,0:T(8,128)S(1)} %fusion.48), custom_call_target="InvertDiagBlocksLowerTriangular" | custom-call | tf_op jit(solution)/shard_map/triangular_solve | solution.py:44
  373.5 3.5 fusion.49
  377.0 0.0 copy-start.1
  377.0 21.4 %fusion.30 = f32[1,1024,128]{1,2,0:T(8,128)S(1)} fusion(f32[128,4096]{1,0:T(8,128)S(1)} %fusion.49, f32[1024,5632]{1,0:T(8,128)} %copy-done), kind=kOutput, calls=%fused_computation.19 | convolution fusion | flops 6442450944 | bytes 19398656 | tf_op jit(solution)/shard_map/dot_general | solution.py:48
  398.4 0.0 copy-done.1
  398.4 17.6 %fusion.33 = f32[1,1024,128]{1,2,0:T(8,128)S(1)} fusion(f32[128,4096]{1,0:T(8,128)S(1)} %fusion.49, f32[1024,5632]{1,0:T(8,128)S(1)} %copy-done.1), kind=kOutput, calls=%fused_computation.20 | convolution fusion | flops 6442450944 | bytes 19398656 | tf_op jit(solution)/shard_map/dot_general | solution.py:48
  416.0 17.7 %fusion.36 = f32[1,1024,128]{1,2,0:T(8,128)S(1)} fusion(f32[128,4096]{1,0:T(8,128)S(1)} %fusion.49, f32[1024,5632]{1,0:T(8,128)S(1)} %copy-done.1), kind=kOutput, calls=%fused_computation.21 | convolution fusion | flops 6442450944 | bytes 19398656 | tf_op jit(solution)/shard_map/dot_general | solution.py:48
  433.7 21.1 %convolution_bitcast_fusion = f32[1,1024,128]{1,2,0:T(8,128)S(1)} fusion(f32[128,4096]{1,0:T(8,128)S(1)} %fusion.49, f32[1024,4096]{1,0:T(8,128)} %param.2), kind=kOutput, calls=%fused_computation.22 | convolution fusion | flops 6442450944 | bytes 19398656 | tf_op jit(solution)/shard_map/dot_general | solution.py:48
  454.8 1.5 pad_maximum_fusion
  456.3 0.0 all-reduce.8.cloned.1.call-update
  456.3 0.7 dynamic-slice_multiply_fusion
  457.1 89.0 %all-reduce.8.cloned.1.call-done = f32[4,1024,128]{1,2,0:T(8,128)} async-done(((f32[4,1024,128]{1,2,0:T(8,128)}), f32[4,1024,128]{1,2,0:T(8,128)}) %all-reduce.8.cloned.1.call-update) | async-done | bytes 2097168 | tf_op jit(solution)/shard_map/psum | solution.py:59
  546.0 2.9 copy.12
  (1 shorter events, 0.0 us)
Async XLA Ops:
  7.2 256.3 %all-reduce.4.cloned.1.call-start = ((), (), s32[]{:S(2)}) async-start(), calls=%async_computation | async-start | bytes 4194304 | tf_op jit(solution)/shard_map/psum | solution.py:36
  13.1 139.7 %collective-permute-start = (f32[1024,1536]{1,0:T(8,128)}, f32[1024,1536]{1,0:T(8,128)}, u32[]{:S(2)}, u32[]{:S(2)}) collective-permute-start(f32[1024,1536]{1,0:T(8,128)} %slice.35), channel_id=1, source_target_pairs={{8,0},{16,8},{24,16},{32,24},{40,32},{48,40},{56,48},{64,56},{72,6... | collective-permute-start | bytes 18874376 | tf_op jit(solution)/shard_map/ppermute | solution.py:14
  156.0 24.8 %copy-start = (f32[1024,5632]{1,0:T(8,128)}, f32[1024,5632]{1,0:T(8,128)S(1)}, u32[]{:S(2)}) copy-start(f32[1024,5632]{1,0:T(8,128)S(1)} %constant_dynamic-update-slice_fusion) | copy-start | bytes 69206016
  193.3 155.5 %all-reduce.6.cloned.1.call-start = ((), (), s32[]{:S(2)}) async-start(), calls=%async_computation.1 | async-start | bytes 131072 | tf_op jit(solution)/shard_map/psum | solution.py:37
  268.2 277.9 %all-reduce.8.cloned.1.call-start = ((), (), s32[]{:S(2)}) async-start(), calls=%async_computation.2 | async-start | bytes 4194304 | tf_op jit(solution)/shard_map/psum | solution.py:59
  377.0 21.4 %copy-start.1 = (f32[1024,5632]{1,0:T(8,128)S(1)}, f32[1024,5632]{1,0:T(8,128)}, u32[]{:S(2)}) copy-start(f32[1024,5632]{1,0:T(8,128)} %copy-done) | copy-start | bytes 69206016
Sparse Core Ops, SparseCore 0:
  193.4 69.9 all-reduce.3
  268.3 80.4 all-reduce.5
  456.5 89.5 all-reduce.7
where the time goes:
time: 560 us; the launch traced here: 556 us
  waiting for transfers between devices  358 us (64%)
  matrix products  137 us (24%)
  other arithmetic  25.9 us (5%)
  local copies, waits for them, and re-layouts  19.8 us (4%)
  between operations  14.1 us (3%)
    ppermute x1, waiting for transfers between devices, passed_along(): lax.ppermute(value, axis, [(source, source + steps) for source in range(i...  118 us
    psum x1, waiting for transfers between devices, shards(): projection = lax.psum(local, 'tm')  89 us
    psum x1, waiting for transfers between devices, shards(): lax.psum(jnp.dot(sketch, sketch.T, precision=lax.Precision.HIGHEST, prefe...  80.4 us
    dot_general x4, matrix products, shards(): lax.dot_general(windows[d], rows, (((1,), (1,)), ((), ())), precision=lax...  77.8 us
    psum x1, waiting for transfers between devices, shards(): sketch = lax.psum(partial_value, 'chan')  70.1 us
    dot_general x4, matrix products, shards(): lax.dot_general(omega[d], windows[d], (((0,), (0,)), ((), ())), precision...  50.7 us
    another operation x3, other arithmetic, shards(): lower = jnp.linalg.cholesky(gram)  12.4 us
  transfers between devices with their start and end apart: 4, of which 4 were waited for; matrix products, arithmetic and copies ran while one was open for 4% of the time, Pallas kernels for 0%

commit v1 on v0

v1 whole, which is shorter than its diff:
```python
import functools
import math

import jax
import jax.numpy as jnp
from jax import lax
from jax.experimental import pallas as pl
from jax.experimental.pallas import tpu as pltpu
from jax.sharding import Mesh
from jax.sharding import PartitionSpec as P

LAG = 512
F32 = jnp.float32
BF16 = jnp.bfloat16
NT = (((1,), (1,)), ((), ()))
NN = (((1,), (0,)), ((), ()))
MIB = 1024 * 1024


def split(value):
    high = value.astype(BF16)
    return high, (value - high.astype(F32)).astype(BF16)


def dot3(a_high, a_low, b_high, b_low, dims):
    dot = functools.partial(lax.dot_general, dimension_numbers=dims, preferred_element_type=F32)
    return dot(a_high, b_high) + (dot(a_high, b_low) + dot(a_low, b_high))


def whole(count):
    return [pl.BlockSpec(memory_space=pltpu.VMEM)] * count


def call(body, outs, args, limit=24):
    return pl.pallas_call(
        body,
        out_shape=[jax.ShapeDtypeStruct(shape, F32) for shape in outs],
        in_specs=whole(len(args)),
        out_specs=whole(len(outs)),
        compiler_params=pltpu.CompilerParams(vmem_limit_bytes=limit * MIB),
    )(*args)


def moved(value, axes, offset):
    count = lax.axis_size(axes)
    return lax.ppermute(value, axes, [(i, (i + offset) % count) for i in range(count)])


def shifted(value, axes, offset):
    count = lax.axis_size(axes)
    pairs = [(i, i + offset) for i in range(count) if 0 <= i + offset < count]
    return lax.ppermute(value, axes, pairs)


def sketch_partial(samples, omega):
    delays, channels, rank = omega.shape
    block = samples.shape[1]
    steps = block // LAG
    margin = (delays - 1) * LAG
    half = rank // 2

    def body(s_ref, o_ref, keep_ref, send_ref, high_ref, low_ref, acc_ref):
        step = pl.program_id(0)

        @pl.when(step == 0)
        def _():
            for d in range(delays):
                high, low = split(o_ref[d].T)
                high_ref[d * rank : (d + 1) * rank, :] = high
                low_ref[d * rank : (d + 1) * rank, :] = low
            acc_ref[...] = jnp.zeros_like(acc_ref)

        s_high, s_low = split(s_ref[...])
        term = dot3(high_ref[...], low_ref[...], s_high, s_low, NN)
        for d in range(delays):
            at = pl.ds(pl.multiple_of((step + delays - 1 - d) * LAG, LAG), LAG)
            acc_ref[:, at] += term[d * rank : (d + 1) * rank, :]

        @pl.when(step == steps - 1)
        def _():
            core = lax.axis_index("core")
            keep_ref[...] = acc_ref[pl.ds(pl.multiple_of(core * half, half), half), :]
            send_ref[...] = acc_ref[pl.ds(pl.multiple_of((1 - core) * half, half), half), :]

    out = jax.ShapeDtypeStruct((half, margin + block), F32)
    spec = pl.BlockSpec((half, margin + block), lambda i: (0, 0))
    return pl.pallas_call(
        body,
        grid=(steps,),
        out_shape=[out, out],
        in_specs=[
            pl.BlockSpec((channels, LAG), lambda i: (0, i)),
            pl.BlockSpec(omega.shape, lambda i: (0, 0, 0)),
        ],
        out_specs=[spec, spec],
        scratch_shapes=[
            pltpu.VMEM((delays * rank, channels), BF16),
            pltpu.VMEM((delays * rank, channels), BF16),
            pltpu.VMEM((rank, margin + block), F32),
        ],
        compiler_params=pltpu.CompilerParams(vmem_limit_bytes=40 * MIB),
        cost_estimate=pl.CostEstimate(
            flops=6 * delays * rank * channels * block, bytes_accessed=samples.size * 4, transcendentals=0
        ),
    )(samples, omega)


def projection_partial(samples, mine, other, delays):
    channels, block = samples.shape
    half, width = mine.shape
    rank = 2 * half
    steps = block // LAG
    piece = channels // 8
    lanes = delays * rank
    gram_rows = rank // delays

    def body(s_ref, mine_ref, other_ref, *refs):
        outs = refs[:8]
        high_ref, low_ref, acc_ref, gram_ref = refs[8:]
        step = pl.program_id(0)

        @pl.when(step == 0)
        def _():
            core = lax.axis_index("core")
            for ref, place in ((mine_ref, core), (other_ref, 1 - core)):
                high, low = split(ref[...])
                at = pl.ds(pl.multiple_of(place * half, half), half)
                high_ref[at, :] = high
                low_ref[at, :] = low
            acc_ref[...] = jnp.zeros_like(acc_ref)
            gram_ref[...] = jnp.zeros_like(gram_ref)

        s_high, s_low = split(s_ref[...])
        highs, lows = [], []
        for d in range(delays):
            at = pl.ds(pl.multiple_of((step + delays - 1 - d) * LAG, LAG), LAG)
            highs.append(high_ref[:, at])
            lows.append(low_ref[:, at])
        gram_ref[...] += dot3(highs[0], lows[0], highs[0], lows[0], NT)
        acc_ref[...] += dot3(s_high, s_low, jnp.concatenate(highs, 0), jnp.concatenate(lows, 0), NT)

        @pl.when(step == steps - 1)
        def _():
            for route, axis in enumerate(("x", "z")):
                here = lax.axis_index(axis)
                for k in range(4):
                    row = route * 4 * piece + lax.rem(here + k, 4) * piece
                    outs[route * 4 + k][:piece, :] = acc_ref[pl.ds(pl.multiple_of(row, piece), piece), :]
            for k in range(4):
                for d in range(delays):
                    outs[k][piece:, d * rank : (d + 1) * rank] = gram_ref[d * gram_rows : (d + 1) * gram_rows, :]

    shapes = [(piece + gram_rows, lanes)] * 4 + [(piece, lanes)] * 4
    return pl.pallas_call(
        body,
        grid=(steps,),
        out_shape=[jax.ShapeDtypeStruct(s, F32) for s in shapes],
        in_specs=[
            pl.BlockSpec((channels, LAG), lambda i: (0, i)),
            pl.BlockSpec((half, width), lambda i: (0, 0)),
            pl.BlockSpec((half, width), lambda i: (0, 0)),
        ],
        out_specs=[pl.BlockSpec(s, lambda i: (0, 0)) for s in shapes],
        scratch_shapes=[
            pltpu.VMEM((rank, width), BF16),
            pltpu.VMEM((rank, width), BF16),
            pltpu.VMEM((channels, lanes), F32),
            pltpu.VMEM((rank, rank), F32),
        ],
        compiler_params=pltpu.CompilerParams(vmem_limit_bytes=40 * MIB),
        cost_estimate=pl.CostEstimate(
            flops=6 * lanes * channels * block, bytes_accessed=samples.size * 4, transcendentals=0
        ),
    )(samples, mine, other)


def shards(samples, omega):
    delays, channels, rank = omega.shape
    block = samples.shape[1]
    margin = (delays - 1) * LAG
    width = margin + block
    half, share = rank // 2, rank // 8
    total = block * lax.axis_size(("x", "z"))

    keep, send = sketch_partial(samples, omega)
    came = moved(send, "core", 1)

    def add_cores(a_ref, b_ref, *outs):
        y = lax.axis_index("y")
        for k in range(4):
            at = pl.ds(pl.multiple_of(lax.rem(y + k, 4) * share, share), share)
            outs[k][...] = a_ref[at, :] + b_ref[at, :]

    parts = call(add_cores, [(share, width)] * 4, [keep, came])
    parts = [parts[0]] + [moved(parts[k], "y", k) for k in (1, 2, 3)]

    def add_chips(a_ref, b_ref, c_ref, d_ref, main_ref, rim_ref):
        value = (a_ref[...] + b_ref[...]) + (c_ref[...] + d_ref[...])
        main_ref[...] = value[:, margin:]
        rim_ref[...] = value[:, :margin]

    main, rim = call(add_chips, [(share, block), (share, margin)], parts)
    rim = shifted(rim, ("x", "z"), -1)

    def add_rim(main_ref, rim_ref, out_ref, last_ref):
        out_ref[...] = main_ref[...]
        value = main_ref[:, block - margin :] + rim_ref[...]
        out_ref[:, block - margin :] = value
        last_ref[...] = value

    main, last = call(add_rim, [(share, block), (share, margin)], [main, rim])
    before = shifted(last, ("x", "z"), 1)

    def join(before_ref, main_ref, out_ref):
        out_ref[:, :margin] = before_ref[...]
        out_ref[:, margin:] = main_ref[...]

    (own,) = call(join, [(share, width)], [before, main])
    rows = [own] + [moved(own, "y", k) for k in (1, 2, 3)]

    def order(a_ref, b_ref, c_ref, d_ref, out_ref):
        y = lax.axis_index("y")
        for k, ref in enumerate((a_ref, b_ref, c_ref, d_ref)):
            at = pl.ds(pl.multiple_of(lax.rem(y - k + 4, 4) * share, share), share)
            out_ref[at, :] = ref[...]

    (mine,) = call(order, [(half, width)], rows)
    other = moved(mine, "core", 1)

    pieces = projection_partial(samples, mine, other, delays)
    first = [pieces[0]] + [moved(pieces[k], "x", k) for k in (1, 2, 3)]
    second = [pieces[4]] + [moved(pieces[4 + k], "z", k) for k in (1, 2, 3)]
    piece, lanes = channels // 8, delays * rank
    quarter = piece // 4
    gram_rows = rank // delays

    def add_first(*refs):
        ins, outs = refs[:8], refs[8:]
        value = (ins[0][...] + ins[1][...]) + (ins[2][...] + ins[3][...])
        outs[0][...] = value
        value = (ins[4][...] + ins[5][...]) + (ins[6][...] + ins[7][...])
        outs[1][...] = value
        z, x = lax.axis_index("z"), lax.axis_index("x")
        for k in range(4):
            at = pl.ds(pl.multiple_of(lax.rem(z + k, 4) * quarter, quarter), quarter)
            outs[2 + k][:quarter, :] = outs[0][at, :]
            outs[2 + k][quarter:, :] = outs[0][piece:, :]
            at = pl.ds(pl.multiple_of(lax.rem(x + k, 4) * quarter, quarter), quarter)
            outs[6 + k][...] = outs[1][at, :]

    sums = call(
        add_first,
        [(piece + gram_rows, lanes), (piece, lanes)]
        + [(quarter + gram_rows, lanes)] * 4
        + [(quarter, lanes)] * 4,
        first + second,
    )[2:]
    first = [sums[0]] + [moved(sums[k], "z", k) for k in (1, 2, 3)]
    second = [sums[4]] + [moved(sums[4 + k], "x", k) for k in (1, 2, 3)]

    def add_second(*refs):
        ins, (one_ref, two_ref, gram_ref) = refs[:8], refs[8:]
        value = (ins[0][...] + ins[1][...]) + (ins[2][...] + ins[3][...])
        one_ref[...] = value[:quarter, :]
        for d in range(delays):
            gram_ref[d * gram_rows : (d + 1) * gram_rows, :] = value[quarter:, d * rank : (d + 1) * rank]
        two_ref[...] = (ins[4][...] + ins[5][...]) + (ins[6][...] + ins[7][...])

    one, two, gram = call(
        add_second, [(quarter, lanes), (quarter, lanes), (rank, rank)], first + second
    )
    first = [one] + [moved(one, "z", k) for k in (1, 2, 3)]
    second = [two] + [moved(two, "x", k) for k in (1, 2, 3)]

    def arrange(*refs):
        ins, outs = refs[:8], refs[8:]
        for route, axis in enumerate(("z", "x")):
            here = lax.axis_index(axis)
            for k in range(4):
                at = pl.ds(pl.multiple_of(lax.rem(here - k + 4, 4) * quarter, quarter), quarter)
                outs[route][at, :] = ins[route * 4 + k][...]

    one, two = call(arrange, [(piece, lanes)] * 2, first + second)
    first = [one] + [moved(one, "x", k) for k in (1, 2, 3)]
    second = [two] + [moved(two, "z", k) for k in (1, 2, 3)]

    lower = jnp.linalg.cholesky(gram)
    inverse = lax.linalg.triangular_solve(lower, jnp.eye(rank, dtype=F32), left_side=True, lower=True)

    def finish(*refs):
        inverse_ref, mine_ref, other_ref = refs[:3]
        ins, (basis_ref, out_ref) = refs[3:11], refs[11:]
        high, low = split(inverse_ref[...])
        for route, axis in enumerate(("x", "z")):
            here = lax.axis_index(axis)
            for k in range(4):
                row = route * 4 * piece + lax.rem(here - k + 4, 4) * piece
                at = pl.ds(pl.multiple_of(row, piece), piece)
                for d in range(delays):
                    a_high, a_low = split(ins[route * 4 + k][:, d * rank : (d + 1) * rank])
                    out_ref[d, at, :] = dot3(a_high, a_low, high, low, NT)
        core, y = lax.axis_index("core"), lax.axis_index("y")
        columns = block // 8
        at = pl.ds(pl.multiple_of(margin + (y * 2 + core) * columns, columns), columns)
        sketch = jnp.concatenate([mine_ref[:, at], other_ref[:, at]], 0)
        swapped = jnp.concatenate([other_ref[:, at], mine_ref[:, at]], 0)
        sketch = jnp.where(core == 0, sketch, swapped)
        s_high, s_low = split(sketch)
        basis_ref[...] = math.sqrt(total) * dot3(high, low, s_high, s_low, NN)

    basis, projection = call(
        finish,
        [(rank, block // 8), (delays, channels, rank)],
        [inverse, mine, other] + first + second,
        40,
    )
    return basis, projection


def solution(mesh):
    fine = Mesh(mesh.devices.reshape(4, 4, 4, 2), ("x", "z", "y", "core"))
    tm, chan = ("x", "z"), ("y", "core")
    return jax.shard_map(
        shards,
        mesh=fine,
        in_specs=(P(chan, tm), P(None, chan, None)),
        out_specs=(P(None, tm + chan), P(None, chan, None)),
        check_vma=False,
    )
```

time: 560 us -> 194 us (0.35)
  waiting for transfers between devices: 358 us -> 60.4 us
  matrix products: 137 us -> 0.25 us
  starting transfers between devices: 1.58 us -> 54.3 us
  Pallas kernels: 0 us -> 41.7 us
  between operations: 14.1 us -> 0.84 us
  local copies, waits for them, and re-layouts: 19.8 us -> 11.3 us
    psum x3 -> x0, waiting for transfers between devices: 239 us -> none  [the longest x1 89 us: shards(): projection = lax.psum(local, 'tm')]
    dot_general x9 -> x0, matrix products: 133 us -> none  [the longest x4 77.8 us: shards(): lax.dot_general(windows[d], rows, (((1,), (1,)), ((), ())), precision=lax...]
    ppermute x1 -> x34, waiting for transfers between devices: 118 us -> 60.4 us  [the longest x32 53 us: moved(): lax.ppermute(value, axes, [(i, (i + offset) % count) for i in range(count)])]
    ppermute x1 -> x34, starting transfers between devices: 1.28 us -> 54.3 us  [the longest x32 49.2 us: moved(): lax.ppermute(value, axes, [(i, (i + offset) % count) for i in range(count)])]
    pallas_call x0 -> x11, Pallas kernels: none -> 41.7 us  [the longest x1 18.2 us: projection_partial(): pl.pallas_call(body, grid=(steps,), out_shape=[jax.ShapeDtypeStruct(s, F3...]
    slice x1 -> x0, local copies, waits for them, and re-layouts: 5.89 us -> none  [shards(): rim = passed_along(samples[:, :margin], 'tm', -1)]
    another operation x3 -> x2, other arithmetic: 12 us -> 10.5 us  [shards(): lax.linalg.triangular_solve(lower, jnp.eye(rank, dtype=F32), left_side=Tr...]
  transfers between devices with their start and end apart: 4 -> 34, of which waited for: 4 -> 14; matrix products, arithmetic and copies ran while one was open for 4% -> 13% of each run, Pallas kernels for 0% -> 0%
where the time goes in v1:
time: 194 us; the launch traced here: 192 us
  waiting for transfers between devices  60.4 us (31%)
  starting transfers between devices  54.3 us (28%)
  Pallas kernels  41.7 us (21%)
  other arithmetic  23.7 us (12%)
  local copies, waits for them, and re-layouts  11.3 us (6%)
    ppermute x32, waiting for transfers between devices, moved(): lax.ppermute(value, axes, [(i, (i + offset) % count) for i in range(count)])  53 us
    ppermute x32, starting transfers between devices, moved(): lax.ppermute(value, axes, [(i, (i + offset) % count) for i in range(count)])  49.2 us
    pallas_call x1, Pallas kernels, projection_partial(): pl.pallas_call(body, grid=(steps,), out_shape=[jax.ShapeDtypeStruct(s, F3...  18.2 us
    pallas_call x1, Pallas kernels, sketch_partial(): pl.pallas_call(body, grid=(steps,), out_shape=[out, out], in_specs=[pl.Bl...  17 us
    another operation x3, other arithmetic, shards(): lower = jnp.linalg.cholesky(gram)  12.4 us
    unnamed x30, local copies, waits for them, and re-layouts  10.6 us
    another operation x2, other arithmetic, shards(): lax.linalg.triangular_solve(lower, jnp.eye(rank, dtype=F32), left_side=Tr...  10.5 us
    ppermute x2, waiting for transfers between devices, shifted(): return lax.ppermute(value, axes, pairs)  7.4 us
  transfers between devices with their start and end apart: 34, of which 14 were waited for; matrix products, arithmetic and copies ran while one was open for 13% of the time, Pallas kernels for 0%

profile of v1, /device:TPU:0, one launch (start us, length us, event | category | flops | bytes accessed | tf_op | source)
XLA Modules:
  0.0 192.5 jit_solution(16770166754568363939)
XLA Ops:
  0.6 1.6 copy-done.14
  2.2 17.0 %shard_map.41 = (f32[64,5632]{1,0:T(8,128)S(1)}, f32[64,5632]{1,0:T(8,128)S(1)}) custom-call(f32[1024,4096]{1,0:T(8,128)} %s_ref.3, f32[4,1024,128]{2,1,0:T(8,128)S(1)} %copy-done.14), custom_call_target="tpu_custom_call" | custom-call | flops 12884901888 | bytes 16777216 | tf_op jit(solution)/shard_map/pallas_call | solution.py:87
  19.4 3.2 %collective-permute-done.b_ref = f32[64,5632]{1,0:T(8,128)S(1)} collective-permute-done((f32[64,5632]{1,0:T(8,128)S(1)}, f32[64,5632]{1,0:T(8,128)S(1)}, u32[]{:S(2)}, u32[]{:S(2)}) %collective-permute-start) | collective-permute-done | bytes 1441824 | tf_op jit(solution)/shard_map/ppermute | solution.py:46
  22.7 1.7 collective-permute-start.1
  24.4 2.9 %collective-permute-start.2 = (f32[16,5632]{1,0:T(8,128)S(1)}, f32[16,5632]{1,0:T(8,128)S(1)}, u32[]{:S(2)}, u32[]{:S(2)}) collective-permute-start(f32[16,5632]{1,0:T(8,128)S(1)} %get-tuple-element.37), channel_id=1, source_target_pairs={{0,4},{2,6},{4,0},{6,2},{1,5},{3,7},{5,1},{7,3},{8,12},{10,14},{12... | collective-permute-start | bytes 1081352 | tf_op jit(solution)/shard_map/ppermute | solution.py:46
  27.4 1.3 collective-permute-start.3
  28.7 5.9 %collective-permute-done.1.b_ref = f32[16,5632]{1,0:T(8,128)S(1)} collective-permute-done((f32[16,5632]{1,0:T(8,128)S(1)}, f32[16,5632]{1,0:T(8,128)S(1)}, u32[]{:S(2)}, u32[]{:S(2)}) %collective-permute-start.1) | collective-permute-done | bytes 360480 | tf_op jit(solution)/shard_map/ppermute | solution.py:46
  34.6 8.9 %collective-permute-done.2.c_ref = f32[16,5632]{1,0:T(8,128)S(1)} collective-permute-done((f32[16,5632]{1,0:T(8,128)S(1)}, f32[16,5632]{1,0:T(8,128)S(1)}, u32[]{:S(2)}, u32[]{:S(2)}) %collective-permute-start.2) | collective-permute-done | bytes 360480 | tf_op jit(solution)/shard_map/ppermute | solution.py:46
  43.6 1.3 collective-permute-start.4
  44.9 5.2 %collective-permute-done.4.rim_ref = f32[16,1536]{1,0:T(8,128)S(1)} collective-permute-done((f32[16,1536]{1,0:T(8,128)S(1)}, f32[16,1536]{1,0:T(8,128)S(1)}, u32[]{:S(2)}, u32[]{:S(2)}) %collective-permute-start.4) | collective-permute-done | bytes 98336 | tf_op jit(solution)/shard_map/ppermute | solution.py:52
  50.1 3.8 %collective-permute-start.5 = (f32[16,1536]{1,0:T(8,128)S(1)}, f32[16,1536]{1,0:T(8,128)S(1)}, u32[]{:S(2)}, u32[]{:S(2)}) collective-permute-start(f32[16,1536]{1,0:T(8,128)S(1)} %get-tuple-element.41), channel_id=1, source_target_pairs={{0,8},{8,16},{16,24},{24,32},{32,40},{40,48},{48,56},{56,64},{64,7... | collective-permute-start | bytes 294920 | tf_op jit(solution)/shard_map/ppermute | solution.py:52
  54.0 2.2 %collective-permute-done.5.before_ref = f32[16,1536]{1,0:T(8,128)S(1)} collective-permute-done((f32[16,1536]{1,0:T(8,128)S(1)}, f32[16,1536]{1,0:T(8,128)S(1)}, u32[]{:S(2)}, u32[]{:S(2)}) %collective-permute-start.5) | collective-permute-done | bytes 98336 | tf_op jit(solution)/shard_map/ppermute | solution.py:52
  56.2 2.5 %collective-permute-start.8 = (f32[16,5632]{1,0:T(8,128)S(1)}, f32[16,5632]{1,0:T(8,128)S(1)}, u32[]{:S(2)}, u32[]{:S(2)}) collective-permute-start(f32[16,5632]{1,0:T(8,128)S(1)} %shard_map.45.a_ref), channel_id=1, source_target_pairs={{0,6},{2,0},{4,2},{6,4},{1,7},{3,1},{5,3},{7,5},{8,14},{10,8},{12,... | collective-permute-start | bytes 1081352 | tf_op jit(solution)/shard_map/ppermute | solution.py:46
  58.7 0.9 collective-permute-start.7
  59.5 0.7 collective-permute-start.6
  60.2 12.5 %collective-permute-done.8.d_ref = f32[16,5632]{1,0:T(8,128)S(1)} collective-permute-done((f32[16,5632]{1,0:T(8,128)S(1)}, f32[16,5632]{1,0:T(8,128)S(1)}, u32[]{:S(2)}, u32[]{:S(2)}) %collective-permute-start.8) | collective-permute-done | bytes 360480 | tf_op jit(solution)/shard_map/ppermute | solution.py:46
  72.8 3.4 %collective-permute-done.6.b_ref = f32[16,5632]{1,0:T(8,128)S(1)} collective-permute-done((f32[16,5632]{1,0:T(8,128)S(1)}, f32[16,5632]{1,0:T(8,128)S(1)}, u32[]{:S(2)}, u32[]{:S(2)}) %collective-permute-start.6) | collective-permute-done | bytes 360480 | tf_op jit(solution)/shard_map/ppermute | solution.py:46
  76.4 3.2 %collective-permute-done.9.other_ref.refs_2_ = f32[64,5632]{1,0:T(8,128)S(1)} collective-permute-done((f32[64,5632]{1,0:T(8,128)S(1)}, f32[64,5632]{1,0:T(8,128)S(1)}, u32[]{:S(2)}, u32[]{:S(2)}) %collective-permute-start.9) | collective-permute-done | bytes 1441824 | tf_op jit(solution)/shard_map/ppermute | solution.py:46
  79.6 18.2 %shard_map.47 = (f32[160,512]{1,0:T(8,128)S(1)}, f32[160,512]{1,0:T(8,128)S(1)}, f32[160,512]{1,0:T(8,128)S(1)}, f32[160,512]{1,0:T(8,128)S(1)}, f32[128,512]{1,...) custom-call(f32[1024,4096]{1,0:T(8,128)} %s_ref.3, ...), custom_call_target="tpu_custom_call" | custom-call | flops 12884901888 | bytes 16777216 | tf_op jit(solution)/shard_map/pallas_call | solution.py:154
  97.8 2.2 %collective-permute-start.13 = (f32[128,512]{1,0:T(8,128)S(1)}, f32[128,512]{1,0:T(8,128)S(1)}, u32[]{:S(2)}, u32[]{:S(2)}) collective-permute-start(f32[128,512]{1,0:T(8,128)S(1)} %get-tuple-element.48), channel_id=1, source_target_pairs={{0,8},{8,16},{16,24},{24,0},{1,9},{9,17},{17,25},{25,1},{2,10},{10... | collective-permute-start | bytes 786440 | tf_op jit(solution)/shard_map/ppermute | solution.py:46
  100.0 3.6 %collective-permute-start.10 = (f32[160,512]{1,0:T(8,128)S(1)}, f32[160,512]{1,0:T(8,128)S(1)}, u32[]{:S(2)}, u32[]{:S(2)}) collective-permute-start(f32[160,512]{1,0:T(8,128)S(1)} %get-tuple-element.44), channel_id=1, source_target_pairs={{0,32},{32,64},{64,96},{96,0},{1,33},{33,65},{65,97},{97,1},{2,34}... | collective-permute-start | bytes 983048 | tf_op jit(solution)/shard_map/ppermute | solution.py:46
  103.6 3.0 %collective-permute-start.11 = (f32[160,512]{1,0:T(8,128)S(1)}, f32[160,512]{1,0:T(8,128)S(1)}, u32[]{:S(2)}, u32[]{:S(2)}) collective-permute-start(f32[160,512]{1,0:T(8,128)S(1)} %get-tuple-element.45), channel_id=1, source_target_pairs={{0,64},{32,96},{64,0},{96,32},{1,65},{33,97},{65,1},{97,33},{2,66}... | collective-permute-start | bytes 983048 | tf_op jit(solution)/shard_map/ppermute | solution.py:46
  106.6 1.1 collective-permute-start.12
  107.8 3.1 %collective-permute-start.14 = (f32[128,512]{1,0:T(8,128)S(1)}, f32[128,512]{1,0:T(8,128)S(1)}, u32[]{:S(2)}, u32[]{:S(2)}) collective-permute-start(f32[128,512]{1,0:T(8,128)S(1)} %get-tuple-element.49), channel_id=1, source_target_pairs={{0,16},{8,24},{16,0},{24,8},{1,17},{9,25},{17,1},{25,9},{2,18},{10... | collective-permute-start | bytes 786440 | tf_op jit(solution)/shard_map/ppermute | solution.py:46
  110.9 1.5 collective-permute-start.15
  112.5 4.7 %collective-permute-done.14.refs_6_ = f32[128,512]{1,0:T(8,128)S(1)} collective-permute-done((f32[128,512]{1,0:T(8,128)S(1)}, f32[128,512]{1,0:T(8,128)S(1)}, u32[]{:S(2)}, u32[]{:S(2)}) %collective-permute-start.14) | collective-permute-done | bytes 262176 | tf_op jit(solution)/shard_map/ppermute | solution.py:46
  117.2 5.5 %collective-permute-done.15.refs_7_ = f32[128,512]{1,0:T(8,128)S(1)} collective-permute-done((f32[128,512]{1,0:T(8,128)S(1)}, f32[128,512]{1,0:T(8,128)S(1)}, u32[]{:S(2)}, u32[]{:S(2)}) %collective-permute-start.15) | collective-permute-done | bytes 262176 | tf_op jit(solution)/shard_map/ppermute | solution.py:46
  122.7 0.9 shard_map.48
  123.6 0.9 collective-permute-start.19
  124.7 3.9 %collective-permute-start.17 = (f32[64,512]{1,0:T(8,128)S(1)}, f32[64,512]{1,0:T(8,128)S(1)}, u32[]{:S(2)}, u32[]{:S(2)}) collective-permute-start(f32[64,512]{1,0:T(8,128)S(1)} %get-tuple-element.53), channel_id=1, source_target_pairs={{0,16},{8,24},{16,0},{24,8},{1,17},{9,25},{17,1},{25,9},{2,18},{10... | collective-permute-start | bytes 393224 | tf_op jit(solution)/shard_map/ppermute | solution.py:46
  128.9 4.6 %collective-permute-start.20 = (f32[32,512]{1,0:T(8,128)S(1)}, f32[32,512]{1,0:T(8,128)S(1)}, u32[]{:S(2)}, u32[]{:S(2)}) collective-permute-start(f32[32,512]{1,0:T(8,128)S(1)} %get-tuple-element.57), channel_id=1, source_target_pairs={{0,64},{32,96},{64,0},{96,32},{1,65},{33,97},{65,1},{97,33},{2,66}... | collective-permute-start | bytes 196616 | tf_op jit(solution)/shard_map/ppermute | solution.py:46
  133.6 2.1 %collective-permute-done.20.refs_6_ = f32[32,512]{1,0:T(8,128)S(1)} collective-permute-done((f32[32,512]{1,0:T(8,128)S(1)}, f32[32,512]{1,0:T(8,128)S(1)}, u32[]{:S(2)}, u32[]{:S(2)}) %collective-permute-start.20) | collective-permute-done | bytes 65568 | tf_op jit(solution)/shard_map/ppermute | solution.py:46
  135.7 2.0 %collective-permute-done.21.refs_7_ = f32[32,512]{1,0:T(8,128)S(1)} collective-permute-done((f32[32,512]{1,0:T(8,128)S(1)}, f32[32,512]{1,0:T(8,128)S(1)}, u32[]{:S(2)}, u32[]{:S(2)}) %collective-permute-start.21) | collective-permute-done | bytes 65568 | tf_op jit(solution)/shard_map/ppermute | solution.py:46
  137.8 1.1 collective-permute-start.24
  138.9 3.0 %collective-permute-start.23 = (f32[32,512]{1,0:T(8,128)S(1)}, f32[32,512]{1,0:T(8,128)S(1)}, u32[]{:S(2)}, u32[]{:S(2)}) collective-permute-start(f32[32,512]{1,0:T(8,128)S(1)} %get-tuple-element.60.refs_0_), channel_id=1, source_target_pairs={{0,16},{8,24},{16,0},{24,8},{1,17},{9,25},{17,1},{25,9},{2,18},{10... | collective-permute-start | bytes 196616 | tf_op jit(solution)/shard_map/ppermute | solution.py:46
  141.9 0.5 collective-permute-start.22
  142.4 1.2 collective-permute-start.27
  143.6 0.5 collective-permute-start.26
  144.1 1.2 collective-permute-start.25
  145.3 0.7 copy.4
  146.1 0.6 copy-done.4
  146.7 0.7 collective-permute-done.22.refs_1_
  147.3 0.6 copy-done.6
  148.0 0.6 copy-done.8
  148.6 0.8 collective-permute-done.26.refs_6_
  149.4 0.6 copy-done.10
  150.1 0.6 copy-done.12
  150.7 0.8 copy-done.1
  151.5 0.8 copy-done.3
  152.4 0.8 copy-done.5
  153.2 0.8 copy-done.7
  154.1 0.8 copy-done.9
  154.9 0.8 copy-done.11
  155.7 0.8 copy-done.13
  156.6 1.4 collective-permute-start.30
  158.0 0.8 fusion.3
  158.8 11.7 %cholesky.17 = f32[128,128]{1,0:T(8,128)S(1)} custom-call(f32[128,128]{1,0:T(8,128)S(1)} %fusion.3), custom_call_target="Cholesky" | custom-call | tf_op jit(solution)/shard_map/jit(cholesky)/cholesky | solution.py:287
  170.6 0.6 compare_reduce_fusion
  171.2 1.5 collective-permute-start.29
  173.1 2.7 %collective-permute-start.33 = (f32[128,512]{1,0:T(8,128)S(1)}, f32[128,512]{1,0:T(8,128)}, u32[]{:S(2)}, u32[]{:S(2)}) collective-permute-start(f32[128,512]{1,0:T(8,128)S(1)} %get-tuple-element.63.refs_7_), channel_id=1, source_target_pairs={{0,24},{8,0},{16,8},{24,16},{1,25},{9,1},{17,9},{25,17},{2,26},{10... | collective-permute-start | bytes 786440 | tf_op jit(solution)/shard_map/ppermute | solution.py:46
  175.8 0.9 collective-permute-start.31
  176.7 0.7 fusion
  177.3 9.8 %custom-call.6 = f32[1,128,128]{1,2,0:T(8,128)S(1)} custom-call(f32[1,128,128]{2,1,0:T(8,128)S(1)} %fusion), custom_call_target="InvertDiagBlocksLowerTriangular" | custom-call | tf_op jit(solution)/shard_map/triangular_solve | solution.py:288
  187.4 5.0 %shard_map.51 = (f32[128,512]{1,0:T(8,128)}, f32[4,1024,128]{2,1,0:T(8,128)}) custom-call(f32[128,128]{1,0:T(8,128)S(1)} %fusion.1.refs_0_, f32[64,5632]{1,0:T(8,128)S(1)} %shard_map.46.mine_ref.refs_1_, f32[64,5632]{1,0:T(8,128)S(1)} %collective-permute-done.9.other_ref.refs_2_, f32[128,512]{1,0:T(8,128)S(1)} %get-tuple-element.62.refs_3_, ...), custom_call_target="tpu_custom_call" | custom-call | tf_op jit(solution)/shard_map/pallas_call | solution.py:35
  (53 shorter events, 2.0 us)
Async XLA Ops:
  0.6 1.6 copy-start.14
  19.3 3.3 %collective-permute-start = (f32[64,5632]{1,0:T(8,128)S(1)}, f32[64,5632]{1,0:T(8,128)S(1)}, u32[]{:S(2)}, u32[]{:S(2)}) collective-permute-start(f32[64,5632]{1,0:T(8,128)S(1)} %get-tuple-element.34), channel_id=1, source_target_pairs={{0,1},{1,0},{2,3},{3,2},{4,5},{5,4},{6,7},{7,6},{8,9},{9,8},{10,11... | collective-permute-start | bytes 4325384 | tf_op jit(solution)/shard_map/ppermute | solution.py:46
  22.7 11.9 %collective-permute-start.1 = (f32[16,5632]{1,0:T(8,128)S(1)}, f32[16,5632]{1,0:T(8,128)S(1)}, u32[]{:S(2)}, u32[]{:S(2)}) collective-permute-start(f32[16,5632]{1,0:T(8,128)S(1)} %get-tuple-element.36), channel_id=1, source_target_pairs={{0,2},{2,4},{4,6},{6,0},{1,3},{3,5},{5,7},{7,1},{8,10},{10,12},{12... | collective-permute-start | bytes 1081352 | tf_op jit(solution)/shard_map/ppermute | solution.py:46
  24.4 19.1 %collective-permute-start.2 = (f32[16,5632]{1,0:T(8,128)S(1)}, f32[16,5632]{1,0:T(8,128)S(1)}, u32[]{:S(2)}, u32[]{:S(2)}) collective-permute-start(f32[16,5632]{1,0:T(8,128)S(1)} %get-tuple-element.37), channel_id=1, source_target_pairs={{0,4},{2,6},{4,0},{6,2},{1,5},{3,7},{5,1},{7,3},{8,12},{10,14},{12... | collective-permute-start | bytes 1081352 | tf_op jit(solution)/shard_map/ppermute | solution.py:46
  27.4 16.2 %collective-permute-start.3 = (f32[16,5632]{1,0:T(8,128)S(1)}, f32[16,5632]{1,0:T(8,128)S(1)}, u32[]{:S(2)}, u32[]{:S(2)}) collective-permute-start(f32[16,5632]{1,0:T(8,128)S(1)} %get-tuple-element.38), channel_id=1, source_target_pairs={{0,6},{2,0},{4,2},{6,4},{1,7},{3,1},{5,3},{7,5},{8,14},{10,8},{12,... | collective-permute-start | bytes 1081352 | tf_op jit(solution)/shard_map/ppermute | solution.py:46
  43.6 6.5 %collective-permute-start.4 = (f32[16,1536]{1,0:T(8,128)S(1)}, f32[16,1536]{1,0:T(8,128)S(1)}, u32[]{:S(2)}, u32[]{:S(2)}) collective-permute-start(f32[16,1536]{1,0:T(8,128)S(1)} %get-tuple-element.40), channel_id=1, source_target_pairs={{8,0},{16,8},{24,16},{32,24},{40,32},{48,40},{56,48},{64,56},{72,6... | collective-permute-start | bytes 294920 | tf_op jit(solution)/shard_map/ppermute | solution.py:52
  50.1 6.0 %collective-permute-start.5 = (f32[16,1536]{1,0:T(8,128)S(1)}, f32[16,1536]{1,0:T(8,128)S(1)}, u32[]{:S(2)}, u32[]{:S(2)}) collective-permute-start(f32[16,1536]{1,0:T(8,128)S(1)} %get-tuple-element.41), channel_id=1, source_target_pairs={{0,8},{8,16},{16,24},{24,32},{32,40},{40,48},{48,56},{56,64},{64,7... | collective-permute-start | bytes 294920 | tf_op jit(solution)/shard_map/ppermute | solution.py:52
  56.2 16.6 %collective-permute-start.8 = (f32[16,5632]{1,0:T(8,128)S(1)}, f32[16,5632]{1,0:T(8,128)S(1)}, u32[]{:S(2)}, u32[]{:S(2)}) collective-permute-start(f32[16,5632]{1,0:T(8,128)S(1)} %shard_map.45.a_ref), channel_id=1, source_target_pairs={{0,6},{2,0},{4,2},{6,4},{1,7},{3,1},{5,3},{7,5},{8,14},{10,8},{12,... | collective-permute-start | bytes 1081352 | tf_op jit(solution)/shard_map/ppermute | solution.py:46
  58.7 14.1 %collective-permute-start.7 = (f32[16,5632]{1,0:T(8,128)S(1)}, f32[16,5632]{1,0:T(8,128)S(1)}, u32[]{:S(2)}, u32[]{:S(2)}) collective-permute-start(f32[16,5632]{1,0:T(8,128)S(1)} %shard_map.45.a_ref), channel_id=1, source_target_pairs={{0,4},{2,6},{4,0},{6,2},{1,5},{3,7},{5,1},{7,3},{8,12},{10,14},{12... | collective-permute-start | bytes 1081352 | tf_op jit(solution)/shard_map/ppermute | solution.py:46
  59.5 16.7 %collective-permute-start.6 = (f32[16,5632]{1,0:T(8,128)S(1)}, f32[16,5632]{1,0:T(8,128)S(1)}, u32[]{:S(2)}, u32[]{:S(2)}) collective-permute-start(f32[16,5632]{1,0:T(8,128)S(1)} %shard_map.45.a_ref), channel_id=1, source_target_pairs={{0,2},{2,4},{4,6},{6,0},{1,3},{3,5},{5,7},{7,1},{8,10},{10,12},{12... | collective-permute-start | bytes 1081352 | tf_op jit(solution)/shard_map/ppermute | solution.py:46
  76.3 3.3 %collective-permute-start.9 = (f32[64,5632]{1,0:T(8,128)S(1)}, f32[64,5632]{1,0:T(8,128)S(1)}, u32[]{:S(2)}, u32[]{:S(2)}) collective-permute-start(f32[64,5632]{1,0:T(8,128)S(1)} %shard_map.46.mine_ref.refs_1_), channel_id=1, source_target_pairs={{0,1},{1,0},{2,3},{3,2},{4,5},{5,4},{6,7},{7,6},{8,9},{9,8},{10,11... | collective-permute-start | bytes 4325384 | tf_op jit(solution)/shard_map/ppermute | solution.py:46
  97.8 13.1 %collective-permute-start.13 = (f32[128,512]{1,0:T(8,128)S(1)}, f32[128,512]{1,0:T(8,128)S(1)}, u32[]{:S(2)}, u32[]{:S(2)}) collective-permute-start(f32[128,512]{1,0:T(8,128)S(1)} %get-tuple-element.48), channel_id=1, source_target_pairs={{0,8},{8,16},{16,24},{24,0},{1,9},{9,17},{17,25},{25,1},{2,10},{10... | collective-permute-start | bytes 786440 | tf_op jit(solution)/shard_map/ppermute | solution.py:46
  100.0 22.7 %collective-permute-start.10 = (f32[160,512]{1,0:T(8,128)S(1)}, f32[160,512]{1,0:T(8,128)S(1)}, u32[]{:S(2)}, u32[]{:S(2)}) collective-permute-start(f32[160,512]{1,0:T(8,128)S(1)} %get-tuple-element.44), channel_id=1, source_target_pairs={{0,32},{32,64},{64,96},{96,0},{1,33},{33,65},{65,97},{97,1},{2,34}... | collective-permute-start | bytes 983048 | tf_op jit(solution)/shard_map/ppermute | solution.py:46
  103.6 19.0 %collective-permute-start.11 = (f32[160,512]{1,0:T(8,128)S(1)}, f32[160,512]{1,0:T(8,128)S(1)}, u32[]{:S(2)}, u32[]{:S(2)}) collective-permute-start(f32[160,512]{1,0:T(8,128)S(1)} %get-tuple-element.45), channel_id=1, source_target_pairs={{0,64},{32,96},{64,0},{96,32},{1,65},{33,97},{65,1},{97,33},{2,66}... | collective-permute-start | bytes 983048 | tf_op jit(solution)/shard_map/ppermute | solution.py:46
  106.6 16.0 %collective-permute-start.12 = (f32[160,512]{1,0:T(8,128)S(1)}, f32[160,512]{1,0:T(8,128)S(1)}, u32[]{:S(2)}, u32[]{:S(2)}) collective-permute-start(f32[160,512]{1,0:T(8,128)S(1)} %get-tuple-element.46), channel_id=1, source_target_pairs={{0,96},{32,0},{64,32},{96,64},{1,97},{33,1},{65,33},{97,65},{2,98}... | collective-permute-start | bytes 983048 | tf_op jit(solution)/shard_map/ppermute | solution.py:46
  107.8 9.4 %collective-permute-start.14 = (f32[128,512]{1,0:T(8,128)S(1)}, f32[128,512]{1,0:T(8,128)S(1)}, u32[]{:S(2)}, u32[]{:S(2)}) collective-permute-start(f32[128,512]{1,0:T(8,128)S(1)} %get-tuple-element.49), channel_id=1, source_target_pairs={{0,16},{8,24},{16,0},{24,8},{1,17},{9,25},{17,1},{25,9},{2,18},{10... | collective-permute-start | bytes 786440 | tf_op jit(solution)/shard_map/ppermute | solution.py:46
  110.9 11.7 %collective-permute-start.15 = (f32[128,512]{1,0:T(8,128)S(1)}, f32[128,512]{1,0:T(8,128)S(1)}, u32[]{:S(2)}, u32[]{:S(2)}) collective-permute-start(f32[128,512]{1,0:T(8,128)S(1)} %get-tuple-element.50), channel_id=1, source_target_pairs={{0,24},{8,0},{16,8},{24,16},{1,25},{9,1},{17,9},{25,17},{2,26},{10... | collective-permute-start | bytes 786440 | tf_op jit(solution)/shard_map/ppermute | solution.py:46
  123.6 9.8 %collective-permute-start.19 = (f32[32,512]{1,0:T(8,128)S(1)}, f32[32,512]{1,0:T(8,128)S(1)}, u32[]{:S(2)}, u32[]{:S(2)}) collective-permute-start(f32[32,512]{1,0:T(8,128)S(1)} %get-tuple-element.56), channel_id=1, source_target_pairs={{0,32},{32,64},{64,96},{96,0},{1,33},{33,65},{65,97},{97,1},{2,34}... | collective-permute-start | bytes 196616 | tf_op jit(solution)/shard_map/ppermute | solution.py:46
  124.5 13.2 %collective-permute-start.16 = (f32[64,512]{1,0:T(8,128)S(1)}, f32[64,512]{1,0:T(8,128)S(1)}, u32[]{:S(2)}, u32[]{:S(2)}) collective-permute-start(f32[64,512]{1,0:T(8,128)S(1)} %get-tuple-element.52), channel_id=1, source_target_pairs={{0,8},{8,16},{16,24},{24,0},{1,9},{9,17},{17,25},{25,1},{2,10},{10... | collective-permute-start | bytes 393224 | tf_op jit(solution)/shard_map/ppermute | solution.py:46
  124.7 13.0 %collective-permute-start.17 = (f32[64,512]{1,0:T(8,128)S(1)}, f32[64,512]{1,0:T(8,128)S(1)}, u32[]{:S(2)}, u32[]{:S(2)}) collective-permute-start(f32[64,512]{1,0:T(8,128)S(1)} %get-tuple-element.53), channel_id=1, source_target_pairs={{0,16},{8,24},{16,0},{24,8},{1,17},{9,25},{17,1},{25,9},{2,18},{10... | collective-permute-start | bytes 393224 | tf_op jit(solution)/shard_map/ppermute | solution.py:46
  128.6 9.1 %collective-permute-start.18 = (f32[64,512]{1,0:T(8,128)S(1)}, f32[64,512]{1,0:T(8,128)S(1)}, u32[]{:S(2)}, u32[]{:S(2)}) collective-permute-start(f32[64,512]{1,0:T(8,128)S(1)} %get-tuple-element.54), channel_id=1, source_target_pairs={{0,24},{8,0},{16,8},{24,16},{1,25},{9,1},{17,9},{25,17},{2,26},{10... | collective-permute-start | bytes 393224 | tf_op jit(solution)/shard_map/ppermute | solution.py:46
  128.9 6.8 %collective-permute-start.20 = (f32[32,512]{1,0:T(8,128)S(1)}, f32[32,512]{1,0:T(8,128)S(1)}, u32[]{:S(2)}, u32[]{:S(2)}) collective-permute-start(f32[32,512]{1,0:T(8,128)S(1)} %get-tuple-element.57), channel_id=1, source_target_pairs={{0,64},{32,96},{64,0},{96,32},{1,65},{33,97},{65,1},{97,33},{2,66}... | collective-permute-start | bytes 196616 | tf_op jit(solution)/shard_map/ppermute | solution.py:46
  133.5 4.3 %collective-permute-start.21 = (f32[32,512]{1,0:T(8,128)S(1)}, f32[32,512]{1,0:T(8,128)S(1)}, u32[]{:S(2)}, u32[]{:S(2)}) collective-permute-start(f32[32,512]{1,0:T(8,128)S(1)} %get-tuple-element.58), channel_id=1, source_target_pairs={{0,96},{32,0},{64,32},{96,64},{1,97},{33,1},{65,33},{97,65},{2,98}... | collective-permute-start | bytes 196616 | tf_op jit(solution)/shard_map/ppermute | solution.py:46
  137.8 11.6 %copy-start = (f32[32,512]{1,0:T(8,128)}, f32[32,512]{1,0:T(8,128)S(1)}, u32[]{:S(2)}) copy-start(f32[32,512]{1,0:T(8,128)S(1)} %get-tuple-element.61.refs_4_) | copy-start | bytes 196612
  137.8 6.3 %collective-permute-start.24 = (f32[32,512]{1,0:T(8,128)S(1)}, f32[32,512]{1,0:T(8,128)S(1)}, u32[]{:S(2)}, u32[]{:S(2)}) collective-permute-start(f32[32,512]{1,0:T(8,128)S(1)} %get-tuple-element.60.refs_0_), channel_id=1, source_target_pairs={{0,24},{8,0},{16,8},{24,16},{1,25},{9,1},{17,9},{25,17},{2,26},{10... | collective-permute-start | bytes 196616 | tf_op jit(solution)/shard_map/ppermute | solution.py:46
  138.9 7.2 %collective-permute-start.23 = (f32[32,512]{1,0:T(8,128)S(1)}, f32[32,512]{1,0:T(8,128)S(1)}, u32[]{:S(2)}, u32[]{:S(2)}) collective-permute-start(f32[32,512]{1,0:T(8,128)S(1)} %get-tuple-element.60.refs_0_), channel_id=1, source_target_pairs={{0,16},{8,24},{16,0},{24,8},{1,17},{9,25},{17,1},{25,9},{2,18},{10... | collective-permute-start | bytes 196616 | tf_op jit(solution)/shard_map/ppermute | solution.py:46
  141.9 5.5 %collective-permute-start.22 = (f32[32,512]{1,0:T(8,128)S(1)}, f32[32,512]{1,0:T(8,128)S(1)}, u32[]{:S(2)}, u32[]{:S(2)}) collective-permute-start(f32[32,512]{1,0:T(8,128)S(1)} %get-tuple-element.60.refs_0_), channel_id=1, source_target_pairs={{0,8},{8,16},{16,24},{24,0},{1,9},{9,17},{17,25},{25,1},{2,10},{10... | collective-permute-start | bytes 196616 | tf_op jit(solution)/shard_map/ppermute | solution.py:46
  142.4 5.6 %collective-permute-start.27 = (f32[32,512]{1,0:T(8,128)S(1)}, f32[32,512]{1,0:T(8,128)S(1)}, u32[]{:S(2)}, u32[]{:S(2)}) collective-permute-start(f32[32,512]{1,0:T(8,128)S(1)} %get-tuple-element.61.refs_4_), channel_id=1, source_target_pairs={{0,96},{32,0},{64,32},{96,64},{1,97},{33,1},{65,33},{97,65},{2,98}... | collective-permute-start | bytes 196616 | tf_op jit(solution)/shard_map/ppermute | solution.py:46
  143.6 5.8 %collective-permute-start.26 = (f32[32,512]{1,0:T(8,128)S(1)}, f32[32,512]{1,0:T(8,128)S(1)}, u32[]{:S(2)}, u32[]{:S(2)}) collective-permute-start(f32[32,512]{1,0:T(8,128)S(1)} %get-tuple-element.61.refs_4_), channel_id=1, source_target_pairs={{0,64},{32,96},{64,0},{96,32},{1,65},{33,97},{65,1},{97,33},{2,66}... | collective-permute-start | bytes 196616 | tf_op jit(solution)/shard_map/ppermute | solution.py:46
  144.1 5.3 %copy-start.2 = (f32[32,512]{1,0:T(8,128)}, f32[32,512]{1,0:T(8,128)S(1)}, u32[]{:S(2)}) copy-start(f32[32,512]{1,0:T(8,128)S(1)} %collective-permute-done.24.refs_3_) | copy-start | bytes 196612
  144.1 5.9 %collective-permute-start.25 = (f32[32,512]{1,0:T(8,128)S(1)}, f32[32,512]{1,0:T(8,128)S(1)}, u32[]{:S(2)}, u32[]{:S(2)}) collective-permute-start(f32[32,512]{1,0:T(8,128)S(1)} %get-tuple-element.61.refs_4_), channel_id=1, source_target_pairs={{0,32},{32,64},{64,96},{96,0},{1,33},{33,65},{65,97},{97,1},{2,34}... | collective-permute-start | bytes 196616 | tf_op jit(solution)/shard_map/ppermute | solution.py:46
  146.1 0.6 copy-start.4
  147.3 0.6 copy-start.6
  148.0 0.6 copy-start.8
  149.4 0.6 copy-start.10
  150.1 0.6 copy-start.12
  150.7 0.8 copy-start.1
  151.5 0.8 copy-start.3
  152.4 0.8 copy-start.5
  153.2 0.8 copy-start.7
  154.1 0.8 copy-start.9
  154.9 0.8 copy-start.11
  155.7 0.8 copy-start.13
  156.6 19.2 %collective-permute-start.30 = (f32[128,512]{1,0:T(8,128)S(1)}, f32[128,512]{1,0:T(8,128)}, u32[]{:S(2)}, u32[]{:S(2)}) collective-permute-start(f32[128,512]{1,0:T(8,128)S(1)} %get-tuple-element.62.refs_3_), channel_id=1, source_target_pairs={{0,96},{32,0},{64,32},{96,64},{1,97},{33,1},{65,33},{97,65},{2,98}... | collective-permute-start | bytes 786440 | tf_op jit(solution)/shard_map/ppermute | solution.py:46
  171.2 16.2 %collective-permute-start.29 = (f32[128,512]{1,0:T(8,128)S(1)}, f32[128,512]{1,0:T(8,128)}, u32[]{:S(2)}, u32[]{:S(2)}) collective-permute-start(f32[128,512]{1,0:T(8,128)S(1)} %get-tuple-element.62.refs_3_), channel_id=1, source_target_pairs={{0,64},{32,96},{64,0},{96,32},{1,65},{33,97},{65,1},{97,33},{2,66}... | collective-permute-start | bytes 786440 | tf_op jit(solution)/shard_map/ppermute | solution.py:46
  172.7 14.7 %collective-permute-start.28 = (f32[128,512]{1,0:T(8,128)S(1)}, f32[128,512]{1,0:T(8,128)}, u32[]{:S(2)}, u32[]{:S(2)}) collective-permute-start(f32[128,512]{1,0:T(8,128)S(1)} %get-tuple-element.62.refs_3_), channel_id=1, source_target_pairs={{0,32},{32,64},{64,96},{96,0},{1,33},{33,65},{65,97},{97,1},{2,34}... | collective-permute-start | bytes 786440 | tf_op jit(solution)/shard_map/ppermute | solution.py:46
  173.1 14.3 %collective-permute-start.33 = (f32[128,512]{1,0:T(8,128)S(1)}, f32[128,512]{1,0:T(8,128)}, u32[]{:S(2)}, u32[]{:S(2)}) collective-permute-start(f32[128,512]{1,0:T(8,128)S(1)} %get-tuple-element.63.refs_7_), channel_id=1, source_target_pairs={{0,24},{8,0},{16,8},{24,16},{1,25},{9,1},{17,9},{25,17},{2,26},{10... | collective-permute-start | bytes 786440 | tf_op jit(solution)/shard_map/ppermute | solution.py:46
  175.8 11.6 %collective-permute-start.32 = (f32[128,512]{1,0:T(8,128)S(1)}, f32[128,512]{1,0:T(8,128)}, u32[]{:S(2)}, u32[]{:S(2)}) collective-permute-start(f32[128,512]{1,0:T(8,128)S(1)} %get-tuple-element.63.refs_7_), channel_id=1, source_target_pairs={{0,16},{8,24},{16,0},{24,8},{1,17},{9,25},{17,1},{25,9},{2,18},{10... | collective-permute-start | bytes 786440 | tf_op jit(solution)/shard_map/ppermute | solution.py:46
  175.8 11.6 %collective-permute-start.31 = (f32[128,512]{1,0:T(8,128)S(1)}, f32[128,512]{1,0:T(8,128)}, u32[]{:S(2)}, u32[]{:S(2)}) collective-permute-start(f32[128,512]{1,0:T(8,128)S(1)} %get-tuple-element.63.refs_7_), channel_id=1, source_target_pairs={{0,8},{8,16},{16,24},{24,0},{1,9},{9,17},{17,25},{25,1},{2,10},{10... | collective-permute-start | bytes 786440 | tf_op jit(solution)/shard_map/ppermute | solution.py:46

commit v2 on v1

v2 whole, which is shorter than its diff:
```python
import functools
import math

import jax
import jax.numpy as jnp
from jax import lax
from jax.experimental import pallas as pl
from jax.experimental.pallas import tpu as pltpu
from jax.sharding import Mesh
from jax.sharding import PartitionSpec as P

LAG = 512
WIDE = 1024
F32 = jnp.float32
BF16 = jnp.bfloat16
NT = (((1,), (1,)), ((), ()))
NN = (((1,), (0,)), ((), ()))
MIB = 1024 * 1024


def split(value):
    high = value.astype(BF16)
    return high, (value - high.astype(F32)).astype(BF16)


def dot3(a_high, a_low, b_high, b_low, dims):
    dot = functools.partial(lax.dot_general, dimension_numbers=dims, preferred_element_type=F32)
    return dot(a_high, b_high) + (dot(a_high, b_low) + dot(a_low, b_high))


def whole(count):
    return [pl.BlockSpec(memory_space=pltpu.VMEM)] * count


def call(body, outs, args, limit=24):
    return pl.pallas_call(
        body,
        out_shape=[jax.ShapeDtypeStruct(shape, F32) for shape in outs],
        in_specs=whole(len(args)),
        out_specs=whole(len(outs)),
        compiler_params=pltpu.CompilerParams(vmem_limit_bytes=limit * MIB),
    )(*args)


AXES = ("x", "z", "y", "core")
SIDE = 4


def along(axis, step, value, blocks=0):
    pairs = []
    for x in range(SIDE):
        for z in range(SIDE):
            for y in range(SIDE):
                for core in range(2):
                    flip = 0 if step is None else (1, 3)[step ^ core]
                    there = {"x": x, "z": z, "y": y}
                    there[axis] ^= flip
                    time = there["x"] * SIDE + there["z"] + blocks
                    if 0 <= time < SIDE * SIDE:
                        pairs.append((index(x, z, y, core), index(time // SIDE, time % SIDE, there["y"], core)))
    return lax.ppermute(value, AXES, pairs)


def index(x, z, y, core):
    return ((x * SIDE + z) * SIDE + y) * 2 + core


def side(axis, step):
    place = lax.axis_index(axis)
    upper = place // 2
    even = lax.rem(place + upper, 2)
    core = lax.axis_index("core")
    return even + (upper - even) * core if step == 0 else upper + (even - upper) * core


def rows_at(which, count):
    return pl.ds(pl.multiple_of(which * count, count), count)


def sketch_partial(samples, omega):
    delays, channels, rank = omega.shape
    block = samples.shape[1]
    steps = block // LAG
    margin = (delays - 1) * LAG
    half = rank // 2

    def body(s_ref, o_ref, keep_ref, send_ref, high_ref, low_ref, acc_ref):
        step = pl.program_id(0)

        @pl.when(step == 0)
        def _():
            for d in range(delays):
                high, low = split(o_ref[d].T)
                high_ref[d * rank : (d + 1) * rank, :] = high
                low_ref[d * rank : (d + 1) * rank, :] = low
            acc_ref[...] = jnp.zeros_like(acc_ref)

        s_high, s_low = split(s_ref[...])
        term = dot3(high_ref[...], low_ref[...], s_high, s_low, NN)
        for d in range(delays):
            at = pl.ds(pl.multiple_of((step + delays - 1 - d) * LAG, LAG), LAG)
            acc_ref[:, at] += term[d * rank : (d + 1) * rank, :]

        @pl.when(step == steps - 1)
        def _():
            core = lax.axis_index("core")
            keep_ref[...] = acc_ref[pl.ds(pl.multiple_of(core * half, half), half), :]
            send_ref[...] = acc_ref[pl.ds(pl.multiple_of((1 - core) * half, half), half), :]

    out = jax.ShapeDtypeStruct((half, margin + block), F32)
    spec = pl.BlockSpec((half, margin + block), lambda i: (0, 0))
    return pl.pallas_call(
        body,
        grid=(steps,),
        out_shape=[out, out],
        in_specs=[
            pl.BlockSpec((channels, LAG), lambda i: (0, i)),
            pl.BlockSpec(omega.shape, lambda i: (0, 0, 0)),
        ],
        out_specs=[spec, spec],
        scratch_shapes=[
            pltpu.VMEM((delays * rank, channels), BF16),
            pltpu.VMEM((delays * rank, channels), BF16),
            pltpu.VMEM((rank, margin + block), F32),
        ],
        compiler_params=pltpu.CompilerParams(vmem_limit_bytes=40 * MIB),
        cost_estimate=pl.CostEstimate(
            flops=6 * delays * rank * channels * block, bytes_accessed=samples.size * 4, transcendentals=0
        ),
    )(samples, omega)


def projection_partial(samples, mine, other, delays, part, axis):
    channels, block = samples.shape
    half, width = mine.shape
    rank = 2 * half
    steps = block // WIDE
    rows = channels // 2
    lanes = delays * rank
    tail = rank // delays if part == 0 else 0

    def body(s_ref, mine_ref, other_ref, keep_ref, send_ref, high_ref, low_ref, acc_ref, gram_ref):
        step = pl.program_id(0)

        @pl.when(step == 0)
        def _():
            core = lax.axis_index("core")
            for ref, place in ((mine_ref, core), (other_ref, 1 - core)):
                high, low = split(ref[...])
                high_ref[rows_at(place, half), :] = high
                low_ref[rows_at(place, half), :] = low
            acc_ref[...] = jnp.zeros_like(acc_ref)
            gram_ref[...] = jnp.zeros_like(gram_ref)

        s_high, s_low = split(s_ref[...])
        highs, lows = [], []
        for d in range(delays):
            at = pl.ds(pl.multiple_of(step * WIDE + (delays - 1 - d) * LAG, LAG), WIDE)
            highs.append(high_ref[:, at])
            lows.append(low_ref[:, at])
        if part == 0:
            gram_ref[...] += dot3(highs[0], lows[0], highs[0], lows[0], NT)
        acc_ref[...] += dot3(s_high, s_low, jnp.concatenate(highs, 0), jnp.concatenate(lows, 0), NT)

        @pl.when(step == steps - 1)
        def _():
            which = side(axis, 0)
            for place, ref in ((which, keep_ref), (1 - which, send_ref)):
                ref[: rows // 2, :] = acc_ref[rows_at(place, rows // 2), :]
                for d in range(delays if tail else 0):
                    ref[rows // 2 :, d * rank : (d + 1) * rank] = gram_ref[d * tail : (d + 1) * tail, :]

    shape = (rows // 2 + tail, lanes)
    return pl.pallas_call(
        body,
        grid=(steps,),
        out_shape=[jax.ShapeDtypeStruct(shape, F32)] * 2,
        in_specs=[
            pl.BlockSpec((rows, WIDE), lambda i: (part, i)),
            pl.BlockSpec((half, width), lambda i: (0, 0)),
            pl.BlockSpec((half, width), lambda i: (0, 0)),
        ],
        out_specs=[pl.BlockSpec(shape, lambda i: (0, 0))] * 2,
        scratch_shapes=[
            pltpu.VMEM((rank, width), BF16),
            pltpu.VMEM((rank, width), BF16),
            pltpu.VMEM((rows, lanes), F32),
            pltpu.VMEM((rank, rank), F32),
        ],
        compiler_params=pltpu.CompilerParams(vmem_limit_bytes=36 * MIB),
        cost_estimate=pl.CostEstimate(
            flops=6 * lanes * rows * block, bytes_accessed=rows * block * 4, transcendentals=0
        ),
    )(samples, mine, other)


def fold(keep, came, axis, step, tail=0):
    count = (keep.shape[0] - tail) // 2

    def body(a_ref, b_ref, keep_ref, send_ref):
        which = side(axis, step)
        for place, ref in ((which, keep_ref), (1 - which, send_ref)):
            at = rows_at(place, count)
            ref[:count, :] = a_ref[at, :] + b_ref[at, :]
            if tail:
                ref[count:, :] = a_ref[2 * count :, :] + b_ref[2 * count :, :]

    return call(body, [(count + tail, keep.shape[1])] * 2, [keep, came], 8)


def add(a, b, tail=0):
    count = a.shape[0] - tail

    def body(a_ref, b_ref, out_ref, *tails):
        out_ref[...] = a_ref[:count, :] + b_ref[:count, :]
        for ref in tails:
            ref[...] = a_ref[count:, :] + b_ref[count:, :]

    return call(body, [(count, a.shape[1])] + [(tail, a.shape[1])] * (tail > 0), [a, b], 8)


def unfold(mine, came, axis, step):
    count = mine.shape[0]

    def body(a_ref, b_ref, out_ref):
        out_ref[rows_at(side(axis, step), count), :] = a_ref[...]
        out_ref[rows_at(1 - side(axis, step), count), :] = b_ref[...]

    return call(body, [(2 * count, mine.shape[1])], [mine, came], 8)[0]


def summed(keep, send, one, two, tail=0):
    keep, send = fold(keep, along(one, 0, send), one, 1, tail)
    (value,) = add(keep, along(one, 1, send))
    (value,) = add(value, along(two, 0, value))
    value, *rest = add(value, along(two, 1, value), tail)
    value = unfold(value, along(one, 1, value), one, 1)
    return (value, along(one, 0, value), *rest)


def inverse_factor(tail, rank):
    deep, delays = tail.shape[0], tail.shape[1] // rank
    panel = 16

    def body(tail_ref, out_ref, left_ref, right_ref):
        for d in range(delays):
            left_ref[d * deep : (d + 1) * deep, :] = tail_ref[:, d * rank : (d + 1) * rank]
        square = (rank, rank)
        same = lax.broadcasted_iota(jnp.int32, square, 0) == lax.broadcasted_iota(jnp.int32, square, 1)
        right_ref[...] = jnp.where(same, 1.0, 0.0)
        row = lax.broadcasted_iota(jnp.int32, (panel, rank), 0)
        for top in range(0, rank, panel):
            end = top + panel
            left, right = left_ref[top:end, :], right_ref[top:end, :]
            columns = [jnp.broadcast_to(left[:, top + m : top + m + 1], (panel, rank)) for m in range(panel)]
            pivots = jnp.zeros((panel, rank), F32)
            for j in range(panel):
                reciprocal = 1.0 / columns[j][j : j + 1, :]
                pivots = jnp.where(row == j, reciprocal, pivots)
                factor = jnp.where(row > j, columns[j] * reciprocal, 0.0)
                for m in range(j + 1, panel):
                    columns[m] = columns[m] - factor * columns[m][j : j + 1, :]
                left = left - factor * left[j : j + 1, :]
                right = right - factor * right[j : j + 1, :]
            if end < rank:
                factors = (left * pivots).T
                below_left, below_right = left_ref[end:, :], right_ref[end:, :]
                for j in range(panel):
                    factor = factors[end:, j : j + 1]
                    below_left = below_left - factor * left[j : j + 1, :]
                    below_right = below_right - factor * right[j : j + 1, :]
                left_ref[end:, :] = below_left
                right_ref[end:, :] = below_right
            out_ref[top:end, :] = right * lax.sqrt(pivots)

    return pl.pallas_call(
        body,
        out_shape=jax.ShapeDtypeStruct((rank, rank), F32),
        in_specs=whole(1),
        out_specs=whole(1)[0],
        scratch_shapes=[pltpu.VMEM((rank, rank), F32)] * 2,
        compiler_params=pltpu.CompilerParams(vmem_limit_bytes=8 * MIB),
    )(tail)


def shards(samples, omega):
    delays, channels, rank = omega.shape
    block = samples.shape[1]
    margin = (delays - 1) * LAG
    width = margin + block
    half, share = rank // 2, rank // 4
    total = block * SIDE * SIDE

    keep, send = sketch_partial(samples, omega)
    came = lax.ppermute(send, "core", [(0, 1), (1, 0)])
    keep, send = fold(keep, came, "y", 0)
    came = along("y", 0, send)

    def add_chips(a_ref, b_ref, main_ref, rim_ref):
        main_ref[...] = a_ref[:, margin:] + b_ref[:, margin:]
        rim_ref[...] = a_ref[:, :margin] + b_ref[:, :margin]

    main, rim = call(add_chips, [(share, block), (share, margin)], [keep, came], 8)
    rim_one = along("y", None, rim, -1)
    rim_two = along("y", 1, rim, -1)
    came = along("y", 1, main)

    def add_rim(main_ref, came_ref, one_ref, two_ref, out_ref, last_ref):
        inner = block - margin
        out_ref[:, :inner] = main_ref[:, :inner] + came_ref[:, :inner]
        value = (main_ref[:, inner:] + came_ref[:, inner:]) + (one_ref[...] + two_ref[...])
        out_ref[:, inner:] = value
        last_ref[...] = value

    main, last = call(add_rim, [(share, block), (share, margin)], [main, came, rim_one, rim_two], 8)

    before = along("y", None, last, 1)
    before_came = along("y", 0, last, 1)
    came = along("y", 0, main)

    def join(before_ref, main_ref, before_came_ref, came_ref, out_ref):
        which = side("y", 0)
        for place, rim_ref, ref in ((which, before_ref, main_ref), (1 - which, before_came_ref, came_ref)):
            out_ref[rows_at(place, share), :margin] = rim_ref[...]
            out_ref[rows_at(place, share), margin:] = ref[...]

    (mine,) = call(join, [(half, width)], [before, main, before_came, came], 8)
    other = lax.ppermute(mine, "core", [(0, 1), (1, 0)])

    first = projection_partial(samples, mine, other, delays, 0, "x")
    second = projection_partial(samples, mine, other, delays, 1, "z")
    first, first_came, gram = summed(*first, "x", "z", rank // delays)
    second, second_came = summed(*second, "z", "x")
    inverse = inverse_factor(gram, rank)

    def finish(inverse_ref, mine_ref, other_ref, *refs):
        ins, (basis_ref, out_ref) = refs[:4], refs[4:]
        high, low = split(inverse_ref[...])
        count = channels // 4
        for part, axis in enumerate(("x", "z")):
            which = side(axis, 0)
            for place, ref in ((which, ins[2 * part]), (1 - which, ins[2 * part + 1])):
                at = pl.ds(pl.multiple_of((2 * part + place) * count, count), count)
                for d in range(delays):
                    a_high, a_low = split(ref[:, d * rank : (d + 1) * rank])
                    out_ref[d, at, :] = dot3(a_high, a_low, high, low, NT)
        core, y = lax.axis_index("core"), lax.axis_index("y")
        columns = block // 8
        at = pl.ds(pl.multiple_of(margin + (y * 2 + core) * columns, columns), columns)
        sketch = jnp.concatenate([mine_ref[:, at], other_ref[:, at]], 0)
        swapped = jnp.concatenate([other_ref[:, at], mine_ref[:, at]], 0)
        s_high, s_low = split(jnp.where(core == 0, sketch, swapped))
        basis_ref[...] = math.sqrt(total) * dot3(high, low, s_high, s_low, NN)

    basis, projection = call(
        finish,
        [(rank, block // 8), (delays, channels, rank)],
        [inverse, mine, other, first, first_came, second, second_came],
        24,
    )
    return basis, projection


def solution(mesh):
    fine = Mesh(mesh.devices.reshape(SIDE, SIDE, SIDE, 2), AXES)
    tm, chan = ("x", "z"), ("y", "core")
    return jax.shard_map(
        shards,
        mesh=fine,
        in_specs=(P(chan, tm), P(None, chan, None)),
        out_specs=(P(None, tm + chan), P(None, chan, None)),
        check_vma=False,
    )
```

time: 194 us -> 154 us (0.79)
  other arithmetic: 23.7 us -> 0 us
  starting transfers between devices: 54.3 us -> 34.1 us
  waiting for transfers between devices: 60.4 us -> 71.9 us
  local copies, waits for them, and re-layouts: 11.3 us -> 1.58 us
  Pallas kernels: 41.7 us -> 44.6 us
    another operation x5 -> x0, other arithmetic: 22.9 us -> none  [the longest x3 12.4 us: shards(): lower = jnp.linalg.cholesky(gram)]
    ppermute x34 -> x21, starting transfers between devices: 54.3 us -> 34.1 us  [the longest x19 34 us: along(): return lax.ppermute(value, AXES, pairs)]
    ppermute x34 -> x21, waiting for transfers between devices: 60.4 us -> 71.9 us  [the longest x19 65.5 us: along(): return lax.ppermute(value, AXES, pairs)]
    unnamed x30 -> x2, local copies, waits for them, and re-layouts: 10.6 us -> 1.58 us
    pallas_call x1 -> x3, Pallas kernels: 18.2 us -> 24.3 us  [the longest x2 20 us: projection_partial(): pl.pallas_call(body, grid=(steps,), out_shape=[jax.ShapeDtypeStruct(shape...]
    pallas_call x9 -> x15, Pallas kernels: 6.46 us -> 3.26 us  [call(): pl.pallas_call(body, out_shape=[jax.ShapeDtypeStruct(shape, F32) for shap...]
  transfers between devices with their start and end apart: 34 -> 21, of which waited for: 14 -> 15; matrix products, arithmetic and copies ran while one was open for 13% -> 0% of each run, Pallas kernels for 0% -> 9%
where the time goes in v2:
time: 154 us; the launch traced here: 153 us
  waiting for transfers between devices  71.9 us (47%)
  Pallas kernels  44.6 us (29%)
  starting transfers between devices  34.1 us (22%)
  local copies, waits for them, and re-layouts  1.58 us (1%)
    ppermute x19, waiting for transfers between devices, along(): return lax.ppermute(value, AXES, pairs)  65.5 us
    ppermute x19, starting transfers between devices, along(): return lax.ppermute(value, AXES, pairs)  34 us
    pallas_call x2, Pallas kernels, projection_partial(): pl.pallas_call(body, grid=(steps,), out_shape=[jax.ShapeDtypeStruct(shape...  20 us
    pallas_call x1, Pallas kernels, sketch_partial(): pl.pallas_call(body, grid=(steps,), out_shape=[out, out], in_specs=[pl.Bl...  17 us
    pallas_call x1, Pallas kernels, inverse_factor(): pl.pallas_call(body, out_shape=jax.ShapeDtypeStruct((rank, rank), F32), i...  4.23 us
    pallas_call x15, Pallas kernels, call(): pl.pallas_call(body, out_shape=[jax.ShapeDtypeStruct(shape, F32) for shap...  3.26 us
    ppermute x1, waiting for transfers between devices, shards(): came = lax.ppermute(send, 'core', [(0, 1), (1, 0)])  3.21 us
    ppermute x1, waiting for transfers between devices, shards(): other = lax.ppermute(mine, 'core', [(0, 1), (1, 0)])  3.2 us
  transfers between devices with their start and end apart: 21, of which 15 were waited for; matrix products, arithmetic and copies ran while one was open for 0% of the time, Pallas kernels for 9%

profile of v2, /device:TPU:0, one launch (start us, length us, event | category | flops | bytes accessed | tf_op | source)
XLA Modules:
  0.0 153.1 jit_solution(16609401197375824455)
XLA Ops:
  0.6 0.0 copy-start
  0.6 1.6 %copy-done = f32[4,1024,128]{2,1,0:T(8,128)S(1)} copy-done((f32[4,1024,128]{2,1,0:T(8,128)S(1)}, f32[4,1024,128]{2,1,0:T(8,128)}, u32[]{:S(2)}) %copy-start) | copy-done | bytes 2097176
  2.2 17.0 %shard_map.41 = (f32[64,5632]{1,0:T(8,128)S(1)}, f32[64,5632]{1,0:T(8,128)S(1)}) custom-call(f32[1024,4096]{1,0:T(8,128)} %s_ref.5, f32[4,1024,128]{2,1,0:T(8,128)S(1)} %copy-done), custom_call_target="tpu_custom_call" | custom-call | flops 12884901888 | bytes 16777216 | tf_op jit(solution)/shard_map/pallas_call | solution.py:112
  19.3 0.1 collective-permute-start
  19.4 3.2 %collective-permute-done.b_ref = f32[64,5632]{1,0:T(8,128)S(1)} collective-permute-done((f32[64,5632]{1,0:T(8,128)S(1)}, f32[64,5632]{1,0:T(8,128)S(1)}, u32[]{:S(2)}, u32[]{:S(2)}) %collective-permute-start) | collective-permute-done | bytes 1441824 | tf_op jit(solution)/shard_map/ppermute | solution.py:295
  22.6 0.1 shard_map.42
  22.7 1.7 %collective-permute-start.1 = (f32[32,5632]{1,0:T(8,128)S(1)}, f32[32,5632]{1,0:T(8,128)S(1)}, u32[]{:S(2)}, u32[]{:S(2)}) collective-permute-start(f32[32,5632]{1,0:T(8,128)S(1)} %get-tuple-element.23), channel_id=1, source_target_pairs={{0,2},{1,7},{2,0},{3,5},{4,6},{5,3},{6,4},{7,1},{8,10},{9,15},{10,... | collective-permute-start | bytes 2162696 | tf_op jit(solution)/shard_map/ppermute | solution.py:61
  24.5 9.6 %collective-permute-done.1.b_ref = f32[32,5632]{1,0:T(8,128)S(1)} collective-permute-done((f32[32,5632]{1,0:T(8,128)S(1)}, f32[32,5632]{1,0:T(8,128)S(1)}, u32[]{:S(2)}, u32[]{:S(2)}) %collective-permute-start.1) | collective-permute-done | bytes 720928 | tf_op jit(solution)/shard_map/ppermute | solution.py:61
  34.1 0.1 shard_map.43
  34.2 3.2 %collective-permute-start.2 = (f32[32,4096]{1,0:T(8,128)S(1)}, f32[32,4096]{1,0:T(8,128)S(1)}, u32[]{:S(2)}, u32[]{:S(2)}) collective-permute-start(f32[32,4096]{1,0:T(8,128)S(1)} %get-tuple-element.24.main_ref), channel_id=1, source_target_pairs={{0,6},{1,3},{2,4},{3,1},{4,2},{5,7},{6,0},{7,5},{8,14},{9,11},{10,... | collective-permute-start | bytes 1572872 | tf_op jit(solution)/shard_map/ppermute | solution.py:61
  37.3 1.3 collective-permute-start.4
  38.6 1.3 collective-permute-start.3
  39.9 8.5 %collective-permute-done.4.two_ref = f32[32,1536]{1,0:T(8,128)S(1)} collective-permute-done((f32[32,1536]{1,0:T(8,128)S(1)}, f32[32,1536]{1,0:T(8,128)S(1)}, u32[]{:S(2)}, u32[]{:S(2)}) %collective-permute-start.4) | collective-permute-done | bytes 196640 | tf_op jit(solution)/shard_map/ppermute | solution.py:61
  48.5 2.1 %collective-permute-done.3.one_ref = f32[32,1536]{1,0:T(8,128)S(1)} collective-permute-done((f32[32,1536]{1,0:T(8,128)S(1)}, f32[32,1536]{1,0:T(8,128)S(1)}, u32[]{:S(2)}, u32[]{:S(2)}) %collective-permute-start.3) | collective-permute-done | bytes 196640 | tf_op jit(solution)/shard_map/ppermute | solution.py:61
  50.6 0.0 collective-permute-done.2.came_ref
  50.6 0.1 shard_map.44
  50.7 0.8 collective-permute-start.7
  51.5 4.5 %collective-permute-start.6 = (f32[32,1536]{1,0:T(8,128)S(1)}, f32[32,1536]{1,0:T(8,128)S(1)}, u32[]{:S(2)}, u32[]{:S(2)}) collective-permute-start(f32[32,1536]{1,0:T(8,128)S(1)} %get-tuple-element.26), channel_id=1, source_target_pairs={{0,10},{1,15},{2,8},{3,13},{4,14},{5,11},{6,12},{7,9},{8,18},{9,23... | collective-permute-start | bytes 589832 | tf_op jit(solution)/shard_map/ppermute | solution.py:61
  56.1 3.8 %collective-permute-start.5 = (f32[32,1536]{1,0:T(8,128)S(1)}, f32[32,1536]{1,0:T(8,128)S(1)}, u32[]{:S(2)}, u32[]{:S(2)}) collective-permute-start(f32[32,1536]{1,0:T(8,128)S(1)} %get-tuple-element.26), channel_id=1, source_target_pairs={{0,8},{1,9},{2,10},{3,11},{4,12},{5,13},{6,14},{7,15},{8,16},{9,17... | collective-permute-start | bytes 589832 | tf_op jit(solution)/shard_map/ppermute | solution.py:61
  59.9 1.3 collective-permute-done.6.before_came_ref
  61.2 4.5 %collective-permute-done.5.before_ref = f32[32,1536]{1,0:T(8,128)S(1)} collective-permute-done((f32[32,1536]{1,0:T(8,128)S(1)}, f32[32,1536]{1,0:T(8,128)S(1)}, u32[]{:S(2)}, u32[]{:S(2)}) %collective-permute-start.5) | collective-permute-done | bytes 196640 | tf_op jit(solution)/shard_map/ppermute | solution.py:61
  65.6 0.0 collective-permute-done.7.came_ref
  65.7 0.1 shard_map.45.mine_ref
  65.8 0.1 collective-permute-start.8
  65.9 3.2 %collective-permute-done.8.other_ref = f32[64,5632]{1,0:T(8,128)S(1)} collective-permute-done((f32[64,5632]{1,0:T(8,128)S(1)}, f32[64,5632]{1,0:T(8,128)S(1)}, u32[]{:S(2)}, u32[]{:S(2)}) %collective-permute-start.8) | collective-permute-done | bytes 1441824 | tf_op jit(solution)/shard_map/ppermute | solution.py:328
  69.1 10.5 %shard_map.46 = (f32[288,512]{1,0:T(8,128)S(1)}, f32[288,512]{1,0:T(8,128)S(1)}) custom-call(f32[1024,4096]{1,0:T(8,128)} %s_ref.5, f32[64,5632]{1,0:T(8,128)S(1)} %shard_map.45.mine_ref, f32[64,5632]{1,0:T(8,128)S(1)} %collective-permute-done.8.other_ref), custom_call_target="tpu_custom_call" | custom-call | flops 6442450944 | bytes 8388608 | tf_op jit(solution)/shard_map/pallas_call | solution.py:174
  79.6 7.3 %collective-permute-start.9 = (f32[288,512]{1,0:T(8,128)S(1)}, f32[288,512]{1,0:T(8,128)S(1)}, u32[]{:S(2)}, u32[]{:S(2)}) collective-permute-start(f32[288,512]{1,0:T(8,128)S(1)} %get-tuple-element.29), channel_id=1, source_target_pairs={{0,32},{1,97},{2,34},{3,99},{4,36},{5,101},{6,38},{7,103},{8,40},{... | collective-permute-start | bytes 1769480 | tf_op jit(solution)/shard_map/ppermute | solution.py:61
  86.9 9.5 %shard_map.53 = (f32[256,512]{1,0:T(8,128)S(1)}, f32[256,512]{1,0:T(8,128)S(1)}) custom-call(f32[1024,4096]{1,0:T(8,128)} %s_ref.5, f32[64,5632]{1,0:T(8,128)S(1)} %shard_map.45.mine_ref, f32[64,5632]{1,0:T(8,128)S(1)} %collective-permute-done.8.other_ref), custom_call_target="tpu_custom_call" | custom-call | flops 6442450944 | bytes 8388608 | tf_op jit(solution)/shard_map/pallas_call | solution.py:174
  96.5 0.1 collective-permute-start.15
  96.5 0.0 collective-permute-done.9.b_ref
  96.6 0.1 shard_map.47
  96.6 2.2 %collective-permute-start.10 = (f32[160,512]{1,0:T(8,128)S(1)}, f32[160,512]{1,0:T(8,128)S(1)}, u32[]{:S(2)}, u32[]{:S(2)}) collective-permute-start(f32[160,512]{1,0:T(8,128)S(1)} %get-tuple-element.31), channel_id=1, source_target_pairs={{0,96},{1,33},{2,98},{3,35},{4,100},{5,37},{6,102},{7,39},{8,104},... | collective-permute-start | bytes 983048 | tf_op jit(solution)/shard_map/ppermute | solution.py:61
  98.8 6.9 %collective-permute-done.15.b_ref = f32[256,512]{1,0:T(8,128)S(1)} collective-permute-done((f32[256,512]{1,0:T(8,128)S(1)}, f32[256,512]{1,0:T(8,128)S(1)}, u32[]{:S(2)}, u32[]{:S(2)}) %collective-permute-start.15) | collective-permute-done | bytes 524320 | tf_op jit(solution)/shard_map/ppermute | solution.py:61
  105.7 0.1 shard_map.54
  105.8 0.1 collective-permute-start.16
  105.9 0.0 collective-permute-done.10.b_ref
  105.9 1.2 collective-permute-start.11
  107.1 8.9 %collective-permute-done.16.b_ref = f32[128,512]{1,0:T(8,128)S(1)} collective-permute-done((f32[128,512]{1,0:T(8,128)S(1)}, f32[128,512]{1,0:T(8,128)S(1)}, u32[]{:S(2)}, u32[]{:S(2)}) %collective-permute-start.16) | collective-permute-done | bytes 262176 | tf_op jit(solution)/shard_map/ppermute | solution.py:61
  116.1 0.1 collective-permute-start.17
  116.2 0.0 collective-permute-done.11.b_ref
  116.2 0.2 collective-permute-start.12
  116.4 6.1 %collective-permute-done.17.b_ref = f32[128,512]{1,0:T(8,128)S(1)} collective-permute-done((f32[128,512]{1,0:T(8,128)S(1)}, f32[128,512]{1,0:T(8,128)S(1)}, u32[]{:S(2)}, u32[]{:S(2)}) %collective-permute-start.17) | collective-permute-done | bytes 262176 | tf_op jit(solution)/shard_map/ppermute | solution.py:61
  122.6 1.7 %collective-permute-start.18 = (f32[128,512]{1,0:T(8,128)S(1)}, f32[128,512]{1,0:T(8,128)S(1)}, u32[]{:S(2)}, u32[]{:S(2)}) collective-permute-start(f32[128,512]{1,0:T(8,128)S(1)} %shard_map.56.a_ref), channel_id=1, source_target_pairs={{0,96},{1,33},{2,98},{3,35},{4,100},{5,37},{6,102},{7,39},{8,104},... | collective-permute-start | bytes 786440 | tf_op jit(solution)/shard_map/ppermute | solution.py:61
  124.2 6.0 %collective-permute-done.18.b_ref = f32[128,512]{1,0:T(8,128)S(1)} collective-permute-done((f32[128,512]{1,0:T(8,128)S(1)}, f32[128,512]{1,0:T(8,128)S(1)}, u32[]{:S(2)}, u32[]{:S(2)}) %collective-permute-start.18) | collective-permute-done | bytes 262176 | tf_op jit(solution)/shard_map/ppermute | solution.py:61
  130.3 0.8 collective-permute-start.19
  131.1 0.0 collective-permute-done.12.b_ref
  131.1 3.3 %collective-permute-start.13 = (f32[128,512]{1,0:T(8,128)S(1)}, f32[128,512]{1,0:T(8,128)S(1)}, u32[]{:S(2)}, u32[]{:S(2)}) collective-permute-start(f32[128,512]{1,0:T(8,128)S(1)} %get-tuple-element.33.a_ref), channel_id=1, source_target_pairs={{0,96},{1,33},{2,98},{3,35},{4,100},{5,37},{6,102},{7,39},{8,104},... | collective-permute-start | bytes 786440 | tf_op jit(solution)/shard_map/ppermute | solution.py:61
  134.4 4.5 %collective-permute-done.19.b_ref = f32[128,512]{1,0:T(8,128)S(1)} collective-permute-done((f32[128,512]{1,0:T(8,128)S(1)}, f32[128,512]{1,0:T(8,128)S(1)}, u32[]{:S(2)}, u32[]{:S(2)}) %collective-permute-start.19) | collective-permute-done | bytes 262176 | tf_op jit(solution)/shard_map/ppermute | solution.py:61
  138.9 0.1 shard_map.58.refs_2_
  139.0 0.1 collective-permute-start.20
  139.1 2.1 %collective-permute-done.13.b_ref = f32[128,512]{1,0:T(8,128)S(1)} collective-permute-done((f32[128,512]{1,0:T(8,128)S(1)}, f32[128,512]{1,0:T(8,128)S(1)}, u32[]{:S(2)}, u32[]{:S(2)}) %collective-permute-start.13) | collective-permute-done | bytes 262176 | tf_op jit(solution)/shard_map/ppermute | solution.py:61
  141.2 0.1 shard_map.52.refs_0_
  141.3 0.3 collective-permute-start.14
  141.5 4.2 %shard_map.51.inverse_ref = f32[128,128]{1,0:T(8,128)S(1)} custom-call(f32[32,512]{1,0:T(8,128)S(1)} %get-tuple-element.32.tail_ref), custom_call_target="tpu_custom_call" | custom-call | tf_op jit(solution)/shard_map/pallas_call | solution.py:276
  145.8 2.5 %collective-permute-done.20.refs_3_ = f32[256,512]{1,0:T(8,128)S(1)} collective-permute-done((f32[256,512]{1,0:T(8,128)S(1)}, f32[256,512]{1,0:T(8,128)S(1)}, u32[]{:S(2)}, u32[]{:S(2)}) %collective-permute-start.20) | collective-permute-done | bytes 524320 | tf_op jit(solution)/shard_map/ppermute | solution.py:61
  148.3 2.4 %collective-permute-done.14.refs_1_ = f32[256,512]{1,0:T(8,128)S(1)} collective-permute-done((f32[256,512]{1,0:T(8,128)S(1)}, f32[256,512]{1,0:T(8,128)S(1)}, u32[]{:S(2)}, u32[]{:S(2)}) %collective-permute-start.14) | collective-permute-done | bytes 524320 | tf_op jit(solution)/shard_map/ppermute | solution.py:61
  150.7 2.4 %shard_map.59 = (f32[128,512]{1,0:T(8,128)}, f32[4,1024,128]{2,1,0:T(8,128)}) custom-call(f32[128,128]{1,0:T(8,128)S(1)} %shard_map.51.inverse_ref, f32[64,5632]{1,0:T(8,128)S(1)} %shard_map.45.mine_ref, f32[64,5632]{1,0:T(8,128)S(1)} %collective-permute-done.8.other_ref, f32[256,512]{1,0:T(8,128)S(1)} %shard_map.52.refs_0_, ...), custom_call_target="tpu_custom_call" | custom-call | tf_op jit(solution)/shard_map/pallas_call | solution.py:36
  (6 shorter events, 0.2 us)
Async XLA Ops:
  0.6 1.6 %copy-start = (f32[4,1024,128]{2,1,0:T(8,128)S(1)}, f32[4,1024,128]{2,1,0:T(8,128)}, u32[]{:S(2)}) copy-start(f32[4,1024,128]{2,1,0:T(8,128)} %o_ref.1) | copy-start | bytes 6291460
  19.3 3.3 %collective-permute-start = (f32[64,5632]{1,0:T(8,128)S(1)}, f32[64,5632]{1,0:T(8,128)S(1)}, u32[]{:S(2)}, u32[]{:S(2)}) collective-permute-start(f32[64,5632]{1,0:T(8,128)S(1)} %get-tuple-element.21), channel_id=1, source_target_pairs={{0,1},{1,0},{2,3},{3,2},{4,5},{5,4},{6,7},{7,6},{8,9},{9,8},{10,11... | collective-permute-start | bytes 4325384 | tf_op jit(solution)/shard_map/ppermute | solution.py:295
  22.7 11.4 %collective-permute-start.1 = (f32[32,5632]{1,0:T(8,128)S(1)}, f32[32,5632]{1,0:T(8,128)S(1)}, u32[]{:S(2)}, u32[]{:S(2)}) collective-permute-start(f32[32,5632]{1,0:T(8,128)S(1)} %get-tuple-element.23), channel_id=1, source_target_pairs={{0,2},{1,7},{2,0},{3,5},{4,6},{5,3},{6,4},{7,1},{8,10},{9,15},{10,... | collective-permute-start | bytes 2162696 | tf_op jit(solution)/shard_map/ppermute | solution.py:61
  34.2 16.4 %collective-permute-start.2 = (f32[32,4096]{1,0:T(8,128)S(1)}, f32[32,4096]{1,0:T(8,128)S(1)}, u32[]{:S(2)}, u32[]{:S(2)}) collective-permute-start(f32[32,4096]{1,0:T(8,128)S(1)} %get-tuple-element.24.main_ref), channel_id=1, source_target_pairs={{0,6},{1,3},{2,4},{3,1},{4,2},{5,7},{6,0},{7,5},{8,14},{9,11},{10,... | collective-permute-start | bytes 1572872 | tf_op jit(solution)/shard_map/ppermute | solution.py:61
  37.3 11.1 %collective-permute-start.4 = (f32[32,1536]{1,0:T(8,128)S(1)}, f32[32,1536]{1,0:T(8,128)S(1)}, u32[]{:S(2)}, u32[]{:S(2)}) collective-permute-start(f32[32,1536]{1,0:T(8,128)S(1)} %get-tuple-element.25), channel_id=1, source_target_pairs={{8,6},{9,3},{10,4},{11,1},{12,2},{13,7},{14,0},{15,5},{16,14},{17,... | collective-permute-start | bytes 589832 | tf_op jit(solution)/shard_map/ppermute | solution.py:61
  38.6 12.0 %collective-permute-start.3 = (f32[32,1536]{1,0:T(8,128)S(1)}, f32[32,1536]{1,0:T(8,128)S(1)}, u32[]{:S(2)}, u32[]{:S(2)}) collective-permute-start(f32[32,1536]{1,0:T(8,128)S(1)} %get-tuple-element.25), channel_id=1, source_target_pairs={{8,0},{9,1},{10,2},{11,3},{12,4},{13,5},{14,6},{15,7},{16,8},{17,9... | collective-permute-start | bytes 589832 | tf_op jit(solution)/shard_map/ppermute | solution.py:61
  50.7 15.0 %collective-permute-start.7 = (f32[32,4096]{1,0:T(8,128)S(1)}, f32[32,4096]{1,0:T(8,128)S(1)}, u32[]{:S(2)}, u32[]{:S(2)}) collective-permute-start(f32[32,4096]{1,0:T(8,128)S(1)} %get-tuple-element.27.main_ref), channel_id=1, source_target_pairs={{0,2},{1,7},{2,0},{3,5},{4,6},{5,3},{6,4},{7,1},{8,10},{9,15},{10,... | collective-permute-start | bytes 1572872 | tf_op jit(solution)/shard_map/ppermute | solution.py:61
  51.5 9.6 %collective-permute-start.6 = (f32[32,1536]{1,0:T(8,128)S(1)}, f32[32,1536]{1,0:T(8,128)S(1)}, u32[]{:S(2)}, u32[]{:S(2)}) collective-permute-start(f32[32,1536]{1,0:T(8,128)S(1)} %get-tuple-element.26), channel_id=1, source_target_pairs={{0,10},{1,15},{2,8},{3,13},{4,14},{5,11},{6,12},{7,9},{8,18},{9,23... | collective-permute-start | bytes 589832 | tf_op jit(solution)/shard_map/ppermute | solution.py:61
  56.1 9.6 %collective-permute-start.5 = (f32[32,1536]{1,0:T(8,128)S(1)}, f32[32,1536]{1,0:T(8,128)S(1)}, u32[]{:S(2)}, u32[]{:S(2)}) collective-permute-start(f32[32,1536]{1,0:T(8,128)S(1)} %get-tuple-element.26), channel_id=1, source_target_pairs={{0,8},{1,9},{2,10},{3,11},{4,12},{5,13},{6,14},{7,15},{8,16},{9,17... | collective-permute-start | bytes 589832 | tf_op jit(solution)/shard_map/ppermute | solution.py:61
  65.8 3.3 %collective-permute-start.8 = (f32[64,5632]{1,0:T(8,128)S(1)}, f32[64,5632]{1,0:T(8,128)S(1)}, u32[]{:S(2)}, u32[]{:S(2)}) collective-permute-start(f32[64,5632]{1,0:T(8,128)S(1)} %shard_map.45.mine_ref), channel_id=1, source_target_pairs={{0,1},{1,0},{2,3},{3,2},{4,5},{5,4},{6,7},{7,6},{8,9},{9,8},{10,11... | collective-permute-start | bytes 4325384 | tf_op jit(solution)/shard_map/ppermute | solution.py:328
  79.6 17.0 %collective-permute-start.9 = (f32[288,512]{1,0:T(8,128)S(1)}, f32[288,512]{1,0:T(8,128)S(1)}, u32[]{:S(2)}, u32[]{:S(2)}) collective-permute-start(f32[288,512]{1,0:T(8,128)S(1)} %get-tuple-element.29), channel_id=1, source_target_pairs={{0,32},{1,97},{2,34},{3,99},{4,36},{5,101},{6,38},{7,103},{8,40},{... | collective-permute-start | bytes 1769480 | tf_op jit(solution)/shard_map/ppermute | solution.py:61
  96.5 9.3 %collective-permute-start.15 = (f32[256,512]{1,0:T(8,128)S(1)}, f32[256,512]{1,0:T(8,128)S(1)}, u32[]{:S(2)}, u32[]{:S(2)}) collective-permute-start(f32[256,512]{1,0:T(8,128)S(1)} %get-tuple-element.35), channel_id=1, source_target_pairs={{0,8},{1,25},{2,10},{3,27},{4,12},{5,29},{6,14},{7,31},{8,0},{9,17... | collective-permute-start | bytes 1572872 | tf_op jit(solution)/shard_map/ppermute | solution.py:61
  96.6 9.2 %collective-permute-start.10 = (f32[160,512]{1,0:T(8,128)S(1)}, f32[160,512]{1,0:T(8,128)S(1)}, u32[]{:S(2)}, u32[]{:S(2)}) collective-permute-start(f32[160,512]{1,0:T(8,128)S(1)} %get-tuple-element.31), channel_id=1, source_target_pairs={{0,96},{1,33},{2,98},{3,35},{4,100},{5,37},{6,102},{7,39},{8,104},... | collective-permute-start | bytes 983048 | tf_op jit(solution)/shard_map/ppermute | solution.py:61
  105.8 10.3 %collective-permute-start.16 = (f32[128,512]{1,0:T(8,128)S(1)}, f32[128,512]{1,0:T(8,128)S(1)}, u32[]{:S(2)}, u32[]{:S(2)}) collective-permute-start(f32[128,512]{1,0:T(8,128)S(1)} %get-tuple-element.37), channel_id=1, source_target_pairs={{0,24},{1,9},{2,26},{3,11},{4,28},{5,13},{6,30},{7,15},{8,16},{9,1... | collective-permute-start | bytes 786440 | tf_op jit(solution)/shard_map/ppermute | solution.py:61
  105.9 10.3 %collective-permute-start.11 = (f32[160,512]{1,0:T(8,128)S(1)}, f32[160,512]{1,0:T(8,128)S(1)}, u32[]{:S(2)}, u32[]{:S(2)}) collective-permute-start(f32[160,512]{1,0:T(8,128)S(1)} %shard_map.48.a_ref), channel_id=1, source_target_pairs={{0,8},{1,25},{2,10},{3,27},{4,12},{5,29},{6,14},{7,31},{8,0},{9,17... | collective-permute-start | bytes 983048 | tf_op jit(solution)/shard_map/ppermute | solution.py:61
  116.1 6.5 %collective-permute-start.17 = (f32[128,512]{1,0:T(8,128)S(1)}, f32[128,512]{1,0:T(8,128)S(1)}, u32[]{:S(2)}, u32[]{:S(2)}) collective-permute-start(f32[128,512]{1,0:T(8,128)S(1)} %shard_map.55.a_ref), channel_id=1, source_target_pairs={{0,32},{1,97},{2,34},{3,99},{4,36},{5,101},{6,38},{7,103},{8,40},{... | collective-permute-start | bytes 786440 | tf_op jit(solution)/shard_map/ppermute | solution.py:61
  116.2 14.9 %collective-permute-start.12 = (f32[160,512]{1,0:T(8,128)S(1)}, f32[160,512]{1,0:T(8,128)S(1)}, u32[]{:S(2)}, u32[]{:S(2)}) collective-permute-start(f32[160,512]{1,0:T(8,128)S(1)} %shard_map.49.a_ref), channel_id=1, source_target_pairs={{0,24},{1,9},{2,26},{3,11},{4,28},{5,13},{6,30},{7,15},{8,16},{9,1... | collective-permute-start | bytes 983048 | tf_op jit(solution)/shard_map/ppermute | solution.py:61
  122.6 7.7 %collective-permute-start.18 = (f32[128,512]{1,0:T(8,128)S(1)}, f32[128,512]{1,0:T(8,128)S(1)}, u32[]{:S(2)}, u32[]{:S(2)}) collective-permute-start(f32[128,512]{1,0:T(8,128)S(1)} %shard_map.56.a_ref), channel_id=1, source_target_pairs={{0,96},{1,33},{2,98},{3,35},{4,100},{5,37},{6,102},{7,39},{8,104},... | collective-permute-start | bytes 786440 | tf_op jit(solution)/shard_map/ppermute | solution.py:61
  130.3 8.7 %collective-permute-start.19 = (f32[128,512]{1,0:T(8,128)S(1)}, f32[128,512]{1,0:T(8,128)S(1)}, u32[]{:S(2)}, u32[]{:S(2)}) collective-permute-start(f32[128,512]{1,0:T(8,128)S(1)} %shard_map.57.a_ref), channel_id=1, source_target_pairs={{0,24},{1,9},{2,26},{3,11},{4,28},{5,13},{6,30},{7,15},{8,16},{9,1... | collective-permute-start | bytes 786440 | tf_op jit(solution)/shard_map/ppermute | solution.py:61
  131.1 10.1 %collective-permute-start.13 = (f32[128,512]{1,0:T(8,128)S(1)}, f32[128,512]{1,0:T(8,128)S(1)}, u32[]{:S(2)}, u32[]{:S(2)}) collective-permute-start(f32[128,512]{1,0:T(8,128)S(1)} %get-tuple-element.33.a_ref), channel_id=1, source_target_pairs={{0,96},{1,33},{2,98},{3,35},{4,100},{5,37},{6,102},{7,39},{8,104},... | collective-permute-start | bytes 786440 | tf_op jit(solution)/shard_map/ppermute | solution.py:61
  139.0 9.3 %collective-permute-start.20 = (f32[256,512]{1,0:T(8,128)S(1)}, f32[256,512]{1,0:T(8,128)S(1)}, u32[]{:S(2)}, u32[]{:S(2)}) collective-permute-start(f32[256,512]{1,0:T(8,128)S(1)} %shard_map.58.refs_2_), channel_id=1, source_target_pairs={{0,8},{1,25},{2,10},{3,27},{4,12},{5,29},{6,14},{7,31},{8,0},{9,17... | collective-permute-start | bytes 1572872 | tf_op jit(solution)/shard_map/ppermute | solution.py:61
  141.3 9.4 %collective-permute-start.14 = (f32[256,512]{1,0:T(8,128)S(1)}, f32[256,512]{1,0:T(8,128)S(1)}, u32[]{:S(2)}, u32[]{:S(2)}) collective-permute-start(f32[256,512]{1,0:T(8,128)S(1)} %shard_map.52.refs_0_), channel_id=1, source_target_pairs={{0,32},{1,97},{2,34},{3,99},{4,36},{5,101},{6,38},{7,103},{8,40},{... | collective-permute-start | bytes 1572872 | tf_op jit(solution)/shard_map/ppermute | solution.py:61

commit v3 on v2

--- a/solution.py
+++ b/solution.py
@@ -32,12 +32,13 @@
     return [pl.BlockSpec(memory_space=pltpu.VMEM)] * count
 
 
-def call(body, outs, args, limit=24):
+def call(body, outs, args, limit=24, scratch=()):
     return pl.pallas_call(
         body,
         out_shape=[jax.ShapeDtypeStruct(shape, F32) for shape in outs],
         in_specs=whole(len(args)),
         out_specs=whole(len(outs)),
+        scratch_shapes=[pltpu.VMEM(shape, F32) for shape in scratch],
         compiler_params=pltpu.CompilerParams(vmem_limit_bytes=limit * MIB),
     )(*args)
 
@@ -65,11 +66,11 @@
     return ((x * SIDE + z) * SIDE + y) * 2 + core
 
 
-def side(axis, step):
+def side(axis, step, core=None):
     place = lax.axis_index(axis)
     upper = place // 2
     even = lax.rem(place + upper, 2)
-    core = lax.axis_index("core")
+    core = lax.axis_index("core") if core is None else core
     return even + (upper - even) * core if step == 0 else upper + (even - upper) * core
 
 
@@ -104,8 +105,8 @@
         @pl.when(step == steps - 1)
         def _():
             core = lax.axis_index("core")
-            keep_ref[...] = acc_ref[pl.ds(pl.multiple_of(core * half, half), half), :]
-            send_ref[...] = acc_ref[pl.ds(pl.multiple_of((1 - core) * half, half), half), :]
+            keep_ref[...] = acc_ref[rows_at(core, half), :]
+            send_ref[...] = acc_ref[rows_at(1 - core, half), :]
 
     out = jax.ShapeDtypeStruct((half, margin + block), F32)
     spec = pl.BlockSpec((half, margin + block), lambda i: (0, 0))
@@ -127,28 +128,39 @@
         cost_estimate=pl.CostEstimate(
             flops=6 * delays * rank * channels * block, bytes_accessed=samples.size * 4, transcendentals=0
         ),
-    )(samples, omega)
-
-
-def projection_partial(samples, mine, other, delays, part, axis):
+    )(samples, pltpu.with_memory_space_constraint(omega, pltpu.HBM))
+
+
+def quarters():
+    core = lax.axis_index("core")
+    own, other = side("y", 0), side("y", 0, 1 - core)
+    return [2 * core + own, 2 * (1 - core) + other, 2 * core + 1 - own, 2 * (1 - core) + 1 - other]
+
+
+def in_order(places):
+    return jnp.minimum(*places), jnp.maximum(*places)
+
+
+def projection_partial(samples, sketches, delays, axis, gram):
     channels, block = samples.shape
-    half, width = mine.shape
-    rank = 2 * half
+    quarter, width = sketches[0][0].shape
+    count = 2 * quarter
+    rank = 2 * count
     steps = block // WIDE
-    rows = channels // 2
-    lanes = delays * rank
-    tail = rank // delays if part == 0 else 0
-
-    def body(s_ref, mine_ref, other_ref, keep_ref, send_ref, high_ref, low_ref, acc_ref, gram_ref):
+    lanes = delays * count
+    tail = rank * rank // lanes if gram else 0
+    flat = [half for pair in sketches for half in pair]
+
+    def body(s_ref, *refs):
+        ins, (keep_ref, send_ref, high_ref, low_ref, acc_ref, gram_ref) = refs[: len(flat)], refs[len(flat) :]
         step = pl.program_id(0)
 
         @pl.when(step == 0)
         def _():
-            core = lax.axis_index("core")
-            for ref, place in ((mine_ref, core), (other_ref, 1 - core)):
+            for place, ref in zip(quarters(), ins):
                 high, low = split(ref[...])
-                high_ref[rows_at(place, half), :] = high
-                low_ref[rows_at(place, half), :] = low
+                high_ref[rows_at(place, quarter), :] = high
+                low_ref[rows_at(place, quarter), :] = low
             acc_ref[...] = jnp.zeros_like(acc_ref)
             gram_ref[...] = jnp.zeros_like(gram_ref)
 
@@ -156,42 +168,42 @@
         highs, lows = [], []
         for d in range(delays):
             at = pl.ds(pl.multiple_of(step * WIDE + (delays - 1 - d) * LAG, LAG), WIDE)
-            highs.append(high_ref[:, at])
-            lows.append(low_ref[:, at])
-        if part == 0:
-            gram_ref[...] += dot3(highs[0], lows[0], highs[0], lows[0], NT)
+            for place in in_order(quarters()[len(flat) - 2 : len(flat)]):
+                highs.append(high_ref[rows_at(place, quarter), at])
+                lows.append(low_ref[rows_at(place, quarter), at])
+        if gram:
+            at = pl.ds(pl.multiple_of(step * WIDE + (delays - 1) * LAG, LAG), WIDE)
+            high, low = high_ref[:, at], low_ref[:, at]
+            gram_ref[...] += dot3(high, low, high, low, NT)
         acc_ref[...] += dot3(s_high, s_low, jnp.concatenate(highs, 0), jnp.concatenate(lows, 0), NT)
 
         @pl.when(step == steps - 1)
         def _():
             which = side(axis, 0)
             for place, ref in ((which, keep_ref), (1 - which, send_ref)):
-                ref[: rows // 2, :] = acc_ref[rows_at(place, rows // 2), :]
-                for d in range(delays if tail else 0):
-                    ref[rows // 2 :, d * rank : (d + 1) * rank] = gram_ref[d * tail : (d + 1) * tail, :]
-
-    shape = (rows // 2 + tail, lanes)
+                ref[: channels // 2, :] = acc_ref[rows_at(place, channels // 2), :]
+                for group in range(lanes // rank if gram else 0):
+                    ref[channels // 2 :, group * rank : (group + 1) * rank] = gram_ref[group * tail : (group + 1) * tail, :]
+
+    shape = (channels // 2 + tail, lanes)
     return pl.pallas_call(
         body,
         grid=(steps,),
         out_shape=[jax.ShapeDtypeStruct(shape, F32)] * 2,
-        in_specs=[
-            pl.BlockSpec((rows, WIDE), lambda i: (part, i)),
-            pl.BlockSpec((half, width), lambda i: (0, 0)),
-            pl.BlockSpec((half, width), lambda i: (0, 0)),
-        ],
+        in_specs=[pl.BlockSpec((channels, WIDE), lambda i: (0, i))]
+        + [pl.BlockSpec((quarter, width), lambda i: (0, 0))] * len(flat),
         out_specs=[pl.BlockSpec(shape, lambda i: (0, 0))] * 2,
         scratch_shapes=[
             pltpu.VMEM((rank, width), BF16),
             pltpu.VMEM((rank, width), BF16),
-            pltpu.VMEM((rows, lanes), F32),
+            pltpu.VMEM((channels, lanes), F32),
             pltpu.VMEM((rank, rank), F32),
         ],
         compiler_params=pltpu.CompilerParams(vmem_limit_bytes=36 * MIB),
         cost_estimate=pl.CostEstimate(
-            flops=6 * lanes * rows * block, bytes_accessed=rows * block * 4, transcendentals=0
+            flops=6 * lanes * channels * block, bytes_accessed=channels * block * 4, transcendentals=0
         ),
-    )(samples, mine, other)
+    )(samples, *flat)
 
 
 def fold(keep, came, axis, step, tail=0):
@@ -229,13 +241,29 @@
     return call(body, [(2 * count, mine.shape[1])], [mine, came], 8)[0]
 
 
-def summed(keep, send, one, two, tail=0):
-    keep, send = fold(keep, along(one, 0, send), one, 1, tail)
-    (value,) = add(keep, along(one, 1, send))
-    (value,) = add(value, along(two, 0, value))
-    value, *rest = add(value, along(two, 1, value), tail)
-    value = unfold(value, along(one, 1, value), one, 1)
-    return (value, along(one, 0, value), *rest)
+def advanced(at, keep, came, one, tail):
+    if at == 0:
+        return *fold(keep, came, one, 1, tail), None
+    if at == 4:
+        value = unfold(keep, came, one, 1)
+        return value, value, None
+    value, *rest = add(keep, came, tail if at == 3 else 0)
+    return value, value, *(rest or [None])
+
+
+def summed_both(first, second, tail):
+    states, tails = [first, second], (0, tail)
+    axes = (("x", "z"), ("z", "x"))
+    came = [along(axes[i][0], 0, states[i][1]) for i in range(2)]
+    for at in range(5):
+        for i in range(2):
+            arrived, _ = lax.optimization_barrier((came[i], states[1 - i][1]))
+            *states[i], rest = advanced(at, states[i][0], arrived, axes[i][0], tails[i])
+            one, two = axes[i]
+            came[i] = along(*((one, 1), (two, 0), (two, 1), (one, 1), (one, 0))[at], states[i][1])
+            if rest is not None:
+                last = rest
+    return (states[0][0], came[0]), (states[1][0], came[1]), last
 
 
 def inverse_factor(tail, rank):
@@ -287,77 +315,108 @@
     delays, channels, rank = omega.shape
     block = samples.shape[1]
     margin = (delays - 1) * LAG
+    inner = block - margin
     width = margin + block
-    half, share = rank // 2, rank // 4
+    half, quarter = rank // 2, rank // 4
     total = block * SIDE * SIDE
 
     keep, send = sketch_partial(samples, omega)
     came = lax.ppermute(send, "core", [(0, 1), (1, 0)])
-    keep, send = fold(keep, came, "y", 0)
-    came = along("y", 0, send)
-
-    def add_chips(a_ref, b_ref, main_ref, rim_ref):
-        main_ref[...] = a_ref[:, margin:] + b_ref[:, margin:]
-        rim_ref[...] = a_ref[:, :margin] + b_ref[:, :margin]
-
-    main, rim = call(add_chips, [(share, block), (share, margin)], [keep, came], 8)
-    rim_one = along("y", None, rim, -1)
-    rim_two = along("y", 1, rim, -1)
-    came = along("y", 1, main)
-
-    def add_rim(main_ref, came_ref, one_ref, two_ref, out_ref, last_ref):
-        inner = block - margin
-        out_ref[:, :inner] = main_ref[:, :inner] + came_ref[:, :inner]
-        value = (main_ref[:, inner:] + came_ref[:, inner:]) + (one_ref[...] + two_ref[...])
-        out_ref[:, inner:] = value
-        last_ref[...] = value
-
-    main, last = call(add_rim, [(share, block), (share, margin)], [main, came, rim_one, rim_two], 8)
-
-    before = along("y", None, last, 1)
-    before_came = along("y", 0, last, 1)
-    came = along("y", 0, main)
-
-    def join(before_ref, main_ref, before_came_ref, came_ref, out_ref):
+
+    def add_cores(a_ref, b_ref, *outs):
         which = side("y", 0)
-        for place, rim_ref, ref in ((which, before_ref, main_ref), (1 - which, before_came_ref, came_ref)):
-            out_ref[rows_at(place, share), :margin] = rim_ref[...]
-            out_ref[rows_at(place, share), margin:] = ref[...]
-
-    (mine,) = call(join, [(half, width)], [before, main, before_came, came], 8)
-    other = lax.ppermute(mine, "core", [(0, 1), (1, 0)])
-
-    first = projection_partial(samples, mine, other, delays, 0, "x")
-    second = projection_partial(samples, mine, other, delays, 1, "z")
-    first, first_came, gram = summed(*first, "x", "z", rank // delays)
-    second, second_came = summed(*second, "z", "x")
+        for to, place in ((0, which), (1, 1 - which)):
+            at = rows_at(place, quarter)
+            outs[to][:, :margin] = a_ref[at, :margin] + b_ref[at, :margin]
+            outs[to][:, margin:] = a_ref[at, block:] + b_ref[at, block:]
+            outs[2 + to][...] = a_ref[at, margin:block] + b_ref[at, margin:block]
+
+    shapes = [(quarter, 2 * margin)] * 2 + [(quarter, inner)] * 2
+    ends, ends_send, middle, middle_send = call(add_cores, shapes, [keep, came], 12)
+    ends_came = along("y", 0, ends_send)
+    middle_came = along("y", 0, middle_send)
+    (ends,) = add(ends, ends_came)
+    ends_came = along("y", 1, ends)
+    (middle,) = add(middle, middle_came)
+    middle_came = along("y", 1, middle)
+
+    def add_ends(a_ref, b_ref, left_ref, right_ref):
+        left_ref[...] = a_ref[:, :margin] + b_ref[:, :margin]
+        right_ref[...] = a_ref[:, margin:] + b_ref[:, margin:]
+
+    left, right = call(add_ends, [(quarter, margin)] * 2, [ends, ends_came], 8)
+    left_came = along("y", None, right, 1)
+    right_came = along("y", None, left, -1)
+
+    def join(left_ref, left_came_ref, right_ref, right_came_ref, middle_ref, middle_came_ref, out_ref):
+        inside = lax.axis_index("x") + lax.axis_index("z") > 0
+        out_ref[:, :margin] = jnp.where(inside, left_ref[...] + left_came_ref[...], 0.0)
+        out_ref[:, margin:block] = middle_ref[...] + middle_came_ref[...]
+        out_ref[:, block:] = right_ref[...] + right_came_ref[...]
+
+    (mine,) = call(join, [(quarter, width)], [left, left_came, right, right_came, middle, middle_came], 8)
+    sketches = [(mine, lax.ppermute(mine, "core", [(0, 1), (1, 0)]))]
+    mine = along("y", 0, mine)
+
+    first = projection_partial(samples, sketches, delays, "x", False)
+    mine, *first = lax.optimization_barrier((mine, *first))
+    sketches.append((mine, lax.ppermute(mine, "core", [(0, 1), (1, 0)])))
+    second = projection_partial(samples, sketches, delays, "z", True)
+    first, second, gram = summed_both(first, second, rank // 2)
     inverse = inverse_factor(gram, rank)
 
-    def finish(inverse_ref, mine_ref, other_ref, *refs):
-        ins, (basis_ref, out_ref) = refs[:4], refs[4:]
-        high, low = split(inverse_ref[...])
-        count = channels // 4
-        for part, axis in enumerate(("x", "z")):
-            which = side(axis, 0)
-            for place, ref in ((which, ins[2 * part]), (1 - which, ins[2 * part + 1])):
-                at = pl.ds(pl.multiple_of((2 * part + place) * count, count), count)
-                for d in range(delays):
-                    a_high, a_low = split(ref[:, d * rank : (d + 1) * rank])
-                    out_ref[d, at, :] = dot3(a_high, a_low, high, low, NT)
+    def multiplied(turned_ref, part, places, refs, add_to):
+        pick = [turned_ref[rows_at(q, quarter), :] for q in in_order(quarters()[2 * part : 2 * part + 2])]
+        none = [jnp.zeros((half, rank), F32)]
+        pick = [split(jnp.concatenate(m, 0)) for m in (pick + none, none + pick)]
+        for place, ref in zip(places, refs):
+            for pair in range(delays // 2):
+                a_high, a_low = split(ref[:, pair * rank : (pair + 1) * rank])
+                for odd in range(2):
+                    add_to(2 * pair + odd, rows_at(place, channels // 2), dot3(a_high, a_low, *pick[odd], NN))
+
+    def finish_first(inverse_ref, *refs):
+        rows, ins, (basis_ref, out_ref, turned_ref, sketch_ref) = refs[:4], refs[4:7], refs[7:]
+        turned_ref[...] = inverse_ref[...].T
+
+        def put(d, at, value):
+            out_ref[d, at, :] = value
+
+        def put_more(d, at, value):
+            out_ref[d, at, :] += value
+
+        which = side("x", 0)
+        multiplied(turned_ref, 0, (which, 1 - which), ins[:2], put)
+        multiplied(turned_ref, 1, (side("z", 0),), ins[2:], put_more)
         core, y = lax.axis_index("core"), lax.axis_index("y")
         columns = block // 8
         at = pl.ds(pl.multiple_of(margin + (y * 2 + core) * columns, columns), columns)
-        sketch = jnp.concatenate([mine_ref[:, at], other_ref[:, at]], 0)
-        swapped = jnp.concatenate([other_ref[:, at], mine_ref[:, at]], 0)
-        s_high, s_low = split(jnp.where(core == 0, sketch, swapped))
+        for place, ref in zip(quarters(), rows):
+            sketch_ref[rows_at(place, quarter), :] = ref[:, at]
+        high, low = split(inverse_ref[...])
+        s_high, s_low = split(sketch_ref[...])
         basis_ref[...] = math.sqrt(total) * dot3(high, low, s_high, s_low, NN)
 
-    basis, projection = call(
-        finish,
-        [(rank, block // 8), (delays, channels, rank)],
-        [inverse, mine, other, first, first_came, second, second_came],
+    shape = (delays, channels, rank)
+    basis, partial, turned = call(
+        finish_first,
+        [(rank, block // 8), shape, (rank, rank)],
+        [inverse, *sketches[0], *sketches[1], *first, second[0]],
         24,
+        [(rank, block // 8)],
     )
+
+    def finish_second(turned_ref, partial_ref, came_ref, out_ref):
+        def put(d, at, value):
+            out_ref[d, at, :] = partial_ref[d, at, :] + value
+
+        place = 1 - side("z", 0)
+        multiplied(turned_ref, 1, (place,), (came_ref,), put)
+        at = rows_at(1 - place, channels // 2)
+        for d in range(delays):
+            out_ref[d, at, :] = partial_ref[d, at, :]
+
+    (projection,) = call(finish_second, [shape], [turned, partial, second[1]], 24)
     return basis, projection
 
 

time: 154 us -> 141 us (0.916)
  waiting for transfers between devices: 71.9 us -> 58.2 us
  Pallas kernels: 44.6 us -> 48.8 us
  local copies, waits for them, and re-layouts: 1.58 us -> 0 us
    ppermute x19, waiting for transfers between devices: 65.5 us -> 52.4 us  [along(): return lax.ppermute(value, AXES, pairs)]
    ppermute x19, starting transfers between devices: 34 us -> 31.4 us  [along(): return lax.ppermute(value, AXES, pairs)]
    pallas_call x15 -> x17, Pallas kernels: 3.26 us -> 5.09 us  [call(): pl.pallas_call(body, out_shape=[jax.ShapeDtypeStruct(shape, F32) for shap...]
    pallas_call x2, Pallas kernels: 20 us -> 21.7 us  [projection_partial(): pl.pallas_call(body, grid=(steps,), out_shape=[jax.ShapeDtypeStruct(shape...]
    unnamed x2 -> x0, local copies, waits for them, and re-layouts: 1.58 us -> none
    ppermute x1 -> x2, waiting for transfers between devices: 3.2 us -> 2.58 us  [the longest x1 1.82 us: shards(): sketches.append((mine, lax.ppermute(mine, 'core', [(0, 1), (1, 0)])))]
  transfers between devices with their start and end apart: 21 -> 22, of which waited for: 15 -> 16; matrix products, arithmetic and copies ran while one was open for 0% -> 0% of each run, Pallas kernels for 9% -> 12%
where the time goes in v3:
time: 141 us; the launch traced here: 140 us
  waiting for transfers between devices  58.2 us (41%)
  Pallas kernels  48.8 us (35%)
  starting transfers between devices  32.7 us (23%)
    ppermute x19, waiting for transfers between devices, along(): return lax.ppermute(value, AXES, pairs)  52.4 us
    ppermute x19, starting transfers between devices, along(): return lax.ppermute(value, AXES, pairs)  31.4 us
    pallas_call x2, Pallas kernels, projection_partial(): pl.pallas_call(body, grid=(steps,), out_shape=[jax.ShapeDtypeStruct(shape...  21.7 us
    pallas_call x1, Pallas kernels, sketch_partial(): pl.pallas_call(body, grid=(steps,), out_shape=[out, out], in_specs=[pl.Bl...  17.7 us
    pallas_call x17, Pallas kernels, call(): pl.pallas_call(body, out_shape=[jax.ShapeDtypeStruct(shape, F32) for shap...  5.09 us
    pallas_call x1, Pallas kernels, inverse_factor(): pl.pallas_call(body, out_shape=jax.ShapeDtypeStruct((rank, rank), F32), i...  4.23 us
    ppermute x1, waiting for transfers between devices, shards(): came = lax.ppermute(send, 'core', [(0, 1), (1, 0)])  3.21 us
  transfers between devices with their start and end apart: 22, of which 16 were waited for; matrix products, arithmetic and copies ran while one was open for 0% of the time, Pallas kernels for 12%

profile of v3, /device:TPU:0, one launch (start us, length us, event | category | flops | bytes accessed | tf_op | source)
XLA Modules:
  0.0 140.4 jit_solution(10517035613962971729)
XLA Ops:
  0.6 17.7 %shard_map.41 = (f32[64,5632]{1,0:T(8,128)S(1)}, f32[64,5632]{1,0:T(8,128)S(1)}) custom-call(f32[1024,4096]{1,0:T(8,128)} %s_ref.5, f32[4,1024,128]{2,1,0:T(8,128)} %o_ref.1), custom_call_target="tpu_custom_call" | custom-call | flops 12884901888 | bytes 16777216 | tf_op jit(solution)/shard_map/pallas_call | solution.py:113
  18.3 0.1 collective-permute-start
  18.4 3.2 %collective-permute-done.b_ref = f32[64,5632]{1,0:T(8,128)S(1)} collective-permute-done((f32[64,5632]{1,0:T(8,128)S(1)}, f32[64,5632]{1,0:T(8,128)S(1)}, u32[]{:S(2)}, u32[]{:S(2)}) %collective-permute-start) | collective-permute-done | bytes 1441824 | tf_op jit(solution)/shard_map/ppermute | solution.py:324
  21.6 0.1 shard_map.42
  21.8 1.7 %collective-permute-start.1 = (f32[32,3072]{1,0:T(8,128)S(1)}, f32[32,3072]{1,0:T(8,128)S(1)}, u32[]{:S(2)}, u32[]{:S(2)}) collective-permute-start(f32[32,3072]{1,0:T(8,128)S(1)} %get-tuple-element.39), channel_id=1, source_target_pairs={{0,2},{1,7},{2,0},{3,5},{4,6},{5,3},{6,4},{7,1},{8,10},{9,15},{10,... | collective-permute-start | bytes 1179656 | tf_op jit(solution)/shard_map/ppermute | solution.py:62
  23.5 0.4 collective-permute-start.5
  23.9 5.8 %collective-permute-done.1.b_ref = f32[32,3072]{1,0:T(8,128)S(1)} collective-permute-done((f32[32,3072]{1,0:T(8,128)S(1)}, f32[32,3072]{1,0:T(8,128)S(1)}, u32[]{:S(2)}, u32[]{:S(2)}) %collective-permute-start.1) | collective-permute-done | bytes 393248 | tf_op jit(solution)/shard_map/ppermute | solution.py:62
  29.7 3.2 %collective-permute-start.2 = (f32[32,3072]{1,0:T(8,128)S(1)}, f32[32,3072]{1,0:T(8,128)S(1)}, u32[]{:S(2)}, u32[]{:S(2)}) collective-permute-start(f32[32,3072]{1,0:T(8,128)S(1)} %shard_map.43.a_ref), channel_id=1, source_target_pairs={{0,6},{1,3},{2,4},{3,1},{4,2},{5,7},{6,0},{7,5},{8,14},{9,11},{10,... | collective-permute-start | bytes 1179656 | tf_op jit(solution)/shard_map/ppermute | solution.py:62
  32.9 0.9 collective-permute-done.5.b_ref
  33.8 3.1 %collective-permute-start.6 = (f32[32,2560]{1,0:T(8,128)S(1)}, f32[32,2560]{1,0:T(8,128)S(1)}, u32[]{:S(2)}, u32[]{:S(2)}) collective-permute-start(f32[32,2560]{1,0:T(8,128)S(1)} %shard_map.45.middle_ref), channel_id=1, source_target_pairs={{0,6},{1,3},{2,4},{3,1},{4,2},{5,7},{6,0},{7,5},{8,14},{9,11},{10,... | collective-permute-start | bytes 983048 | tf_op jit(solution)/shard_map/ppermute | solution.py:62
  36.9 1.9 %collective-permute-done.2.b_ref = f32[32,3072]{1,0:T(8,128)S(1)} collective-permute-done((f32[32,3072]{1,0:T(8,128)S(1)}, f32[32,3072]{1,0:T(8,128)S(1)}, u32[]{:S(2)}, u32[]{:S(2)}) %collective-permute-start.2) | collective-permute-done | bytes 393248 | tf_op jit(solution)/shard_map/ppermute | solution.py:62
  38.8 3.9 %collective-permute-start.3 = (f32[32,1536]{1,0:T(8,128)S(1)}, f32[32,1536]{1,0:T(8,128)S(1)}, u32[]{:S(2)}, u32[]{:S(2)}) collective-permute-start(f32[32,1536]{1,0:T(8,128)S(1)} %get-tuple-element.41.right_ref), channel_id=1, source_target_pairs={{0,8},{1,9},{2,10},{3,11},{4,12},{5,13},{6,14},{7,15},{8,16},{9,17... | collective-permute-start | bytes 589832 | tf_op jit(solution)/shard_map/ppermute | solution.py:62
  42.7 1.3 collective-permute-start.4
  44.0 0.0 collective-permute-done.6.middle_came_ref
  44.0 1.8 %collective-permute-done.3.left_came_ref = f32[32,1536]{1,0:T(8,128)S(1)} collective-permute-done((f32[32,1536]{1,0:T(8,128)S(1)}, f32[32,1536]{1,0:T(8,128)S(1)}, u32[]{:S(2)}, u32[]{:S(2)}) %collective-permute-start.3) | collective-permute-done | bytes 196640 | tf_op jit(solution)/shard_map/ppermute | solution.py:62
  45.9 4.4 %collective-permute-done.4.right_came_ref = f32[32,1536]{1,0:T(8,128)S(1)} collective-permute-done((f32[32,1536]{1,0:T(8,128)S(1)}, f32[32,1536]{1,0:T(8,128)S(1)}, u32[]{:S(2)}, u32[]{:S(2)}) %collective-permute-start.4) | collective-permute-done | bytes 196640 | tf_op jit(solution)/shard_map/ppermute | solution.py:62
  50.3 0.1 shard_map.46.refs_0_
  50.4 0.1 collective-permute-start.7
  50.5 1.4 %collective-permute-start.8 = (f32[32,5632]{1,0:T(8,128)S(1)}, f32[32,5632]{1,0:T(8,128)S(1)}, u32[]{:S(2)}, u32[]{:S(2)}) collective-permute-start(f32[32,5632]{1,0:T(8,128)S(1)} %shard_map.46.refs_0_), channel_id=1, source_target_pairs={{0,2},{1,7},{2,0},{3,5},{4,6},{5,3},{6,4},{7,1},{8,10},{9,15},{10,... | collective-permute-start | bytes 2162696 | tf_op jit(solution)/shard_map/ppermute | solution.py:62
  51.9 0.8 collective-permute-done.7.refs_1_
  52.6 10.4 %shard_map.47 = (f32[512,256]{1,0:T(8,128)S(1)}, f32[512,256]{1,0:T(8,128)S(1)}) custom-call(f32[1024,4096]{1,0:T(8,128)} %s_ref.5, f32[32,5632]{1,0:T(8,128)S(1)} %shard_map.46.refs_0_, f32[32,5632]{1,0:T(8,128)S(1)} %collective-permute-done.7.refs_1_), custom_call_target="tpu_custom_call" | custom-call | flops 6442450944 | bytes 16777216 | tf_op jit(solution)/shard_map/pallas_call | solution.py:189
  63.1 0.0 collective-permute-done.8.refs_2_
  63.1 1.1 collective-permute-start.9
  64.2 1.8 %collective-permute-done.9.refs_3_ = f32[32,5632]{1,0:T(8,128)S(1)} collective-permute-done((f32[32,5632]{1,0:T(8,128)S(1)}, f32[32,5632]{1,0:T(8,128)S(1)}, u32[]{:S(2)}, u32[]{:S(2)}) %collective-permute-start.9) | collective-permute-done | bytes 720928 | tf_op jit(solution)/shard_map/ppermute | solution.py:363
  66.1 11.3 %shard_map.48 = (f32[576,256]{1,0:T(8,128)S(1)}, f32[576,256]{1,0:T(8,128)S(1)}) custom-call(f32[1024,4096]{1,0:T(8,128)} %s_ref.5, f32[32,5632]{1,0:T(8,128)S(1)} %shard_map.46.refs_0_, f32[32,5632]{1,0:T(8,128)S(1)} %collective-permute-done.7.refs_1_, f32[32,5632]{1,0:T(8,128)S(1)} %collective-permute-done.8.refs_2_, ...), custom_call_target="tpu_custom_call" | custom-call | flops 6442450944 | bytes 16777216 | tf_op jit(solution)/shard_map/pallas_call | solution.py:189
  77.4 2.0 %collective-permute-start.10 = (f32[576,256]{1,0:T(8,128)S(1)}, f32[576,256]{1,0:T(8,128)S(1)}, u32[]{:S(2)}, u32[]{:S(2)}) collective-permute-start(f32[576,256]{1,0:T(8,128)S(1)} %get-tuple-element.48), channel_id=1, source_target_pairs={{0,8},{1,25},{2,10},{3,27},{4,12},{5,29},{6,14},{7,31},{8,0},{9,17... | collective-permute-start | bytes 1769480 | tf_op jit(solution)/shard_map/ppermute | solution.py:62
  79.4 1.5 %collective-permute-start.11 = (f32[512,256]{1,0:T(8,128)S(1)}, f32[512,256]{1,0:T(8,128)S(1)}, u32[]{:S(2)}, u32[]{:S(2)}) collective-permute-start(f32[512,256]{1,0:T(8,128)S(1)} %get-tuple-element.50), channel_id=1, source_target_pairs={{0,32},{1,97},{2,34},{3,99},{4,36},{5,101},{6,38},{7,103},{8,40},{... | collective-permute-start | bytes 1572872 | tf_op jit(solution)/shard_map/ppermute | solution.py:62
  80.9 7.7 %collective-permute-done.11.b_ref = f32[512,256]{1,0:T(8,128)S(1)} collective-permute-done((f32[512,256]{1,0:T(8,128)S(1)}, f32[512,256]{1,0:T(8,128)S(1)}, u32[]{:S(2)}, u32[]{:S(2)}) %collective-permute-start.11) | collective-permute-done | bytes 524320 | tf_op jit(solution)/shard_map/ppermute | solution.py:62
  88.6 0.1 shard_map.49
  88.6 0.0 collective-permute-done.10.b_ref
  88.6 0.1 shard_map.50
  88.7 3.1 %collective-permute-start.12 = (f32[320,256]{1,0:T(8,128)S(1)}, f32[320,256]{1,0:T(8,128)S(1)}, u32[]{:S(2)}, u32[]{:S(2)}) collective-permute-start(f32[320,256]{1,0:T(8,128)S(1)} %get-tuple-element.55), channel_id=1, source_target_pairs={{0,24},{1,9},{2,26},{3,11},{4,28},{5,13},{6,30},{7,15},{8,16},{9,1... | collective-permute-start | bytes 983048 | tf_op jit(solution)/shard_map/ppermute | solution.py:62
  91.9 1.9 %collective-permute-start.13 = (f32[256,256]{1,0:T(8,128)S(1)}, f32[256,256]{1,0:T(8,128)S(1)}, u32[]{:S(2)}, u32[]{:S(2)}) collective-permute-start(f32[256,256]{1,0:T(8,128)S(1)} %get-tuple-element.52), channel_id=1, source_target_pairs={{0,96},{1,33},{2,98},{3,35},{4,100},{5,37},{6,102},{7,39},{8,104},... | collective-permute-start | bytes 786440 | tf_op jit(solution)/shard_map/ppermute | solution.py:62
  93.8 5.7 %collective-permute-done.13.b_ref = f32[256,256]{1,0:T(8,128)S(1)} collective-permute-done((f32[256,256]{1,0:T(8,128)S(1)}, f32[256,256]{1,0:T(8,128)S(1)}, u32[]{:S(2)}, u32[]{:S(2)}) %collective-permute-start.13) | collective-permute-done | bytes 262176 | tf_op jit(solution)/shard_map/ppermute | solution.py:62
  99.5 0.0 collective-permute-done.12.b_ref
  99.5 0.4 collective-permute-start.14
  99.9 0.8 collective-permute-start.15
  100.7 5.6 %collective-permute-done.15.b_ref = f32[256,256]{1,0:T(8,128)S(1)} collective-permute-done((f32[256,256]{1,0:T(8,128)S(1)}, f32[256,256]{1,0:T(8,128)S(1)}, u32[]{:S(2)}, u32[]{:S(2)}) %collective-permute-start.15) | collective-permute-done | bytes 262176 | tf_op jit(solution)/shard_map/ppermute | solution.py:62
  106.3 0.4 collective-permute-done.14.b_ref
  106.7 2.0 %collective-permute-start.16 = (f32[320,256]{1,0:T(8,128)S(1)}, f32[320,256]{1,0:T(8,128)S(1)}, u32[]{:S(2)}, u32[]{:S(2)}) collective-permute-start(f32[320,256]{1,0:T(8,128)S(1)} %shard_map.54.a_ref), channel_id=1, source_target_pairs={{0,96},{1,33},{2,98},{3,35},{4,100},{5,37},{6,102},{7,39},{8,104},... | collective-permute-start | bytes 983048 | tf_op jit(solution)/shard_map/ppermute | solution.py:62
  108.7 1.6 %collective-permute-start.17 = (f32[256,256]{1,0:T(8,128)S(1)}, f32[256,256]{1,0:T(8,128)S(1)}, u32[]{:S(2)}, u32[]{:S(2)}) collective-permute-start(f32[256,256]{1,0:T(8,128)S(1)} %shard_map.53.a_ref), channel_id=1, source_target_pairs={{0,24},{1,9},{2,26},{3,11},{4,28},{5,13},{6,30},{7,15},{8,16},{9,1... | collective-permute-start | bytes 786440 | tf_op jit(solution)/shard_map/ppermute | solution.py:62
  110.3 6.0 %collective-permute-done.17.b_ref = f32[256,256]{1,0:T(8,128)S(1)} collective-permute-done((f32[256,256]{1,0:T(8,128)S(1)}, f32[256,256]{1,0:T(8,128)S(1)}, u32[]{:S(2)}, u32[]{:S(2)}) %collective-permute-start.17) | collective-permute-done | bytes 262176 | tf_op jit(solution)/shard_map/ppermute | solution.py:62
  116.3 1.4 collective-permute-start.18
  117.7 0.0 collective-permute-done.16.b_ref
  117.8 1.6 %collective-permute-start.20 = (f32[256,256]{1,0:T(8,128)S(1)}, f32[256,256]{1,0:T(8,128)S(1)}, u32[]{:S(2)}, u32[]{:S(2)}) collective-permute-start(f32[256,256]{1,0:T(8,128)S(1)} %get-tuple-element.64.a_ref), channel_id=1, source_target_pairs={{0,24},{1,9},{2,26},{3,11},{4,28},{5,13},{6,30},{7,15},{8,16},{9,1... | collective-permute-start | bytes 786440 | tf_op jit(solution)/shard_map/ppermute | solution.py:62
  119.3 7.5 %collective-permute-done.18.b_ref = f32[256,256]{1,0:T(8,128)S(1)} collective-permute-done((f32[256,256]{1,0:T(8,128)S(1)}, f32[256,256]{1,0:T(8,128)S(1)}, u32[]{:S(2)}, u32[]{:S(2)}) %collective-permute-start.18) | collective-permute-done | bytes 262176 | tf_op jit(solution)/shard_map/ppermute | solution.py:62
  126.8 0.1 shard_map.58.refs_4_
  126.9 0.1 collective-permute-start.19
  127.0 1.2 collective-permute-done.20.b_ref
  128.2 0.1 shard_map.59.refs_6_
  128.3 0.1 collective-permute-start.21
  128.3 4.2 %shard_map.57.inverse_ref = f32[128,128]{1,0:T(8,128)S(1)} custom-call(f32[64,256]{1,0:T(8,128)S(1)} %get-tuple-element.63.tail_ref), custom_call_target="tpu_custom_call" | custom-call | tf_op jit(solution)/shard_map/pallas_call | solution.py:304
  132.6 3.5 %collective-permute-done.19.refs_5_ = f32[512,256]{1,0:T(8,128)S(1)} collective-permute-done((f32[512,256]{1,0:T(8,128)S(1)}, f32[512,256]{1,0:T(8,128)S(1)}, u32[]{:S(2)}, u32[]{:S(2)}) %collective-permute-start.19) | collective-permute-done | bytes 524320 | tf_op jit(solution)/shard_map/ppermute | solution.py:62
  136.1 2.3 %shard_map.60 = (f32[128,512]{1,0:T(8,128)}, f32[4,1024,128]{2,1,0:T(8,128)S(1)}, f32[128,128]{1,0:T(8,128)S(1)}) custom-call(f32[128,128]{1,0:T(8,128)S(1)} %shard_map.57.inverse_ref, f32[32,5632]{1,0:T(8,128)S(1)} %shard_map.46.refs_0_, f32[32,5632]{1,0:T(8,128)S(1)} %collective-permute-done.7.refs_1_, f32[32,5632]{1,0:T(8,128)S(1)} %collective-permute-done.8.refs_2_, ...), custom_call_target="tpu_custom_call" | custom-call | tf_op jit(solution)/shard_map/pallas_call | solution.py:36
  138.4 0.0 collective-permute-done.21.came_ref
  138.4 2.0 %shard_map.61 = f32[4,1024,128]{2,1,0:T(8,128)} custom-call(f32[128,128]{1,0:T(8,128)S(1)} %get-tuple-element.68.turned_ref, f32[4,1024,128]{2,1,0:T(8,128)S(1)} %get-tuple-element.69.partial_ref, f32[512,256]{1,0:T(8,128)S(1)} %collective-permute-done.21.came_ref), custom_call_target="tpu_custom_call" | custom-call | tf_op jit(solution)/shard_map/pallas_call | solution.py:36
  (9 shorter events, 0.3 us)
Async XLA Ops:
  18.3 3.3 %collective-permute-start = (f32[64,5632]{1,0:T(8,128)S(1)}, f32[64,5632]{1,0:T(8,128)S(1)}, u32[]{:S(2)}, u32[]{:S(2)}) collective-permute-start(f32[64,5632]{1,0:T(8,128)S(1)} %get-tuple-element.37), channel_id=1, source_target_pairs={{0,1},{1,0},{2,3},{3,2},{4,5},{5,4},{6,7},{7,6},{8,9},{9,8},{10,11... | collective-permute-start | bytes 4325384 | tf_op jit(solution)/shard_map/ppermute | solution.py:324
  21.8 7.9 %collective-permute-start.1 = (f32[32,3072]{1,0:T(8,128)S(1)}, f32[32,3072]{1,0:T(8,128)S(1)}, u32[]{:S(2)}, u32[]{:S(2)}) collective-permute-start(f32[32,3072]{1,0:T(8,128)S(1)} %get-tuple-element.39), channel_id=1, source_target_pairs={{0,2},{1,7},{2,0},{3,5},{4,6},{5,3},{6,4},{7,1},{8,10},{9,15},{10,... | collective-permute-start | bytes 1179656 | tf_op jit(solution)/shard_map/ppermute | solution.py:62
  23.5 10.2 %collective-permute-start.5 = (f32[32,2560]{1,0:T(8,128)S(1)}, f32[32,2560]{1,0:T(8,128)S(1)}, u32[]{:S(2)}, u32[]{:S(2)}) collective-permute-start(f32[32,2560]{1,0:T(8,128)S(1)} %get-tuple-element.43), channel_id=1, source_target_pairs={{0,2},{1,7},{2,0},{3,5},{4,6},{5,3},{6,4},{7,1},{8,10},{9,15},{10,... | collective-permute-start | bytes 983048 | tf_op jit(solution)/shard_map/ppermute | solution.py:62
  29.7 9.1 %collective-permute-start.2 = (f32[32,3072]{1,0:T(8,128)S(1)}, f32[32,3072]{1,0:T(8,128)S(1)}, u32[]{:S(2)}, u32[]{:S(2)}) collective-permute-start(f32[32,3072]{1,0:T(8,128)S(1)} %shard_map.43.a_ref), channel_id=1, source_target_pairs={{0,6},{1,3},{2,4},{3,1},{4,2},{5,7},{6,0},{7,5},{8,14},{9,11},{10,... | collective-permute-start | bytes 1179656 | tf_op jit(solution)/shard_map/ppermute | solution.py:62
  33.8 10.2 %collective-permute-start.6 = (f32[32,2560]{1,0:T(8,128)S(1)}, f32[32,2560]{1,0:T(8,128)S(1)}, u32[]{:S(2)}, u32[]{:S(2)}) collective-permute-start(f32[32,2560]{1,0:T(8,128)S(1)} %shard_map.45.middle_ref), channel_id=1, source_target_pairs={{0,6},{1,3},{2,4},{3,1},{4,2},{5,7},{6,0},{7,5},{8,14},{9,11},{10,... | collective-permute-start | bytes 983048 | tf_op jit(solution)/shard_map/ppermute | solution.py:62
  38.8 7.1 %collective-permute-start.3 = (f32[32,1536]{1,0:T(8,128)S(1)}, f32[32,1536]{1,0:T(8,128)S(1)}, u32[]{:S(2)}, u32[]{:S(2)}) collective-permute-start(f32[32,1536]{1,0:T(8,128)S(1)} %get-tuple-element.41.right_ref), channel_id=1, source_target_pairs={{0,8},{1,9},{2,10},{3,11},{4,12},{5,13},{6,14},{7,15},{8,16},{9,17... | collective-permute-start | bytes 589832 | tf_op jit(solution)/shard_map/ppermute | solution.py:62
  42.7 7.6 %collective-permute-start.4 = (f32[32,1536]{1,0:T(8,128)S(1)}, f32[32,1536]{1,0:T(8,128)S(1)}, u32[]{:S(2)}, u32[]{:S(2)}) collective-permute-start(f32[32,1536]{1,0:T(8,128)S(1)} %get-tuple-element.40.left_ref), channel_id=1, source_target_pairs={{8,0},{9,1},{10,2},{11,3},{12,4},{13,5},{14,6},{15,7},{16,8},{17,9... | collective-permute-start | bytes 589832 | tf_op jit(solution)/shard_map/ppermute | solution.py:62
  50.4 2.3 %collective-permute-start.7 = (f32[32,5632]{1,0:T(8,128)S(1)}, f32[32,5632]{1,0:T(8,128)S(1)}, u32[]{:S(2)}, u32[]{:S(2)}) collective-permute-start(f32[32,5632]{1,0:T(8,128)S(1)} %shard_map.46.refs_0_), channel_id=1, source_target_pairs={{0,1},{1,0},{2,3},{3,2},{4,5},{5,4},{6,7},{7,6},{8,9},{9,8},{10,11... | collective-permute-start | bytes 2162696 | tf_op jit(solution)/shard_map/ppermute | solution.py:358
  50.5 12.6 %collective-permute-start.8 = (f32[32,5632]{1,0:T(8,128)S(1)}, f32[32,5632]{1,0:T(8,128)S(1)}, u32[]{:S(2)}, u32[]{:S(2)}) collective-permute-start(f32[32,5632]{1,0:T(8,128)S(1)} %shard_map.46.refs_0_), channel_id=1, source_target_pairs={{0,2},{1,7},{2,0},{3,5},{4,6},{5,3},{6,4},{7,1},{8,10},{9,15},{10,... | collective-permute-start | bytes 2162696 | tf_op jit(solution)/shard_map/ppermute | solution.py:62
  63.1 3.0 %collective-permute-start.9 = (f32[32,5632]{1,0:T(8,128)S(1)}, f32[32,5632]{1,0:T(8,128)S(1)}, u32[]{:S(2)}, u32[]{:S(2)}) collective-permute-start(f32[32,5632]{1,0:T(8,128)S(1)} %collective-permute-done.8.refs_2_), channel_id=1, source_target_pairs={{0,1},{1,0},{2,3},{3,2},{4,5},{5,4},{6,7},{7,6},{8,9},{9,8},{10,11... | collective-permute-start | bytes 2162696 | tf_op jit(solution)/shard_map/ppermute | solution.py:363
  77.4 11.2 %collective-permute-start.10 = (f32[576,256]{1,0:T(8,128)S(1)}, f32[576,256]{1,0:T(8,128)S(1)}, u32[]{:S(2)}, u32[]{:S(2)}) collective-permute-start(f32[576,256]{1,0:T(8,128)S(1)} %get-tuple-element.48), channel_id=1, source_target_pairs={{0,8},{1,25},{2,10},{3,27},{4,12},{5,29},{6,14},{7,31},{8,0},{9,17... | collective-permute-start | bytes 1769480 | tf_op jit(solution)/shard_map/ppermute | solution.py:62
  79.4 9.2 %collective-permute-start.11 = (f32[512,256]{1,0:T(8,128)S(1)}, f32[512,256]{1,0:T(8,128)S(1)}, u32[]{:S(2)}, u32[]{:S(2)}) collective-permute-start(f32[512,256]{1,0:T(8,128)S(1)} %get-tuple-element.50), channel_id=1, source_target_pairs={{0,32},{1,97},{2,34},{3,99},{4,36},{5,101},{6,38},{7,103},{8,40},{... | collective-permute-start | bytes 1572872 | tf_op jit(solution)/shard_map/ppermute | solution.py:62
  88.7 10.8 %collective-permute-start.12 = (f32[320,256]{1,0:T(8,128)S(1)}, f32[320,256]{1,0:T(8,128)S(1)}, u32[]{:S(2)}, u32[]{:S(2)}) collective-permute-start(f32[320,256]{1,0:T(8,128)S(1)} %get-tuple-element.55), channel_id=1, source_target_pairs={{0,24},{1,9},{2,26},{3,11},{4,28},{5,13},{6,30},{7,15},{8,16},{9,1... | collective-permute-start | bytes 983048 | tf_op jit(solution)/shard_map/ppermute | solution.py:62
  91.9 7.6 %collective-permute-start.13 = (f32[256,256]{1,0:T(8,128)S(1)}, f32[256,256]{1,0:T(8,128)S(1)}, u32[]{:S(2)}, u32[]{:S(2)}) collective-permute-start(f32[256,256]{1,0:T(8,128)S(1)} %get-tuple-element.52), channel_id=1, source_target_pairs={{0,96},{1,33},{2,98},{3,35},{4,100},{5,37},{6,102},{7,39},{8,104},... | collective-permute-start | bytes 786440 | tf_op jit(solution)/shard_map/ppermute | solution.py:62
  99.5 7.2 %collective-permute-start.14 = (f32[320,256]{1,0:T(8,128)S(1)}, f32[320,256]{1,0:T(8,128)S(1)}, u32[]{:S(2)}, u32[]{:S(2)}) collective-permute-start(f32[320,256]{1,0:T(8,128)S(1)} %shard_map.52.a_ref), channel_id=1, source_target_pairs={{0,32},{1,97},{2,34},{3,99},{4,36},{5,101},{6,38},{7,103},{8,40},{... | collective-permute-start | bytes 983048 | tf_op jit(solution)/shard_map/ppermute | solution.py:62
  99.9 6.4 %collective-permute-start.15 = (f32[256,256]{1,0:T(8,128)S(1)}, f32[256,256]{1,0:T(8,128)S(1)}, u32[]{:S(2)}, u32[]{:S(2)}) collective-permute-start(f32[256,256]{1,0:T(8,128)S(1)} %shard_map.51.a_ref), channel_id=1, source_target_pairs={{0,8},{1,25},{2,10},{3,27},{4,12},{5,29},{6,14},{7,31},{8,0},{9,17... | collective-permute-start | bytes 786440 | tf_op jit(solution)/shard_map/ppermute | solution.py:62
  106.7 11.0 %collective-permute-start.16 = (f32[320,256]{1,0:T(8,128)S(1)}, f32[320,256]{1,0:T(8,128)S(1)}, u32[]{:S(2)}, u32[]{:S(2)}) collective-permute-start(f32[320,256]{1,0:T(8,128)S(1)} %shard_map.54.a_ref), channel_id=1, source_target_pairs={{0,96},{1,33},{2,98},{3,35},{4,100},{5,37},{6,102},{7,39},{8,104},... | collective-permute-start | bytes 983048 | tf_op jit(solution)/shard_map/ppermute | solution.py:62
  108.7 7.6 %collective-permute-start.17 = (f32[256,256]{1,0:T(8,128)S(1)}, f32[256,256]{1,0:T(8,128)S(1)}, u32[]{:S(2)}, u32[]{:S(2)}) collective-permute-start(f32[256,256]{1,0:T(8,128)S(1)} %shard_map.53.a_ref), channel_id=1, source_target_pairs={{0,24},{1,9},{2,26},{3,11},{4,28},{5,13},{6,30},{7,15},{8,16},{9,1... | collective-permute-start | bytes 786440 | tf_op jit(solution)/shard_map/ppermute | solution.py:62
  116.3 10.5 %collective-permute-start.18 = (f32[256,256]{1,0:T(8,128)S(1)}, f32[256,256]{1,0:T(8,128)S(1)}, u32[]{:S(2)}, u32[]{:S(2)}) collective-permute-start(f32[256,256]{1,0:T(8,128)S(1)} %shard_map.55.a_ref), channel_id=1, source_target_pairs={{0,96},{1,33},{2,98},{3,35},{4,100},{5,37},{6,102},{7,39},{8,104},... | collective-permute-start | bytes 786440 | tf_op jit(solution)/shard_map/ppermute | solution.py:62
  117.8 10.4 %collective-permute-start.20 = (f32[256,256]{1,0:T(8,128)S(1)}, f32[256,256]{1,0:T(8,128)S(1)}, u32[]{:S(2)}, u32[]{:S(2)}) collective-permute-start(f32[256,256]{1,0:T(8,128)S(1)} %get-tuple-element.64.a_ref), channel_id=1, source_target_pairs={{0,24},{1,9},{2,26},{3,11},{4,28},{5,13},{6,30},{7,15},{8,16},{9,1... | collective-permute-start | bytes 786440 | tf_op jit(solution)/shard_map/ppermute | solution.py:62
  126.9 9.3 %collective-permute-start.19 = (f32[512,256]{1,0:T(8,128)S(1)}, f32[512,256]{1,0:T(8,128)S(1)}, u32[]{:S(2)}, u32[]{:S(2)}) collective-permute-start(f32[512,256]{1,0:T(8,128)S(1)} %shard_map.58.refs_4_), channel_id=1, source_target_pairs={{0,32},{1,97},{2,34},{3,99},{4,36},{5,101},{6,38},{7,103},{8,40},{... | collective-permute-start | bytes 1572872 | tf_op jit(solution)/shard_map/ppermute | solution.py:62
  128.3 10.1 %collective-permute-start.21 = (f32[512,256]{1,0:T(8,128)S(1)}, f32[512,256]{1,0:T(8,128)S(1)}, u32[]{:S(2)}, u32[]{:S(2)}) collective-permute-start(f32[512,256]{1,0:T(8,128)S(1)} %shard_map.59.refs_6_), channel_id=1, source_target_pairs={{0,8},{1,25},{2,10},{3,27},{4,12},{5,29},{6,14},{7,31},{8,0},{9,17... | collective-permute-start | bytes 1572872 | tf_op jit(solution)/shard_map/ppermute | solution.py:62

commit v4 on v3

--- a/solution.py
+++ b/solution.py
@@ -11,11 +11,13 @@
 
 LAG = 512
 WIDE = 1024
+AHEAD = 3
 F32 = jnp.float32
 BF16 = jnp.bfloat16
 NT = (((1,), (1,)), ((), ()))
 NN = (((1,), (0,)), ((), ()))
 MIB = 1024 * 1024
+WEIGHT = int(2e10)
 
 
 def split(value):
@@ -32,7 +34,7 @@
     return [pl.BlockSpec(memory_space=pltpu.VMEM)] * count
 
 
-def call(body, outs, args, limit=24, scratch=()):
+def call(body, outs, args, limit=24, scratch=(), weight=0):
     return pl.pallas_call(
         body,
         out_shape=[jax.ShapeDtypeStruct(shape, F32) for shape in outs],
@@ -40,6 +42,7 @@
         out_specs=whole(len(outs)),
         scratch_shapes=[pltpu.VMEM(shape, F32) for shape in scratch],
         compiler_params=pltpu.CompilerParams(vmem_limit_bytes=limit * MIB),
+        cost_estimate=pl.CostEstimate(flops=weight, bytes_accessed=0, transcendentals=0) if weight else None,
     )(*args)
 
 
@@ -85,46 +88,56 @@
     margin = (delays - 1) * LAG
     half = rank // 2
 
-    def body(s_ref, o_ref, keep_ref, send_ref, high_ref, low_ref, acc_ref):
-        step = pl.program_id(0)
-
-        @pl.when(step == 0)
-        def _():
+    def body(s_hbm, o_hbm, keep_ref, send_ref, s_ref, o_ref, high_ref, low_ref, acc_ref, s_sem, o_sem):
+        def fetch(step):
+            at = pl.ds(pl.multiple_of(step * LAG, LAG), LAG)
+            return pltpu.make_async_copy(s_hbm.at[:, at], s_ref.at[:, at], s_sem.at[step])
+
+        fetch_omega = pltpu.make_async_copy(o_hbm, o_ref, o_sem)
+        fetch_omega.start()
+        fetch(0).start()
+        acc_ref[...] = jnp.zeros_like(acc_ref)
+        fetch_omega.wait()
+        for step in range(1, AHEAD):
+            fetch(step).start()
+        for d in range(delays):
+            high, low = split(o_ref[d].T)
+            high_ref[d * rank : (d + 1) * rank, :] = high
+            low_ref[d * rank : (d + 1) * rank, :] = low
+
+        @pl.loop(0, steps)
+        def _(step):
+            fetch(step).wait()
+
+            @pl.when(step + AHEAD < steps)
+            def _():
+                fetch(step + AHEAD).start()
+
+            s_high, s_low = split(s_ref[:, pl.ds(pl.multiple_of(step * LAG, LAG), LAG)])
+            term = dot3(high_ref[...], low_ref[...], s_high, s_low, NN)
             for d in range(delays):
-                high, low = split(o_ref[d].T)
-                high_ref[d * rank : (d + 1) * rank, :] = high
-                low_ref[d * rank : (d + 1) * rank, :] = low
-            acc_ref[...] = jnp.zeros_like(acc_ref)
-
-        s_high, s_low = split(s_ref[...])
-        term = dot3(high_ref[...], low_ref[...], s_high, s_low, NN)
-        for d in range(delays):
-            at = pl.ds(pl.multiple_of((step + delays - 1 - d) * LAG, LAG), LAG)
-            acc_ref[:, at] += term[d * rank : (d + 1) * rank, :]
-
-        @pl.when(step == steps - 1)
-        def _():
-            core = lax.axis_index("core")
-            keep_ref[...] = acc_ref[rows_at(core, half), :]
-            send_ref[...] = acc_ref[rows_at(1 - core, half), :]
+                at = pl.ds(pl.multiple_of((step + delays - 1 - d) * LAG, LAG), LAG)
+                acc_ref[:, at] += term[d * rank : (d + 1) * rank, :]
+
+        core = lax.axis_index("core")
+        keep_ref[...] = acc_ref[rows_at(core, half), :]
+        send_ref[...] = acc_ref[rows_at(1 - core, half), :]
 
     out = jax.ShapeDtypeStruct((half, margin + block), F32)
-    spec = pl.BlockSpec((half, margin + block), lambda i: (0, 0))
     return pl.pallas_call(
         body,
-        grid=(steps,),
-        out_shape=[out, out],
-        in_specs=[
-            pl.BlockSpec((channels, LAG), lambda i: (0, i)),
-            pl.BlockSpec(omega.shape, lambda i: (0, 0, 0)),
-        ],
-        out_specs=[spec, spec],
+        out_shape=[out, out, pltpu.VMEM(samples.shape, F32)],
+        in_specs=[pl.BlockSpec(memory_space=pltpu.HBM)] * 2,
+        out_specs=whole(3),
         scratch_shapes=[
+            pltpu.VMEM(omega.shape, F32),
             pltpu.VMEM((delays * rank, channels), BF16),
             pltpu.VMEM((delays * rank, channels), BF16),
             pltpu.VMEM((rank, margin + block), F32),
+            pltpu.SemaphoreType.DMA((steps,)),
+            pltpu.SemaphoreType.DMA,
         ],
-        compiler_params=pltpu.CompilerParams(vmem_limit_bytes=40 * MIB),
+        compiler_params=pltpu.CompilerParams(vmem_limit_bytes=20 * MIB),
         cost_estimate=pl.CostEstimate(
             flops=6 * delays * rank * channels * block, bytes_accessed=samples.size * 4, transcendentals=0
         ),
@@ -141,69 +154,70 @@
     return jnp.minimum(*places), jnp.maximum(*places)
 
 
-def projection_partial(samples, sketches, delays, axis, gram):
+def projection_partial(samples, sketch, delays, axis):
     channels, block = samples.shape
-    quarter, width = sketches[0][0].shape
+    quarter, width = sketch[0].shape
     count = 2 * quarter
-    rank = 2 * count
     steps = block // WIDE
     lanes = delays * count
-    tail = rank * rank // lanes if gram else 0
-    flat = [half for pair in sketches for half in pair]
-
-    def body(s_ref, *refs):
-        ins, (keep_ref, send_ref, high_ref, low_ref, acc_ref, gram_ref) = refs[: len(flat)], refs[len(flat) :]
-        step = pl.program_id(0)
-
-        @pl.when(step == 0)
-        def _():
-            for place, ref in zip(quarters(), ins):
-                high, low = split(ref[...])
-                high_ref[rows_at(place, quarter), :] = high
-                low_ref[rows_at(place, quarter), :] = low
-            acc_ref[...] = jnp.zeros_like(acc_ref)
-            gram_ref[...] = jnp.zeros_like(gram_ref)
-
-        s_high, s_low = split(s_ref[...])
-        highs, lows = [], []
-        for d in range(delays):
-            at = pl.ds(pl.multiple_of(step * WIDE + (delays - 1 - d) * LAG, LAG), WIDE)
-            for place in in_order(quarters()[len(flat) - 2 : len(flat)]):
-                highs.append(high_ref[rows_at(place, quarter), at])
-                lows.append(low_ref[rows_at(place, quarter), at])
-        if gram:
-            at = pl.ds(pl.multiple_of(step * WIDE + (delays - 1) * LAG, LAG), WIDE)
-            high, low = high_ref[:, at], low_ref[:, at]
-            gram_ref[...] += dot3(high, low, high, low, NT)
-        acc_ref[...] += dot3(s_high, s_low, jnp.concatenate(highs, 0), jnp.concatenate(lows, 0), NT)
-
-        @pl.when(step == steps - 1)
-        def _():
-            which = side(axis, 0)
-            for place, ref in ((which, keep_ref), (1 - which, send_ref)):
-                ref[: channels // 2, :] = acc_ref[rows_at(place, channels // 2), :]
-                for group in range(lanes // rank if gram else 0):
-                    ref[channels // 2 :, group * rank : (group + 1) * rank] = gram_ref[group * tail : (group + 1) * tail, :]
-
-    shape = (channels // 2 + tail, lanes)
+
+    def body(s_ref, mine_ref, other_ref, keep_ref, send_ref, high_ref, low_ref, acc_ref):
+        core = lax.axis_index("core")
+        for place, ref in ((core, mine_ref), (1 - core, other_ref)):
+            high, low = split(ref[...])
+            high_ref[rows_at(place, quarter), :] = high
+            low_ref[rows_at(place, quarter), :] = low
+        acc_ref[...] = jnp.zeros_like(acc_ref)
+
+        @pl.loop(0, steps)
+        def _(step):
+            s_high, s_low = split(s_ref[:, pl.ds(pl.multiple_of(step * WIDE, WIDE), WIDE)])
+            highs, lows = [], []
+            for d in range(delays):
+                at = pl.ds(pl.multiple_of(step * WIDE + (delays - 1 - d) * LAG, LAG), WIDE)
+                highs.append(high_ref[:, at])
+                lows.append(low_ref[:, at])
+            acc_ref[...] += dot3(s_high, s_low, jnp.concatenate(highs, 0), jnp.concatenate(lows, 0), NT)
+
+        which = side(axis, 0)
+        for place, ref in ((which, keep_ref), (1 - which, send_ref)):
+            ref[...] = acc_ref[rows_at(place, channels // 2), :]
+
     return pl.pallas_call(
         body,
-        grid=(steps,),
-        out_shape=[jax.ShapeDtypeStruct(shape, F32)] * 2,
-        in_specs=[pl.BlockSpec((channels, WIDE), lambda i: (0, i))]
-        + [pl.BlockSpec((quarter, width), lambda i: (0, 0))] * len(flat),
-        out_specs=[pl.BlockSpec(shape, lambda i: (0, 0))] * 2,
+        out_shape=[jax.ShapeDtypeStruct((channels // 2, lanes), F32)] * 2,
+        in_specs=whole(3),
+        out_specs=whole(2),
         scratch_shapes=[
-            pltpu.VMEM((rank, width), BF16),
-            pltpu.VMEM((rank, width), BF16),
+            pltpu.VMEM((count, width), BF16),
+            pltpu.VMEM((count, width), BF16),
             pltpu.VMEM((channels, lanes), F32),
-            pltpu.VMEM((rank, rank), F32),
         ],
-        compiler_params=pltpu.CompilerParams(vmem_limit_bytes=36 * MIB),
-        cost_estimate=pl.CostEstimate(
-            flops=6 * lanes * channels * block, bytes_accessed=channels * block * 4, transcendentals=0
-        ),
-    )(samples, *flat)
+        compiler_params=pltpu.CompilerParams(vmem_limit_bytes=24 * MIB),
+        cost_estimate=pl.CostEstimate(flops=4 * WEIGHT, bytes_accessed=channels * block * 4, transcendentals=0),
+    )(samples, *sketch)
+
+
+def with_gram(keep, send, sketches, margin):
+    quarter, width = sketches[0][0].shape
+    rank = 4 * quarter
+    rows, lanes = keep.shape
+    tail = rank * rank // lanes
+
+    def body(keep_ref, send_ref, *refs):
+        ins, outs, (sketch_ref, gram_ref) = refs[:4], refs[4:6], refs[6:]
+        for place, ref in zip(quarters(), ins):
+            sketch_ref[rows_at(place, quarter), :] = ref[:, margin:]
+        high, low = split(sketch_ref[...])
+        gram_ref[...] = dot3(high, low, high, low, NT)
+        for ref, out_ref in zip((keep_ref, send_ref), outs):
+            out_ref[:rows, :] = ref[...]
+            for group in range(lanes // rank):
+                out_ref[rows:, group * rank : (group + 1) * rank] = gram_ref[group * tail : (group + 1) * tail, :]
+
+    flat = [half for pair in sketches for half in pair]
+    shapes = [(rows + tail, lanes)] * 2
+    return call(body, shapes, [keep, send, *flat], 16, [(rank, width - margin), (rank, rank)])
 
 
 def fold(keep, came, axis, step, tail=0):
@@ -217,7 +231,7 @@
             if tail:
                 ref[count:, :] = a_ref[2 * count :, :] + b_ref[2 * count :, :]
 
-    return call(body, [(count + tail, keep.shape[1])] * 2, [keep, came], 8)
+    return call(body, [(count + tail, keep.shape[1])] * 2, [keep, came], 8, weight=WEIGHT)
 
 
 def add(a, b, tail=0):
@@ -228,7 +242,7 @@
         for ref in tails:
             ref[...] = a_ref[count:, :] + b_ref[count:, :]
 
-    return call(body, [(count, a.shape[1])] + [(tail, a.shape[1])] * (tail > 0), [a, b], 8)
+    return call(body, [(count, a.shape[1])] + [(tail, a.shape[1])] * (tail > 0), [a, b], 8, weight=WEIGHT)
 
 
 def unfold(mine, came, axis, step):
@@ -238,7 +252,7 @@
         out_ref[rows_at(side(axis, step), count), :] = a_ref[...]
         out_ref[rows_at(1 - side(axis, step), count), :] = b_ref[...]
 
-    return call(body, [(2 * count, mine.shape[1])], [mine, came], 8)[0]
+    return call(body, [(2 * count, mine.shape[1])], [mine, came], 8, weight=WEIGHT)[0]
 
 
 def advanced(at, keep, came, one, tail):
@@ -252,7 +266,7 @@
 
 
 def summed_both(first, second, tail):
-    states, tails = [first, second], (0, tail)
+    states, tails = [first, second], (tail, 0)
     axes = (("x", "z"), ("z", "x"))
     came = [along(axes[i][0], 0, states[i][1]) for i in range(2)]
     for at in range(5):
@@ -320,7 +334,7 @@
     half, quarter = rank // 2, rank // 4
     total = block * SIDE * SIDE
 
-    keep, send = sketch_partial(samples, omega)
+    keep, send, samples = sketch_partial(samples, omega)
     came = lax.ppermute(send, "core", [(0, 1), (1, 0)])
 
     def add_cores(a_ref, b_ref, *outs):
@@ -358,10 +372,11 @@
     sketches = [(mine, lax.ppermute(mine, "core", [(0, 1), (1, 0)]))]
     mine = along("y", 0, mine)
 
-    first = projection_partial(samples, sketches, delays, "x", False)
+    first = projection_partial(samples, sketches[0], delays, "x")
     mine, *first = lax.optimization_barrier((mine, *first))
     sketches.append((mine, lax.ppermute(mine, "core", [(0, 1), (1, 0)])))
-    second = projection_partial(samples, sketches, delays, "z", True)
+    first = with_gram(*first, sketches, margin)
+    second = projection_partial(samples, sketches[1], delays, "z")
     first, second, gram = summed_both(first, second, rank // 2)
     inverse = inverse_factor(gram, rank)
 

time: 141 us -> 132 us (0.936)
  waiting for transfers between devices: 58.2 us -> 47.9 us
  Pallas kernels: 48.8 us -> 42.8 us
  starting transfers between devices: 32.7 us -> 38.6 us
    ppermute x19, waiting for transfers between devices: 52.4 us -> 42.2 us  [along(): return lax.ppermute(value, AXES, pairs)]
    pallas_call x3, Pallas kernels: 39.4 us -> 32.3 us  [the longest x1 16.9 us: sketch_partial(): pl.pallas_call(body, out_shape=[out, out, pltpu.VMEM(samples.shape, F32)]...]
    ppermute x19, starting transfers between devices: 31.4 us -> 37.8 us  [along(): return lax.ppermute(value, AXES, pairs)]
    pallas_call x17 -> x18, Pallas kernels: 5.09 us -> 6.24 us  [call(): pl.pallas_call(body, out_shape=[jax.ShapeDtypeStruct(shape, F32) for shap...]
  transfers between devices with their start and end apart: 22 -> 22, of which waited for: 16 -> 18; matrix products, arithmetic and copies ran while one was open for 0% -> 0% of each run, Pallas kernels for 12% -> 17%
where the time goes in v4:
time: 132 us; the launch traced here: 130 us
  waiting for transfers between devices  47.9 us (36%)
  Pallas kernels  42.8 us (32%)
  starting transfers between devices  38.6 us (29%)
    ppermute x19, waiting for transfers between devices, along(): return lax.ppermute(value, AXES, pairs)  42.2 us
    ppermute x19, starting transfers between devices, along(): return lax.ppermute(value, AXES, pairs)  37.8 us
    pallas_call x1, Pallas kernels, sketch_partial(): pl.pallas_call(body, out_shape=[out, out, pltpu.VMEM(samples.shape, F32)]...  16.9 us
    pallas_call x2, Pallas kernels, projection_partial(): pl.pallas_call(body, out_shape=[jax.ShapeDtypeStruct((channels // 2, lane...  15.4 us
    pallas_call x18, Pallas kernels, call(): pl.pallas_call(body, out_shape=[jax.ShapeDtypeStruct(shape, F32) for shap...  6.24 us
    pallas_call x1, Pallas kernels, inverse_factor(): pl.pallas_call(body, out_shape=jax.ShapeDtypeStruct((rank, rank), F32), i...  4.23 us
    ppermute x1, waiting for transfers between devices, shards(): came = lax.ppermute(send, 'core', [(0, 1), (1, 0)])  3.21 us
  transfers between devices with their start and end apart: 22, of which 18 were waited for; matrix products, arithmetic and copies ran while one was open for 0% of the time, Pallas kernels for 17%

profile of v4, /device:TPU:0, one launch (start us, length us, event | category | flops | bytes accessed | tf_op | source)
XLA Modules:
  0.0 130.1 jit_solution(3710051635584012302)
XLA Ops:
  0.6 16.9 %shard_map.41 = (f32[64,5632]{1,0:T(8,128)S(1)}, f32[64,5632]{1,0:T(8,128)S(1)}, f32[1024,4096]{1,0:T(8,128)S(1)}) custom-call(f32[1024,4096]{1,0:T(8,128)} %s_hbm.1, f32[4,1024,128]{2,1,0:T(8,128)} %o_hbm.1), custom_call_target="tpu_custom_call" | custom-call | flops 12884901888 | bytes 16777216 | tf_op jit(solution)/shard_map/pallas_call | solution.py:127
  17.5 0.1 collective-permute-start
  17.6 3.2 %collective-permute-done.b_ref = f32[64,5632]{1,0:T(8,128)S(1)} collective-permute-done((f32[64,5632]{1,0:T(8,128)S(1)}, f32[64,5632]{1,0:T(8,128)S(1)}, u32[]{:S(2)}, u32[]{:S(2)}) %collective-permute-start) | collective-permute-done | bytes 1441824 | tf_op jit(solution)/shard_map/ppermute | solution.py:338
  20.8 0.1 shard_map.42
  20.9 1.7 %collective-permute-start.1 = (f32[32,3072]{1,0:T(8,128)S(1)}, f32[32,3072]{1,0:T(8,128)S(1)}, u32[]{:S(2)}, u32[]{:S(2)}) collective-permute-start(f32[32,3072]{1,0:T(8,128)S(1)} %get-tuple-element.42), channel_id=1, source_target_pairs={{0,2},{1,7},{2,0},{3,5},{4,6},{5,3},{6,4},{7,1},{8,10},{9,15},{10,... | collective-permute-start | bytes 1179656 | tf_op jit(solution)/shard_map/ppermute | solution.py:65
  22.7 0.4 collective-permute-start.5
  23.0 5.8 %collective-permute-done.1.b_ref = f32[32,3072]{1,0:T(8,128)S(1)} collective-permute-done((f32[32,3072]{1,0:T(8,128)S(1)}, f32[32,3072]{1,0:T(8,128)S(1)}, u32[]{:S(2)}, u32[]{:S(2)}) %collective-permute-start.1) | collective-permute-done | bytes 393248 | tf_op jit(solution)/shard_map/ppermute | solution.py:65
  28.8 3.2 %collective-permute-start.2 = (f32[32,3072]{1,0:T(8,128)S(1)}, f32[32,3072]{1,0:T(8,128)S(1)}, u32[]{:S(2)}, u32[]{:S(2)}) collective-permute-start(f32[32,3072]{1,0:T(8,128)S(1)} %shard_map.43.a_ref), channel_id=1, source_target_pairs={{0,6},{1,3},{2,4},{3,1},{4,2},{5,7},{6,0},{7,5},{8,14},{9,11},{10,... | collective-permute-start | bytes 1179656 | tf_op jit(solution)/shard_map/ppermute | solution.py:65
  32.0 0.9 collective-permute-done.5.b_ref
  33.0 3.1 %collective-permute-start.6 = (f32[32,2560]{1,0:T(8,128)S(1)}, f32[32,2560]{1,0:T(8,128)S(1)}, u32[]{:S(2)}, u32[]{:S(2)}) collective-permute-start(f32[32,2560]{1,0:T(8,128)S(1)} %shard_map.45.middle_ref), channel_id=1, source_target_pairs={{0,6},{1,3},{2,4},{3,1},{4,2},{5,7},{6,0},{7,5},{8,14},{9,11},{10,... | collective-permute-start | bytes 983048 | tf_op jit(solution)/shard_map/ppermute | solution.py:65
  36.1 1.9 %collective-permute-done.2.b_ref = f32[32,3072]{1,0:T(8,128)S(1)} collective-permute-done((f32[32,3072]{1,0:T(8,128)S(1)}, f32[32,3072]{1,0:T(8,128)S(1)}, u32[]{:S(2)}, u32[]{:S(2)}) %collective-permute-start.2) | collective-permute-done | bytes 393248 | tf_op jit(solution)/shard_map/ppermute | solution.py:65
  38.0 1.3 collective-permute-start.4
  39.3 4.6 %collective-permute-start.3 = (f32[32,1536]{1,0:T(8,128)S(1)}, f32[32,1536]{1,0:T(8,128)S(1)}, u32[]{:S(2)}, u32[]{:S(2)}) collective-permute-start(f32[32,1536]{1,0:T(8,128)S(1)} %get-tuple-element.44.right_ref), channel_id=1, source_target_pairs={{0,8},{1,9},{2,10},{3,11},{4,12},{5,13},{6,14},{7,15},{8,16},{9,17... | collective-permute-start | bytes 589832 | tf_op jit(solution)/shard_map/ppermute | solution.py:65
  43.8 0.0 collective-permute-done.6.middle_came_ref
  43.8 1.8 %collective-permute-done.4.right_came_ref = f32[32,1536]{1,0:T(8,128)S(1)} collective-permute-done((f32[32,1536]{1,0:T(8,128)S(1)}, f32[32,1536]{1,0:T(8,128)S(1)}, u32[]{:S(2)}, u32[]{:S(2)}) %collective-permute-start.4) | collective-permute-done | bytes 196640 | tf_op jit(solution)/shard_map/ppermute | solution.py:65
  45.7 1.3 %collective-permute-done.3.left_came_ref = f32[32,1536]{1,0:T(8,128)S(1)} collective-permute-done((f32[32,1536]{1,0:T(8,128)S(1)}, f32[32,1536]{1,0:T(8,128)S(1)}, u32[]{:S(2)}, u32[]{:S(2)}) %collective-permute-start.3) | collective-permute-done | bytes 196640 | tf_op jit(solution)/shard_map/ppermute | solution.py:65
  47.0 0.1 shard_map.46.mine_ref.refs_0_
  47.1 0.1 collective-permute-start.8
  47.2 1.5 %collective-permute-start.7 = (f32[32,5632]{1,0:T(8,128)S(1)}, f32[32,5632]{1,0:T(8,128)S(1)}, u32[]{:S(2)}, u32[]{:S(2)}) collective-permute-start(f32[32,5632]{1,0:T(8,128)S(1)} %shard_map.46.mine_ref.refs_0_), channel_id=1, source_target_pairs={{0,2},{1,7},{2,0},{3,5},{4,6},{5,3},{6,4},{7,1},{8,10},{9,15},{10,... | collective-permute-start | bytes 2162696 | tf_op jit(solution)/shard_map/ppermute | solution.py:65
  48.7 0.7 collective-permute-done.8.other_ref.refs_1_
  49.3 0.0 copy-start
  49.3 7.7 %shard_map.47 = (f32[512,256]{1,0:T(8,128)S(1)}, f32[512,256]{1,0:T(8,128)S(1)}) custom-call(f32[1024,4096]{1,0:T(8,128)S(1)} %get-tuple-element.47.s_ref, f32[32,5632]{1,0:T(8,128)S(1)} %shard_map.46.mine_ref.refs_0_, f32[32,5632]{1,0:T(8,128)S(1)} %collective-permute-done.8.other_ref.refs_1_), custom_call_target="tpu_custom_call" | custom-call | flops 80000000000 | bytes 16777216 | tf_op jit(solution)/shard_map/pallas_call | solution.py:186
  57.1 1.5 %collective-permute-done.7.refs_2_.mine_ref = f32[32,5632]{1,0:T(8,128)S(1)} collective-permute-done((f32[32,5632]{1,0:T(8,128)S(1)}, f32[32,5632]{1,0:T(8,128)S(1)}, u32[]{:S(2)}, u32[]{:S(2)}) %collective-permute-start.7) | collective-permute-done | bytes 720928 | tf_op jit(solution)/shard_map/ppermute | solution.py:65
  58.5 0.6 collective-permute-start.9
  59.1 1.8 %collective-permute-done.9.refs_3_.other_ref = f32[32,5632]{1,0:T(8,128)S(1)} collective-permute-done((f32[32,5632]{1,0:T(8,128)S(1)}, f32[32,5632]{1,0:T(8,128)S(1)}, u32[]{:S(2)}, u32[]{:S(2)}) %collective-permute-start.9) | collective-permute-done | bytes 720928 | tf_op jit(solution)/shard_map/ppermute | solution.py:377
  61.0 0.0 copy-done
  61.0 1.2 shard_map.48
  62.1 8.1 %collective-permute-start.10 = (f32[576,256]{1,0:T(8,128)S(1)}, f32[576,256]{1,0:T(8,128)S(1)}, u32[]{:S(2)}, u32[]{:S(2)}) collective-permute-start(f32[576,256]{1,0:T(8,128)S(1)} %get-tuple-element.54), channel_id=1, source_target_pairs={{0,32},{1,97},{2,34},{3,99},{4,36},{5,101},{6,38},{7,103},{8,40},{... | collective-permute-start | bytes 1769480 | tf_op jit(solution)/shard_map/ppermute | solution.py:65
  70.3 7.7 %shard_map.49 = (f32[512,256]{1,0:T(8,128)S(1)}, f32[512,256]{1,0:T(8,128)S(1)}) custom-call(f32[1024,4096]{1,0:T(8,128)S(1)} %get-tuple-element.47.s_ref, f32[32,5632]{1,0:T(8,128)S(1)} %collective-permute-done.7.refs_2_.mine_ref, f32[32,5632]{1,0:T(8,128)S(1)} %collective-permute-done.9.refs_3_.other_ref), custom_call_target="tpu_custom_call" | custom-call | flops 80000000000 | bytes 16777216 | tf_op jit(solution)/shard_map/pallas_call | solution.py:186
  78.0 0.1 collective-permute-start.12
  78.1 0.0 collective-permute-done.10.b_ref
  78.1 0.1 shard_map.50
  78.2 3.7 %collective-permute-start.11 = (f32[320,256]{1,0:T(8,128)S(1)}, f32[320,256]{1,0:T(8,128)S(1)}, u32[]{:S(2)}, u32[]{:S(2)}) collective-permute-start(f32[320,256]{1,0:T(8,128)S(1)} %get-tuple-element.58), channel_id=1, source_target_pairs={{0,96},{1,33},{2,98},{3,35},{4,100},{5,37},{6,102},{7,39},{8,104},... | collective-permute-start | bytes 983048 | tf_op jit(solution)/shard_map/ppermute | solution.py:65
  81.9 5.4 %collective-permute-done.12.b_ref = f32[512,256]{1,0:T(8,128)S(1)} collective-permute-done((f32[512,256]{1,0:T(8,128)S(1)}, f32[512,256]{1,0:T(8,128)S(1)}, u32[]{:S(2)}, u32[]{:S(2)}) %collective-permute-start.12) | collective-permute-done | bytes 524320 | tf_op jit(solution)/shard_map/ppermute | solution.py:65
  87.3 0.1 shard_map.51
  87.3 0.1 collective-permute-start.14
  87.4 0.0 collective-permute-done.11.b_ref
  87.5 1.2 collective-permute-start.13
  88.7 8.2 %collective-permute-done.14.b_ref = f32[256,256]{1,0:T(8,128)S(1)} collective-permute-done((f32[256,256]{1,0:T(8,128)S(1)}, f32[256,256]{1,0:T(8,128)S(1)}, u32[]{:S(2)}, u32[]{:S(2)}) %collective-permute-start.14) | collective-permute-done | bytes 262176 | tf_op jit(solution)/shard_map/ppermute | solution.py:65
  96.9 0.2 collective-permute-start.16
  97.1 0.3 collective-permute-done.13.b_ref
  97.5 1.1 collective-permute-start.15
  98.6 4.8 %collective-permute-done.16.b_ref = f32[256,256]{1,0:T(8,128)S(1)} collective-permute-done((f32[256,256]{1,0:T(8,128)S(1)}, f32[256,256]{1,0:T(8,128)S(1)}, u32[]{:S(2)}, u32[]{:S(2)}) %collective-permute-start.16) | collective-permute-done | bytes 262176 | tf_op jit(solution)/shard_map/ppermute | solution.py:65
  103.4 3.0 %collective-permute-start.18 = (f32[256,256]{1,0:T(8,128)S(1)}, f32[256,256]{1,0:T(8,128)S(1)}, u32[]{:S(2)}, u32[]{:S(2)}) collective-permute-start(f32[256,256]{1,0:T(8,128)S(1)} %shard_map.55.a_ref), channel_id=1, source_target_pairs={{0,96},{1,33},{2,98},{3,35},{4,100},{5,37},{6,102},{7,39},{8,104},... | collective-permute-start | bytes 786440 | tf_op jit(solution)/shard_map/ppermute | solution.py:65
  106.4 0.0 collective-permute-done.15.b_ref
  106.5 2.8 %collective-permute-start.17 = (f32[256,256]{1,0:T(8,128)S(1)}, f32[256,256]{1,0:T(8,128)S(1)}, u32[]{:S(2)}, u32[]{:S(2)}) collective-permute-start(f32[256,256]{1,0:T(8,128)S(1)} %get-tuple-element.69.a_ref), channel_id=1, source_target_pairs={{0,96},{1,33},{2,98},{3,35},{4,100},{5,37},{6,102},{7,39},{8,104},... | collective-permute-start | bytes 786440 | tf_op jit(solution)/shard_map/ppermute | solution.py:65
  109.3 1.8 %collective-permute-done.18.b_ref = f32[256,256]{1,0:T(8,128)S(1)} collective-permute-done((f32[256,256]{1,0:T(8,128)S(1)}, f32[256,256]{1,0:T(8,128)S(1)}, u32[]{:S(2)}, u32[]{:S(2)}) %collective-permute-start.18) | collective-permute-done | bytes 262176 | tf_op jit(solution)/shard_map/ppermute | solution.py:65
  111.1 1.3 collective-permute-start.20
  112.4 1.7 %collective-permute-done.17.b_ref = f32[256,256]{1,0:T(8,128)S(1)} collective-permute-done((f32[256,256]{1,0:T(8,128)S(1)}, f32[256,256]{1,0:T(8,128)S(1)}, u32[]{:S(2)}, u32[]{:S(2)}) %collective-permute-start.17) | collective-permute-done | bytes 262176 | tf_op jit(solution)/shard_map/ppermute | solution.py:65
  114.2 0.1 shard_map.59.refs_4_
  114.2 0.0 copy-start.1
  114.2 0.4 collective-permute-start.19
  114.6 4.2 %collective-permute-done.20.b_ref = f32[256,256]{1,0:T(8,128)S(1)} collective-permute-done((f32[256,256]{1,0:T(8,128)S(1)}, f32[256,256]{1,0:T(8,128)S(1)}, u32[]{:S(2)}, u32[]{:S(2)}) %collective-permute-start.20) | collective-permute-done | bytes 262176 | tf_op jit(solution)/shard_map/ppermute | solution.py:65
  118.8 0.1 shard_map.60.refs_6_
  118.9 0.1 collective-permute-start.21
  118.9 4.2 %shard_map.57.inverse_ref = f32[128,128]{1,0:T(8,128)S(1)} custom-call(f32[64,256]{1,0:T(8,128)S(1)} %get-tuple-element.68.tail_ref), custom_call_target="tpu_custom_call" | custom-call | tf_op jit(solution)/shard_map/pallas_call | solution.py:318
  123.2 0.3 collective-permute-done.19.refs_5_
  123.5 0.0 copy-done.1
  123.5 2.3 %shard_map.61 = (f32[128,512]{1,0:T(8,128)}, f32[4,1024,128]{2,1,0:T(8,128)S(1)}, f32[128,128]{1,0:T(8,128)S(1)}) custom-call(f32[128,128]{1,0:T(8,128)S(1)} %shard_map.57.inverse_ref, f32[32,5632]{1,0:T(8,128)S(1)} %shard_map.46.mine_ref.refs_0_, f32[32,5632]{1,0:T(8,128)S(1)} %copy-done.1, f32[32,5632]{1,0:T(8,128)S(1)} %collective-permute-done.7.refs_2_.mine_ref, ...), custom_call_target="tpu_custom_call" | custom-call | tf_op jit(solution)/shard_map/pallas_call | solution.py:38
  125.8 2.3 %collective-permute-done.21.came_ref = f32[512,256]{1,0:T(8,128)S(1)} collective-permute-done((f32[512,256]{1,0:T(8,128)S(1)}, f32[512,256]{1,0:T(8,128)S(1)}, u32[]{:S(2)}, u32[]{:S(2)}) %collective-permute-start.21) | collective-permute-done | bytes 524320 | tf_op jit(solution)/shard_map/ppermute | solution.py:65
  128.1 2.0 %shard_map.62 = f32[4,1024,128]{2,1,0:T(8,128)} custom-call(f32[128,128]{1,0:T(8,128)S(1)} %get-tuple-element.74.turned_ref, f32[4,1024,128]{2,1,0:T(8,128)S(1)} %get-tuple-element.75.partial_ref, f32[512,256]{1,0:T(8,128)S(1)} %collective-permute-done.21.came_ref), custom_call_target="tpu_custom_call" | custom-call | tf_op jit(solution)/shard_map/pallas_call | solution.py:38
  (9 shorter events, 0.3 us)
Async XLA Ops:
  17.5 3.3 %collective-permute-start = (f32[64,5632]{1,0:T(8,128)S(1)}, f32[64,5632]{1,0:T(8,128)S(1)}, u32[]{:S(2)}, u32[]{:S(2)}) collective-permute-start(f32[64,5632]{1,0:T(8,128)S(1)} %get-tuple-element.40), channel_id=1, source_target_pairs={{0,1},{1,0},{2,3},{3,2},{4,5},{5,4},{6,7},{7,6},{8,9},{9,8},{10,11... | collective-permute-start | bytes 4325384 | tf_op jit(solution)/shard_map/ppermute | solution.py:338
  20.9 7.9 %collective-permute-start.1 = (f32[32,3072]{1,0:T(8,128)S(1)}, f32[32,3072]{1,0:T(8,128)S(1)}, u32[]{:S(2)}, u32[]{:S(2)}) collective-permute-start(f32[32,3072]{1,0:T(8,128)S(1)} %get-tuple-element.42), channel_id=1, source_target_pairs={{0,2},{1,7},{2,0},{3,5},{4,6},{5,3},{6,4},{7,1},{8,10},{9,15},{10,... | collective-permute-start | bytes 1179656 | tf_op jit(solution)/shard_map/ppermute | solution.py:65
  22.7 10.2 %collective-permute-start.5 = (f32[32,2560]{1,0:T(8,128)S(1)}, f32[32,2560]{1,0:T(8,128)S(1)}, u32[]{:S(2)}, u32[]{:S(2)}) collective-permute-start(f32[32,2560]{1,0:T(8,128)S(1)} %get-tuple-element.46), channel_id=1, source_target_pairs={{0,2},{1,7},{2,0},{3,5},{4,6},{5,3},{6,4},{7,1},{8,10},{9,15},{10,... | collective-permute-start | bytes 983048 | tf_op jit(solution)/shard_map/ppermute | solution.py:65
  28.8 9.1 %collective-permute-start.2 = (f32[32,3072]{1,0:T(8,128)S(1)}, f32[32,3072]{1,0:T(8,128)S(1)}, u32[]{:S(2)}, u32[]{:S(2)}) collective-permute-start(f32[32,3072]{1,0:T(8,128)S(1)} %shard_map.43.a_ref), channel_id=1, source_target_pairs={{0,6},{1,3},{2,4},{3,1},{4,2},{5,7},{6,0},{7,5},{8,14},{9,11},{10,... | collective-permute-start | bytes 1179656 | tf_op jit(solution)/shard_map/ppermute | solution.py:65
  33.0 10.9 %collective-permute-start.6 = (f32[32,2560]{1,0:T(8,128)S(1)}, f32[32,2560]{1,0:T(8,128)S(1)}, u32[]{:S(2)}, u32[]{:S(2)}) collective-permute-start(f32[32,2560]{1,0:T(8,128)S(1)} %shard_map.45.middle_ref), channel_id=1, source_target_pairs={{0,6},{1,3},{2,4},{3,1},{4,2},{5,7},{6,0},{7,5},{8,14},{9,11},{10,... | collective-permute-start | bytes 983048 | tf_op jit(solution)/shard_map/ppermute | solution.py:65
  38.0 7.7 %collective-permute-start.4 = (f32[32,1536]{1,0:T(8,128)S(1)}, f32[32,1536]{1,0:T(8,128)S(1)}, u32[]{:S(2)}, u32[]{:S(2)}) collective-permute-start(f32[32,1536]{1,0:T(8,128)S(1)} %get-tuple-element.43.left_ref), channel_id=1, source_target_pairs={{8,0},{9,1},{10,2},{11,3},{12,4},{13,5},{14,6},{15,7},{16,8},{17,9... | collective-permute-start | bytes 589832 | tf_op jit(solution)/shard_map/ppermute | solution.py:65
  39.3 7.7 %collective-permute-start.3 = (f32[32,1536]{1,0:T(8,128)S(1)}, f32[32,1536]{1,0:T(8,128)S(1)}, u32[]{:S(2)}, u32[]{:S(2)}) collective-permute-start(f32[32,1536]{1,0:T(8,128)S(1)} %get-tuple-element.44.right_ref), channel_id=1, source_target_pairs={{0,8},{1,9},{2,10},{3,11},{4,12},{5,13},{6,14},{7,15},{8,16},{9,17... | collective-permute-start | bytes 589832 | tf_op jit(solution)/shard_map/ppermute | solution.py:65
  47.1 2.3 %collective-permute-start.8 = (f32[32,5632]{1,0:T(8,128)S(1)}, f32[32,5632]{1,0:T(8,128)S(1)}, u32[]{:S(2)}, u32[]{:S(2)}) collective-permute-start(f32[32,5632]{1,0:T(8,128)S(1)} %shard_map.46.mine_ref.refs_0_), channel_id=1, source_target_pairs={{0,1},{1,0},{2,3},{3,2},{4,5},{5,4},{6,7},{7,6},{8,9},{9,8},{10,11... | collective-permute-start | bytes 2162696 | tf_op jit(solution)/shard_map/ppermute | solution.py:372
  47.2 11.4 %collective-permute-start.7 = (f32[32,5632]{1,0:T(8,128)S(1)}, f32[32,5632]{1,0:T(8,128)S(1)}, u32[]{:S(2)}, u32[]{:S(2)}) collective-permute-start(f32[32,5632]{1,0:T(8,128)S(1)} %shard_map.46.mine_ref.refs_0_), channel_id=1, source_target_pairs={{0,2},{1,7},{2,0},{3,5},{4,6},{5,3},{6,4},{7,1},{8,10},{9,15},{10,... | collective-permute-start | bytes 2162696 | tf_op jit(solution)/shard_map/ppermute | solution.py:65
  49.3 11.6 %copy-start = (f32[32,5632]{1,0:T(8,128)}, f32[32,5632]{1,0:T(8,128)S(1)}, u32[]{:S(2)}) copy-start(f32[32,5632]{1,0:T(8,128)S(1)} %collective-permute-done.8.other_ref.refs_1_) | copy-start | bytes 2162692
  58.5 2.4 %collective-permute-start.9 = (f32[32,5632]{1,0:T(8,128)S(1)}, f32[32,5632]{1,0:T(8,128)S(1)}, u32[]{:S(2)}, u32[]{:S(2)}) collective-permute-start(f32[32,5632]{1,0:T(8,128)S(1)} %collective-permute-done.7.refs_2_.mine_ref), channel_id=1, source_target_pairs={{0,1},{1,0},{2,3},{3,2},{4,5},{5,4},{6,7},{7,6},{8,9},{9,8},{10,11... | collective-permute-start | bytes 2162696 | tf_op jit(solution)/shard_map/ppermute | solution.py:377
  62.1 16.0 %collective-permute-start.10 = (f32[576,256]{1,0:T(8,128)S(1)}, f32[576,256]{1,0:T(8,128)S(1)}, u32[]{:S(2)}, u32[]{:S(2)}) collective-permute-start(f32[576,256]{1,0:T(8,128)S(1)} %get-tuple-element.54), channel_id=1, source_target_pairs={{0,32},{1,97},{2,34},{3,99},{4,36},{5,101},{6,38},{7,103},{8,40},{... | collective-permute-start | bytes 1769480 | tf_op jit(solution)/shard_map/ppermute | solution.py:65
  78.0 9.3 %collective-permute-start.12 = (f32[512,256]{1,0:T(8,128)S(1)}, f32[512,256]{1,0:T(8,128)S(1)}, u32[]{:S(2)}, u32[]{:S(2)}) collective-permute-start(f32[512,256]{1,0:T(8,128)S(1)} %get-tuple-element.55), channel_id=1, source_target_pairs={{0,8},{1,25},{2,10},{3,27},{4,12},{5,29},{6,14},{7,31},{8,0},{9,17... | collective-permute-start | bytes 1572872 | tf_op jit(solution)/shard_map/ppermute | solution.py:65
  78.2 9.2 %collective-permute-start.11 = (f32[320,256]{1,0:T(8,128)S(1)}, f32[320,256]{1,0:T(8,128)S(1)}, u32[]{:S(2)}, u32[]{:S(2)}) collective-permute-start(f32[320,256]{1,0:T(8,128)S(1)} %get-tuple-element.58), channel_id=1, source_target_pairs={{0,96},{1,33},{2,98},{3,35},{4,100},{5,37},{6,102},{7,39},{8,104},... | collective-permute-start | bytes 983048 | tf_op jit(solution)/shard_map/ppermute | solution.py:65
  87.3 9.6 %collective-permute-start.14 = (f32[256,256]{1,0:T(8,128)S(1)}, f32[256,256]{1,0:T(8,128)S(1)}, u32[]{:S(2)}, u32[]{:S(2)}) collective-permute-start(f32[256,256]{1,0:T(8,128)S(1)} %get-tuple-element.61), channel_id=1, source_target_pairs={{0,24},{1,9},{2,26},{3,11},{4,28},{5,13},{6,30},{7,15},{8,16},{9,1... | collective-permute-start | bytes 786440 | tf_op jit(solution)/shard_map/ppermute | solution.py:65
  87.5 10.0 %collective-permute-start.13 = (f32[320,256]{1,0:T(8,128)S(1)}, f32[320,256]{1,0:T(8,128)S(1)}, u32[]{:S(2)}, u32[]{:S(2)}) collective-permute-start(f32[320,256]{1,0:T(8,128)S(1)} %shard_map.52.a_ref), channel_id=1, source_target_pairs={{0,8},{1,25},{2,10},{3,27},{4,12},{5,29},{6,14},{7,31},{8,0},{9,17... | collective-permute-start | bytes 983048 | tf_op jit(solution)/shard_map/ppermute | solution.py:65
  96.9 6.5 %collective-permute-start.16 = (f32[256,256]{1,0:T(8,128)S(1)}, f32[256,256]{1,0:T(8,128)S(1)}, u32[]{:S(2)}, u32[]{:S(2)}) collective-permute-start(f32[256,256]{1,0:T(8,128)S(1)} %shard_map.53.a_ref), channel_id=1, source_target_pairs={{0,32},{1,97},{2,34},{3,99},{4,36},{5,101},{6,38},{7,103},{8,40},{... | collective-permute-start | bytes 786440 | tf_op jit(solution)/shard_map/ppermute | solution.py:65
  97.5 9.0 %collective-permute-start.15 = (f32[320,256]{1,0:T(8,128)S(1)}, f32[320,256]{1,0:T(8,128)S(1)}, u32[]{:S(2)}, u32[]{:S(2)}) collective-permute-start(f32[320,256]{1,0:T(8,128)S(1)} %shard_map.54.a_ref), channel_id=1, source_target_pairs={{0,24},{1,9},{2,26},{3,11},{4,28},{5,13},{6,30},{7,15},{8,16},{9,1... | collective-permute-start | bytes 983048 | tf_op jit(solution)/shard_map/ppermute | solution.py:65
  103.4 7.7 %collective-permute-start.18 = (f32[256,256]{1,0:T(8,128)S(1)}, f32[256,256]{1,0:T(8,128)S(1)}, u32[]{:S(2)}, u32[]{:S(2)}) collective-permute-start(f32[256,256]{1,0:T(8,128)S(1)} %shard_map.55.a_ref), channel_id=1, source_target_pairs={{0,96},{1,33},{2,98},{3,35},{4,100},{5,37},{6,102},{7,39},{8,104},... | collective-permute-start | bytes 786440 | tf_op jit(solution)/shard_map/ppermute | solution.py:65
  106.5 7.7 %collective-permute-start.17 = (f32[256,256]{1,0:T(8,128)S(1)}, f32[256,256]{1,0:T(8,128)S(1)}, u32[]{:S(2)}, u32[]{:S(2)}) collective-permute-start(f32[256,256]{1,0:T(8,128)S(1)} %get-tuple-element.69.a_ref), channel_id=1, source_target_pairs={{0,96},{1,33},{2,98},{3,35},{4,100},{5,37},{6,102},{7,39},{8,104},... | collective-permute-start | bytes 786440 | tf_op jit(solution)/shard_map/ppermute | solution.py:65
  111.1 7.7 %collective-permute-start.20 = (f32[256,256]{1,0:T(8,128)S(1)}, f32[256,256]{1,0:T(8,128)S(1)}, u32[]{:S(2)}, u32[]{:S(2)}) collective-permute-start(f32[256,256]{1,0:T(8,128)S(1)} %shard_map.58.a_ref), channel_id=1, source_target_pairs={{0,24},{1,9},{2,26},{3,11},{4,28},{5,13},{6,30},{7,15},{8,16},{9,1... | collective-permute-start | bytes 786440 | tf_op jit(solution)/shard_map/ppermute | solution.py:65
  114.2 9.3 %copy-start.1 = (f32[32,5632]{1,0:T(8,128)S(1)}, f32[32,5632]{1,0:T(8,128)}, u32[]{:S(2)}) copy-start(f32[32,5632]{1,0:T(8,128)} %copy-done) | copy-start | bytes 2162692
  114.2 9.3 %collective-permute-start.19 = (f32[512,256]{1,0:T(8,128)S(1)}, f32[512,256]{1,0:T(8,128)S(1)}, u32[]{:S(2)}, u32[]{:S(2)}) collective-permute-start(f32[512,256]{1,0:T(8,128)S(1)} %shard_map.59.refs_4_), channel_id=1, source_target_pairs={{0,32},{1,97},{2,34},{3,99},{4,36},{5,101},{6,38},{7,103},{8,40},{... | collective-permute-start | bytes 1572872 | tf_op jit(solution)/shard_map/ppermute | solution.py:65
  118.9 9.3 %collective-permute-start.21 = (f32[512,256]{1,0:T(8,128)S(1)}, f32[512,256]{1,0:T(8,128)S(1)}, u32[]{:S(2)}, u32[]{:S(2)}) collective-permute-start(f32[512,256]{1,0:T(8,128)S(1)} %shard_map.60.refs_6_), channel_id=1, source_target_pairs={{0,8},{1,25},{2,10},{3,27},{4,12},{5,29},{6,14},{7,31},{8,0},{9,17... | collective-permute-start | bytes 1572872 | tf_op jit(solution)/shard_map/ppermute | solution.py:65

commit v5 on v4

--- a/solution.py
+++ b/solution.py
@@ -81,67 +81,104 @@
     return pl.ds(pl.multiple_of(which * count, count), count)
 
 
-def sketch_partial(samples, omega):
+def sketch_ends(samples, omega):
     delays, channels, rank = omega.shape
     block = samples.shape[1]
     steps = block // LAG
-    margin = (delays - 1) * LAG
-    half = rank // 2
-
-    def body(s_hbm, o_hbm, keep_ref, send_ref, s_ref, o_ref, high_ref, low_ref, acc_ref, s_sem, o_sem):
-        def fetch(step):
-            at = pl.ds(pl.multiple_of(step * LAG, LAG), LAG)
-            return pltpu.make_async_copy(s_hbm.at[:, at], s_ref.at[:, at], s_sem.at[step])
+    reach = delays - 1
+    margin, half = reach * LAG, rank // 2
+    edge = 2 * reach
+
+    def place(at):
+        inner = steps - edge
+        moved = jnp.where(at < edge, at + inner, at - reach)
+        return jnp.where(at < reach, at, moved)
+
+    def body(s_hbm, o_hbm, keep_ref, send_ref, middle_ref, s_ref, high_ref, low_ref, o_ref, acc_ref, s_sem, o_sem):
+        def fetch(at):
+            columns = pl.ds(pl.multiple_of(place(at) * LAG, LAG), LAG)
+            return pltpu.make_async_copy(s_hbm.at[:, columns], s_ref.at[:, columns], s_sem.at[at])
 
         fetch_omega = pltpu.make_async_copy(o_hbm, o_ref, o_sem)
         fetch_omega.start()
         fetch(0).start()
         acc_ref[...] = jnp.zeros_like(acc_ref)
         fetch_omega.wait()
-        for step in range(1, AHEAD):
-            fetch(step).start()
+        for at in range(1, AHEAD):
+            fetch(at).start()
         for d in range(delays):
             high, low = split(o_ref[d].T)
             high_ref[d * rank : (d + 1) * rank, :] = high
             low_ref[d * rank : (d + 1) * rank, :] = low
 
-        @pl.loop(0, steps)
-        def _(step):
-            fetch(step).wait()
-
-            @pl.when(step + AHEAD < steps)
+        @pl.loop(0, edge)
+        def _(at):
+            fetch(at).wait()
+
+            @pl.when(at + AHEAD < steps)
             def _():
-                fetch(step + AHEAD).start()
-
-            s_high, s_low = split(s_ref[:, pl.ds(pl.multiple_of(step * LAG, LAG), LAG)])
+                fetch(at + AHEAD).start()
+
+            s_high, s_low = split(s_ref[:, pl.ds(pl.multiple_of(place(at) * LAG, LAG), LAG)])
             term = dot3(high_ref[...], low_ref[...], s_high, s_low, NN)
             for d in range(delays):
-                at = pl.ds(pl.multiple_of((step + delays - 1 - d) * LAG, LAG), LAG)
-                acc_ref[:, at] += term[d * rank : (d + 1) * rank, :]
-
+                to = pl.ds(pl.multiple_of((place(at) + reach - d) * LAG, LAG), LAG)
+                acc_ref[:, to] += term[d * rank : (d + 1) * rank, :]
+
+        for at in range(edge, steps):
+            if at >= edge + AHEAD:
+                fetch(at).start()
+            fetch(at).wait()
         core = lax.axis_index("core")
-        keep_ref[...] = acc_ref[rows_at(core, half), :]
-        send_ref[...] = acc_ref[rows_at(1 - core, half), :]
-
-    out = jax.ShapeDtypeStruct((half, margin + block), F32)
+        for which, ref in ((core, keep_ref), (1 - core, send_ref)):
+            ref[:, :margin] = acc_ref[rows_at(which, half), :margin]
+            ref[:, margin:] = acc_ref[rows_at(which, half), block:]
+        middle_ref[...] = acc_ref[:, margin:block]
+
+    ends = jax.ShapeDtypeStruct((half, 2 * margin), F32)
     return pl.pallas_call(
         body,
-        out_shape=[out, out, pltpu.VMEM(samples.shape, F32)],
+        out_shape=[
+            ends,
+            ends,
+            jax.ShapeDtypeStruct((rank, block - margin), F32),
+            pltpu.VMEM(samples.shape, F32),
+            jax.ShapeDtypeStruct((delays * rank, channels), BF16),
+            jax.ShapeDtypeStruct((delays * rank, channels), BF16),
+        ],
         in_specs=[pl.BlockSpec(memory_space=pltpu.HBM)] * 2,
-        out_specs=whole(3),
+        out_specs=whole(6),
         scratch_shapes=[
             pltpu.VMEM(omega.shape, F32),
-            pltpu.VMEM((delays * rank, channels), BF16),
-            pltpu.VMEM((delays * rank, channels), BF16),
             pltpu.VMEM((rank, margin + block), F32),
             pltpu.SemaphoreType.DMA((steps,)),
             pltpu.SemaphoreType.DMA,
         ],
         compiler_params=pltpu.CompilerParams(vmem_limit_bytes=20 * MIB),
-        cost_estimate=pl.CostEstimate(
-            flops=6 * delays * rank * channels * block, bytes_accessed=samples.size * 4, transcendentals=0
-        ),
+        cost_estimate=pl.CostEstimate(flops=4 * WEIGHT, bytes_accessed=samples.size * 4, transcendentals=0),
     )(samples, pltpu.with_memory_space_constraint(omega, pltpu.HBM))
+
+
+def sketch_middle(middle, samples, high, low, delays):
+    rank, inner = middle.shape
+    block = samples.shape[1]
+    reach = delays - 1
+    half = rank // 2
+
+    def body(middle_ref, s_ref, high_ref, low_ref, keep_ref, send_ref, acc_ref):
+        acc_ref[...] = middle_ref[...]
+        for step in range(reach, block // LAG - reach):
+            s_high, s_low = split(s_ref[:, step * LAG : (step + 1) * LAG])
+            term = dot3(high_ref[...], low_ref[...], s_high, s_low, NN)
+            for d in range(delays):
+                acc_ref[:, (step - d) * LAG : (step - d + 1) * LAG] += term[d * rank : (d + 1) * rank, :]
+        core = lax.axis_index("core")
+        for which, ref in ((core, keep_ref), (1 - core, send_ref)):
+            ref[...] = acc_ref[rows_at(which, half), :]
+
+    return call(
+        body, [(half, inner)] * 2, [middle, samples, high, low], 16, [(rank, inner)], weight=2 * WEIGHT
+    )
 
 
 def quarters():
@@ -198,40 +235,40 @@
     )(samples, *sketch)
 
 
-def with_gram(keep, send, sketches, margin):
+def fold_with_gram(keep, came, axis, step, sketches, margin):
     quarter, width = sketches[0][0].shape
     rank = 4 * quarter
-    rows, lanes = keep.shape
+    count, lanes = keep.shape[0] // 2, keep.shape[1]
     tail = rank * rank // lanes
 
-    def body(keep_ref, send_ref, *refs):
+    def body(a_ref, b_ref, *refs):
         ins, outs, (sketch_ref, gram_ref) = refs[:4], refs[4:6], refs[6:]
         for place, ref in zip(quarters(), ins):
             sketch_ref[rows_at(place, quarter), :] = ref[:, margin:]
         high, low = split(sketch_ref[...])
         gram_ref[...] = dot3(high, low, high, low, NT)
-        for ref, out_ref in zip((keep_ref, send_ref), outs):
-            out_ref[:rows, :] = ref[...]
+        which = side(axis, step)
+        for place, ref in zip((which, 1 - which), outs):
+            at = rows_at(place, count)
+            ref[:count, :] = a_ref[at, :] + b_ref[at, :]
             for group in range(lanes // rank):
-                out_ref[rows:, group * rank : (group + 1) * rank] = gram_ref[group * tail : (group + 1) * tail, :]
+                ref[count:, group * rank : (group + 1) * rank] = gram_ref[group * tail : (group + 1) * tail, :]
 
     flat = [half for pair in sketches for half in pair]
-    shapes = [(rows + tail, lanes)] * 2
-    return call(body, shapes, [keep, send, *flat], 16, [(rank, width - margin), (rank, rank)])
-
-
-def fold(keep, came, axis, step, tail=0):
-    count = (keep.shape[0] - tail) // 2
+    scratch = [(rank, width - margin), (rank, rank)]
+    return call(body, [(count + tail, lanes)] * 2, [keep, came, *flat], 16, scratch, weight=WEIGHT)
+
+
+def fold(keep, came, axis, step):
+    count = keep.shape[0] // 2
 
     def body(a_ref, b_ref, keep_ref, send_ref):
         which = side(axis, step)
         for place, ref in ((which, keep_ref), (1 - which, send_ref)):
             at = rows_at(place, count)
-            ref[:count, :] = a_ref[at, :] + b_ref[at, :]
-            if tail:
-                ref[count:, :] = a_ref[2 * count :, :] + b_ref[2 * count :, :]
-
-    return call(body, [(count + tail, keep.shape[1])] * 2, [keep, came], 8, weight=WEIGHT)
+            ref[...] = a_ref[at, :] + b_ref[at, :]
+
+    return call(body, [(count, keep.shape[1])] * 2, [keep, came], 8, weight=WEIGHT)
 
 
 def add(a, b, tail=0):
@@ -256,8 +293,6 @@
 
 
 def advanced(at, keep, came, one, tail):
-    if at == 0:
-        return *fold(keep, came, one, 1, tail), None
     if at == 4:
         value = unfold(keep, came, one, 1)
         return value, value, None
@@ -265,19 +300,25 @@
     return value, value, *(rest or [None])
 
 
-def summed_both(first, second, tail):
-    states, tails = [first, second], (tail, 0)
+def summed_both(first, second, sketches, margin):
+    states = [first, second]
     axes = (("x", "z"), ("z", "x"))
     came = [along(axes[i][0], 0, states[i][1]) for i in range(2)]
     for at in range(5):
         for i in range(2):
             arrived, _ = lax.optimization_barrier((came[i], states[1 - i][1]))
-            *states[i], rest = advanced(at, states[i][0], arrived, axes[i][0], tails[i])
             one, two = axes[i]
+            if at > 0:
+                tail = 0 if i else states[i][0].shape[0] - first[0].shape[0] // 2
+                *states[i], rest = advanced(at, states[i][0], arrived, one, tail)
+                if rest is not None:
+                    gram = add(rest, along(one, 0, rest))[0]
+            elif i == 0:
+                states[i] = fold_with_gram(states[i][0], arrived, one, 1, sketches, margin)
+            else:
+                states[i] = fold(states[i][0], arrived, one, 1)
             came[i] = along(*((one, 1), (two, 0), (two, 1), (one, 1), (one, 0))[at], states[i][1])
-            if rest is not None:
-                last = rest
-    return (states[0][0], came[0]), (states[1][0], came[1]), last
+    return (states[0][0], came[0]), (states[1][0], came[1]), gram
 
 
 def inverse_factor(tail, rank):
@@ -334,19 +375,10 @@
     half, quarter = rank // 2, rank // 4
     total = block * SIDE * SIDE
 
-    keep, send, samples = sketch_partial(samples, omega)
-    came = lax.ppermute(send, "core", [(0, 1), (1, 0)])
-
-    def add_cores(a_ref, b_ref, *outs):
-        which = side("y", 0)
-        for to, place in ((0, which), (1, 1 - which)):
-            at = rows_at(place, quarter)
-            outs[to][:, :margin] = a_ref[at, :margin] + b_ref[at, :margin]
-            outs[to][:, margin:] = a_ref[at, block:] + b_ref[at, block:]
-            outs[2 + to][...] = a_ref[at, margin:block] + b_ref[at, margin:block]
-
-    shapes = [(quarter, 2 * margin)] * 2 + [(quarter, inner)] * 2
-    ends, ends_send, middle, middle_send = call(add_cores, shapes, [keep, came], 12)
+    ends, ends_send, middle, samples, high, low = sketch_ends(samples, omega)
+    middle, middle_send = sketch_middle(middle, samples, high, low, delays)
+    ends, ends_send = fold(ends, lax.ppermute(ends_send, "core", [(0, 1), (1, 0)]), "y", 0)
+    middle, middle_send = fold(middle, lax.ppermute(middle_send, "core", [(0, 1), (1, 0)]), "y", 0)
     ends_came = along("y", 0, ends_send)
     middle_came = along("y", 0, middle_send)
     (ends,) = add(ends, ends_came)
@@ -375,34 +407,45 @@
     first = projection_partial(samples, sketches[0], delays, "x")
     mine, *first = lax.optimization_barrier((mine, *first))
     sketches.append((mine, lax.ppermute(mine, "core", [(0, 1), (1, 0)])))
-    first = with_gram(*first, sketches, margin)
     second = projection_partial(samples, sketches[1], delays, "z")
-    first, second, gram = summed_both(first, second, rank // 2)
+    first, second, gram = summed_both(first, second, sketches, margin)
     inverse = inverse_factor(gram, rank)
 
-    def multiplied(turned_ref, part, places, refs, add_to):
+    def multiplied(turned_ref, part, ref, put):
         pick = [turned_ref[rows_at(q, quarter), :] for q in in_order(quarters()[2 * part : 2 * part + 2])]
         none = [jnp.zeros((half, rank), F32)]
         pick = [split(jnp.concatenate(m, 0)) for m in (pick + none, none + pick)]
-        for place, ref in zip(places, refs):
-            for pair in range(delays // 2):
-                a_high, a_low = split(ref[:, pair * rank : (pair + 1) * rank])
-                for odd in range(2):
-                    add_to(2 * pair + odd, rows_at(place, channels // 2), dot3(a_high, a_low, *pick[odd], NN))
+        for pair in range(delays // 2):
+            a_high, a_low = split(ref[:, pair * rank : (pair + 1) * rank])
+            for odd in range(2):
+                put(2 * pair + odd, dot3(a_high, a_low, *pick[odd], NN))
 
     def finish_first(inverse_ref, *refs):
-        rows, ins, (basis_ref, out_ref, turned_ref, sketch_ref) = refs[:4], refs[4:7], refs[7:]
+        rows, ins, outs, (mine_ref, sketch_ref, sem, both_ref) = refs[:4], refs[4:7], refs[7:11], refs[11:]
+        basis_ref, out_ref, partial_ref, turned_ref = outs
         turned_ref[...] = inverse_ref[...].T
-
-        def put(d, at, value):
-            out_ref[d, at, :] = value
-
-        def put_more(d, at, value):
-            out_ref[d, at, :] += value
-
-        which = side("x", 0)
-        multiplied(turned_ref, 0, (which, 1 - which), ins[:2], put)
-        multiplied(turned_ref, 1, (side("z", 0),), ins[2:], put_more)
+        which = side("z", 0)
+        here = side("x", 0)
+
+        def put_first(place):
+            def put(d, value):
+                both_ref[d, rows_at(place, channels // 2), :] = value
+
+            return put
+
+        multiplied(turned_ref, 0, ins[0], put_first(here))
+        multiplied(turned_ref, 0, ins[1], put_first(1 - here))
+
+        def copy(d):
+            return pltpu.make_async_copy(mine_ref.at[d], out_ref.at[d, rows_at(which, channels // 2), :], sem.at[d])
+
+        def put_second(d, value):
+            mine_ref[d] = both_ref[d, rows_at(which, channels // 2), :] + value
+            copy(d).start()
+
+        multiplied(turned_ref, 1, ins[2], put_second)
+        for d in range(delays):
+            partial_ref[d] = both_ref[d, rows_at(1 - which, channels // 2), :]
         core, y = lax.axis_index("core"), lax.axis_index("y")
         columns = block // 8
         at = pl.ds(pl.multiple_of(margin + (y * 2 + core) * columns, columns), columns)
@@ -411,27 +454,48 @@
         high, low = split(inverse_ref[...])
         s_high, s_low = split(sketch_ref[...])
         basis_ref[...] = math.sqrt(total) * dot3(high, low, s_high, s_low, NN)
-
-    shape = (delays, channels, rank)
-    basis, partial, turned = call(
+        for d in range(delays):
+            copy(d).wait()
+
+    shape, part_shape = (delays, channels, rank), (delays, channels // 2, rank)
+    outs = [jax.ShapeDtypeStruct(s, F32) for s in ((rank, block // 8), shape, part_shape, (rank, rank))]
+    basis, projection, partial, turned = pl.pallas_call(
         finish_first,
-        [(rank, block // 8), shape, (rank, rank)],
-        [inverse, *sketches[0], *sketches[1], *first, second[0]],
-        24,
-        [(rank, block // 8)],
-    )
-
-    def finish_second(turned_ref, partial_ref, came_ref, out_ref):
-        def put(d, at, value):
-            out_ref[d, at, :] = partial_ref[d, at, :] + value
-
-        place = 1 - side("z", 0)
-        multiplied(turned_ref, 1, (place,), (came_ref,), put)
-        at = rows_at(1 - place, channels // 2)
+        out_shape=outs,
+        in_specs=whole(8),
+        out_specs=whole(1) + [pl.BlockSpec(memory_space=pltpu.HBM)] + whole(2),
+        scratch_shapes=[
+            pltpu.VMEM(part_shape, F32),
+            pltpu.VMEM((rank, block // 8), F32),
+            pltpu.SemaphoreType.DMA((delays,)),
+            pltpu.VMEM(shape, F32),
+        ],
+        compiler_params=pltpu.CompilerParams(vmem_limit_bytes=24 * MIB),
+    )(inverse, *sketches[0], *sketches[1], *first, second[0])
+
+    def finish_second(turned_ref, partial_ref, came_ref, _, out_ref, mine_ref, sem):
+        which = 1 - side("z", 0)
+
+        def copy(d):
+            return pltpu.make_async_copy(mine_ref.at[d], out_ref.at[d, rows_at(which, channels // 2), :], sem.at[d])
+
+        def put(d, value):
+            mine_ref[d] = partial_ref[d] + value
+            copy(d).start()
+
+        multiplied(turned_ref, 1, came_ref, put)
         for d in range(delays):
-            out_ref[d, at, :] = partial_ref[d, at, :]
-
-    (projection,) = call(finish_second, [shape], [turned, partial, second[1]], 24)
+            copy(d).wait()
+
+    projection = pl.pallas_call(
+        finish_second,
+        out_shape=outs[1],
+        in_specs=whole(3) + [pl.BlockSpec(memory_space=pltpu.HBM)],
+        out_specs=pl.BlockSpec(memory_space=pltpu.HBM),
+        scratch_shapes=[pltpu.VMEM(part_shape, F32), pltpu.SemaphoreType.DMA((delays,))],
+        input_output_aliases={3: 0},
+        compiler_params=pltpu.CompilerParams(vmem_limit_bytes=16 * MIB),
+    )(turned, partial, second[1], projection)
     return basis, projection
 
 

time: 132 us -> 128 us (0.970)
  waiting for transfers between devices: 47.9 us -> 40.4 us
  starting transfers between devices: 38.6 us -> 42.6 us
    ppermute x19 -> x20, starting transfers between devices: 37.8 us -> 41.2 us  [along(): return lax.ppermute(value, AXES, pairs)]
    ppermute x1 -> x2, waiting for transfers between devices: 3.21 us -> 0.01 us  [the longest x1 0.01 us: shards(): lax.ppermute(ends_send, 'core', [(0, 1), (1, 0)])]
    ppermute x19 -> x20, waiting for transfers between devices: 42.2 us -> 39.8 us  [along(): return lax.ppermute(value, AXES, pairs)]
    ppermute x1, waiting for transfers between devices: 1.82 us -> 0.01 us  [shards(): sketches.append((mine, lax.ppermute(mine, 'core', [(0, 1), (1, 0)])))]
    pallas_call x1 -> x3, Pallas kernels: 16.9 us -> 17.7 us  [the longest x1 13.3 us: sketch_ends(): pl.pallas_call(body, out_shape=[ends, ends, jax.ShapeDtypeStruct((rank, b...]
  transfers between devices with their start and end apart: 22 -> 24, of which waited for: 18 -> 17; matrix products, arithmetic and copies ran while one was open for 0% -> 0% of each run, Pallas kernels for 17% -> 22%
where the time goes in v5:
time: 128 us; the launch traced here: 127 us
  Pallas kernels  42.8 us (33%)
  starting transfers between devices  42.6 us (33%)
  waiting for transfers between devices  40.4 us (32%)
    ppermute x20, starting transfers between devices, along(): return lax.ppermute(value, AXES, pairs)  41.2 us
    ppermute x20, waiting for transfers between devices, along(): return lax.ppermute(value, AXES, pairs)  39.8 us
    pallas_call x2, Pallas kernels, projection_partial(): pl.pallas_call(body, out_shape=[jax.ShapeDtypeStruct((channels // 2, lane...  15.4 us
    pallas_call x1, Pallas kernels, sketch_ends(): pl.pallas_call(body, out_shape=[ends, ends, jax.ShapeDtypeStruct((rank, b...  13.3 us
    pallas_call x18, Pallas kernels, call(): pl.pallas_call(body, out_shape=[jax.ShapeDtypeStruct(shape, F32) for shap...  5.43 us
    pallas_call x1, Pallas kernels, inverse_factor(): pl.pallas_call(body, out_shape=jax.ShapeDtypeStruct((rank, rank), F32), i...  4.23 us
    pallas_call x1, Pallas kernels, shards(): pl.pallas_call(finish_first, out_shape=outs, in_specs=whole(8), out_specs...  3.02 us
  transfers between devices with their start and end apart: 24, of which 17 were waited for; matrix products, arithmetic and copies ran while one was open for 0% of the time, Pallas kernels for 22%

profile of v5, /device:TPU:0, one launch (start us, length us, event | category | flops | bytes accessed | tf_op | source)
XLA Modules:
  0.0 126.8 jit_solution(13437674250366804669)
XLA Ops:
  0.6 13.3 %shard_map.41 = (f32[64,3072]{1,0:T(8,128)S(1)}, f32[64,3072]{1,0:T(8,128)S(1)}, f32[128,2560]{1,0:T(8,128)S(1)}, f32[1024,4096]{1,0:T(8,128)S(1)}, bf16[512,102...) custom-call(f32[1024,4096]{1,0:T(8,128)} %s_hbm.1, f32[4,1024,128]{2,1,0:T(8,128)} %o_hbm.1), custom_call_target="tpu_custom_call" | custom-call | flops 80000000000 | bytes 16777216 | tf_op jit(solution)/shard_map/pallas_call | solution.py:139
  13.9 0.1 collective-permute-start
  14.0 3.5 %shard_map.45 = (f32[64,2560]{1,0:T(8,128)S(1)}, f32[64,2560]{1,0:T(8,128)S(1)}) custom-call(f32[128,2560]{1,0:T(8,128)S(1)} %get-tuple-element.49.middle_ref, f32[1024,4096]{1,0:T(8,128)S(1)} %get-tuple-element.50.s_ref, bf16[512,1024]{1,0:T(8,128)(2,1)S(1)} %get-tuple-element.51.high_ref, bf16[512,1024]{1,0:T(8,128)(2,1)S(1)} %get-tuple-element.52.low_ref), custom_call_target="tpu_custom_call" | custom-call | flops 40000000000 | tf_op jit(solution)/shard_map/pallas_call | solution.py:38
  17.5 0.6 collective-permute-start.5
  18.1 0.0 collective-permute-done.b_ref
  18.1 0.1 shard_map.42
  18.2 1.7 %collective-permute-start.1 = (f32[32,3072]{1,0:T(8,128)S(1)}, f32[32,3072]{1,0:T(8,128)S(1)}, u32[]{:S(2)}, u32[]{:S(2)}) collective-permute-start(f32[32,3072]{1,0:T(8,128)S(1)} %get-tuple-element.46), channel_id=1, source_target_pairs={{0,2},{1,7},{2,0},{3,5},{4,6},{5,3},{6,4},{7,1},{8,10},{9,15},{10,... | collective-permute-start | bytes 1179656 | tf_op jit(solution)/shard_map/ppermute | solution.py:65
  19.9 0.0 collective-permute-done.5.b_ref
  19.9 0.1 shard_map.46
  20.0 1.6 %collective-permute-start.6 = (f32[32,2560]{1,0:T(8,128)S(1)}, f32[32,2560]{1,0:T(8,128)S(1)}, u32[]{:S(2)}, u32[]{:S(2)}) collective-permute-start(f32[32,2560]{1,0:T(8,128)S(1)} %get-tuple-element.56), channel_id=1, source_target_pairs={{0,2},{1,7},{2,0},{3,5},{4,6},{5,3},{6,4},{7,1},{8,10},{9,15},{10,... | collective-permute-start | bytes 983048 | tf_op jit(solution)/shard_map/ppermute | solution.py:65
  21.6 4.4 %collective-permute-done.1.b_ref = f32[32,3072]{1,0:T(8,128)S(1)} collective-permute-done((f32[32,3072]{1,0:T(8,128)S(1)}, f32[32,3072]{1,0:T(8,128)S(1)}, u32[]{:S(2)}, u32[]{:S(2)}) %collective-permute-start.1) | collective-permute-done | bytes 393248 | tf_op jit(solution)/shard_map/ppermute | solution.py:65
  26.1 3.2 %collective-permute-start.2 = (f32[32,3072]{1,0:T(8,128)S(1)}, f32[32,3072]{1,0:T(8,128)S(1)}, u32[]{:S(2)}, u32[]{:S(2)}) collective-permute-start(f32[32,3072]{1,0:T(8,128)S(1)} %shard_map.43.a_ref), channel_id=1, source_target_pairs={{0,6},{1,3},{2,4},{3,1},{4,2},{5,7},{6,0},{7,5},{8,14},{9,11},{10,... | collective-permute-start | bytes 1179656 | tf_op jit(solution)/shard_map/ppermute | solution.py:65
  29.3 1.0 collective-permute-done.6.b_ref
  30.3 3.1 %collective-permute-start.7 = (f32[32,2560]{1,0:T(8,128)S(1)}, f32[32,2560]{1,0:T(8,128)S(1)}, u32[]{:S(2)}, u32[]{:S(2)}) collective-permute-start(f32[32,2560]{1,0:T(8,128)S(1)} %shard_map.47.middle_ref), channel_id=1, source_target_pairs={{0,6},{1,3},{2,4},{3,1},{4,2},{5,7},{6,0},{7,5},{8,14},{9,11},{10,... | collective-permute-start | bytes 983048 | tf_op jit(solution)/shard_map/ppermute | solution.py:65
  33.4 1.8 %collective-permute-done.2.b_ref = f32[32,3072]{1,0:T(8,128)S(1)} collective-permute-done((f32[32,3072]{1,0:T(8,128)S(1)}, f32[32,3072]{1,0:T(8,128)S(1)}, u32[]{:S(2)}, u32[]{:S(2)}) %collective-permute-start.2) | collective-permute-done | bytes 393248 | tf_op jit(solution)/shard_map/ppermute | solution.py:65
  35.2 1.3 %collective-permute-start.4 = (f32[32,1536]{1,0:T(8,128)S(1)}, f32[32,1536]{1,0:T(8,128)S(1)}, u32[]{:S(2)}, u32[]{:S(2)}) collective-permute-start(f32[32,1536]{1,0:T(8,128)S(1)} %get-tuple-element.47.left_ref), channel_id=1, source_target_pairs={{8,0},{9,1},{10,2},{11,3},{12,4},{13,5},{14,6},{15,7},{16,8},{17,9... | collective-permute-start | bytes 589832 | tf_op jit(solution)/shard_map/ppermute | solution.py:65
  36.5 4.6 %collective-permute-start.3 = (f32[32,1536]{1,0:T(8,128)S(1)}, f32[32,1536]{1,0:T(8,128)S(1)}, u32[]{:S(2)}, u32[]{:S(2)}) collective-permute-start(f32[32,1536]{1,0:T(8,128)S(1)} %get-tuple-element.48.right_ref), channel_id=1, source_target_pairs={{0,8},{1,9},{2,10},{3,11},{4,12},{5,13},{6,14},{7,15},{8,16},{9,17... | collective-permute-start | bytes 589832 | tf_op jit(solution)/shard_map/ppermute | solution.py:65
  41.1 0.0 collective-permute-done.7.middle_came_ref
  41.1 1.8 %collective-permute-done.4.right_came_ref = f32[32,1536]{1,0:T(8,128)S(1)} collective-permute-done((f32[32,1536]{1,0:T(8,128)S(1)}, f32[32,1536]{1,0:T(8,128)S(1)}, u32[]{:S(2)}, u32[]{:S(2)}) %collective-permute-start.4) | collective-permute-done | bytes 196640 | tf_op jit(solution)/shard_map/ppermute | solution.py:65
  42.9 1.3 %collective-permute-done.3.left_came_ref = f32[32,1536]{1,0:T(8,128)S(1)} collective-permute-done((f32[32,1536]{1,0:T(8,128)S(1)}, f32[32,1536]{1,0:T(8,128)S(1)}, u32[]{:S(2)}, u32[]{:S(2)}) %collective-permute-start.3) | collective-permute-done | bytes 196640 | tf_op jit(solution)/shard_map/ppermute | solution.py:65
  44.2 0.1 shard_map.48.mine_ref.refs_0_
  44.3 0.1 collective-permute-start.9
  44.4 1.5 %collective-permute-start.8 = (f32[32,5632]{1,0:T(8,128)S(1)}, f32[32,5632]{1,0:T(8,128)S(1)}, u32[]{:S(2)}, u32[]{:S(2)}) collective-permute-start(f32[32,5632]{1,0:T(8,128)S(1)} %shard_map.48.mine_ref.refs_0_), channel_id=1, source_target_pairs={{0,2},{1,7},{2,0},{3,5},{4,6},{5,3},{6,4},{7,1},{8,10},{9,15},{10,... | collective-permute-start | bytes 2162696 | tf_op jit(solution)/shard_map/ppermute | solution.py:65
  45.9 0.7 collective-permute-done.9.other_ref.refs_1_
  46.6 7.7 %shard_map.49 = (f32[512,256]{1,0:T(8,128)S(1)}, f32[512,256]{1,0:T(8,128)S(1)}) custom-call(f32[1024,4096]{1,0:T(8,128)S(1)} %get-tuple-element.50.s_ref, f32[32,5632]{1,0:T(8,128)S(1)} %shard_map.48.mine_ref.refs_0_, f32[32,5632]{1,0:T(8,128)S(1)} %collective-permute-done.9.other_ref.refs_1_), custom_call_target="tpu_custom_call" | custom-call | flops 80000000000 | bytes 16777216 | tf_op jit(solution)/shard_map/pallas_call | solution.py:223
  54.3 1.5 %collective-permute-done.8.mine_ref.refs_2_ = f32[32,5632]{1,0:T(8,128)S(1)} collective-permute-done((f32[32,5632]{1,0:T(8,128)S(1)}, f32[32,5632]{1,0:T(8,128)S(1)}, u32[]{:S(2)}, u32[]{:S(2)}) %collective-permute-start.8) | collective-permute-done | bytes 720928 | tf_op jit(solution)/shard_map/ppermute | solution.py:65
  55.8 0.6 collective-permute-start.11
  56.4 8.1 %collective-permute-start.10 = (f32[512,256]{1,0:T(8,128)S(1)}, f32[512,256]{1,0:T(8,128)S(1)}, u32[]{:S(2)}, u32[]{:S(2)}) collective-permute-start(f32[512,256]{1,0:T(8,128)S(1)} %get-tuple-element.60), channel_id=1, source_target_pairs={{0,32},{1,97},{2,34},{3,99},{4,36},{5,101},{6,38},{7,103},{8,40},{... | collective-permute-start | bytes 1572872 | tf_op jit(solution)/shard_map/ppermute | solution.py:65
  64.5 0.0 collective-permute-done.11.other_ref.refs_3_
  64.5 7.7 %shard_map.50 = (f32[512,256]{1,0:T(8,128)S(1)}, f32[512,256]{1,0:T(8,128)S(1)}) custom-call(f32[1024,4096]{1,0:T(8,128)S(1)} %get-tuple-element.50.s_ref, f32[32,5632]{1,0:T(8,128)S(1)} %collective-permute-done.8.mine_ref.refs_2_, f32[32,5632]{1,0:T(8,128)S(1)} %collective-permute-done.11.other_ref.refs_3_), custom_call_target="tpu_custom_call" | custom-call | flops 80000000000 | bytes 16777216 | tf_op jit(solution)/shard_map/pallas_call | solution.py:223
  72.2 0.1 collective-permute-start.13
  72.3 0.0 collective-permute-done.10.b_ref
  72.3 1.2 shard_map.51
  73.5 3.4 %collective-permute-start.12 = (f32[320,256]{1,0:T(8,128)S(1)}, f32[320,256]{1,0:T(8,128)S(1)}, u32[]{:S(2)}, u32[]{:S(2)}) collective-permute-start(f32[320,256]{1,0:T(8,128)S(1)} %get-tuple-element.65), channel_id=1, source_target_pairs={{0,96},{1,33},{2,98},{3,35},{4,100},{5,37},{6,102},{7,39},{8,104},... | collective-permute-start | bytes 983048 | tf_op jit(solution)/shard_map/ppermute | solution.py:65
  76.9 4.5 %collective-permute-done.13.b_ref = f32[512,256]{1,0:T(8,128)S(1)} collective-permute-done((f32[512,256]{1,0:T(8,128)S(1)}, f32[512,256]{1,0:T(8,128)S(1)}, u32[]{:S(2)}, u32[]{:S(2)}) %collective-permute-start.13) | collective-permute-done | bytes 524320 | tf_op jit(solution)/shard_map/ppermute | solution.py:65
  81.5 0.1 shard_map.52
  81.5 0.1 collective-permute-start.15
  81.6 0.4 collective-permute-done.12.b_ref
  82.0 2.1 %collective-permute-start.14 = (f32[320,256]{1,0:T(8,128)S(1)}, f32[320,256]{1,0:T(8,128)S(1)}, u32[]{:S(2)}, u32[]{:S(2)}) collective-permute-start(f32[320,256]{1,0:T(8,128)S(1)} %shard_map.53.a_ref), channel_id=1, source_target_pairs={{0,8},{1,25},{2,10},{3,27},{4,12},{5,29},{6,14},{7,31},{8,0},{9,17... | collective-permute-start | bytes 983048 | tf_op jit(solution)/shard_map/ppermute | solution.py:65
  84.1 7.4 %collective-permute-done.15.b_ref = f32[256,256]{1,0:T(8,128)S(1)} collective-permute-done((f32[256,256]{1,0:T(8,128)S(1)}, f32[256,256]{1,0:T(8,128)S(1)}, u32[]{:S(2)}, u32[]{:S(2)}) %collective-permute-start.15) | collective-permute-done | bytes 262176 | tf_op jit(solution)/shard_map/ppermute | solution.py:65
  91.6 2.3 %collective-permute-start.17 = (f32[256,256]{1,0:T(8,128)S(1)}, f32[256,256]{1,0:T(8,128)S(1)}, u32[]{:S(2)}, u32[]{:S(2)}) collective-permute-start(f32[256,256]{1,0:T(8,128)S(1)} %shard_map.54.a_ref), channel_id=1, source_target_pairs={{0,32},{1,97},{2,34},{3,99},{4,36},{5,101},{6,38},{7,103},{8,40},{... | collective-permute-start | bytes 786440 | tf_op jit(solution)/shard_map/ppermute | solution.py:65
  93.8 0.0 collective-permute-done.14.b_ref
  93.9 0.1 collective-permute-start.16
  94.0 4.2 %collective-permute-done.17.b_ref = f32[256,256]{1,0:T(8,128)S(1)} collective-permute-done((f32[256,256]{1,0:T(8,128)S(1)}, f32[256,256]{1,0:T(8,128)S(1)}, u32[]{:S(2)}, u32[]{:S(2)}) %collective-permute-start.17) | collective-permute-done | bytes 262176 | tf_op jit(solution)/shard_map/ppermute | solution.py:65
  98.2 3.7 %collective-permute-start.20 = (f32[256,256]{1,0:T(8,128)S(1)}, f32[256,256]{1,0:T(8,128)S(1)}, u32[]{:S(2)}, u32[]{:S(2)}) collective-permute-start(f32[256,256]{1,0:T(8,128)S(1)} %shard_map.56.a_ref), channel_id=1, source_target_pairs={{0,96},{1,33},{2,98},{3,35},{4,100},{5,37},{6,102},{7,39},{8,104},... | collective-permute-start | bytes 786440 | tf_op jit(solution)/shard_map/ppermute | solution.py:65
  102.0 0.3 collective-permute-done.16.b_ref
  102.3 0.1 collective-permute-start.18
  102.4 3.6 %collective-permute-start.19 = (f32[256,256]{1,0:T(8,128)S(1)}, f32[256,256]{1,0:T(8,128)S(1)}, u32[]{:S(2)}, u32[]{:S(2)}) collective-permute-start(f32[256,256]{1,0:T(8,128)S(1)} %get-tuple-element.76.a_ref), channel_id=1, source_target_pairs={{0,96},{1,33},{2,98},{3,35},{4,100},{5,37},{6,102},{7,39},{8,104},... | collective-permute-start | bytes 786440 | tf_op jit(solution)/shard_map/ppermute | solution.py:65
  106.0 0.6 collective-permute-done.20.b_ref
  106.6 0.5 collective-permute-start.22
  107.1 4.2 %collective-permute-done.19.b_ref = f32[256,256]{1,0:T(8,128)S(1)} collective-permute-done((f32[256,256]{1,0:T(8,128)S(1)}, f32[256,256]{1,0:T(8,128)S(1)}, u32[]{:S(2)}, u32[]{:S(2)}) %collective-permute-start.19) | collective-permute-done | bytes 262176 | tf_op jit(solution)/shard_map/ppermute | solution.py:65
  111.3 0.1 shard_map.61.refs_4_
  111.3 0.1 collective-permute-start.21
  111.4 4.5 %collective-permute-done.22.b_ref = f32[256,256]{1,0:T(8,128)S(1)} collective-permute-done((f32[256,256]{1,0:T(8,128)S(1)}, f32[256,256]{1,0:T(8,128)S(1)}, u32[]{:S(2)}, u32[]{:S(2)}) %collective-permute-start.22) | collective-permute-done | bytes 262176 | tf_op jit(solution)/shard_map/ppermute | solution.py:65
  115.9 0.1 shard_map.62.refs_6_
  116.0 0.1 collective-permute-start.23
  116.1 0.0 collective-permute-done.18.b_ref
  116.1 4.2 %shard_map.59.inverse_ref = f32[128,128]{1,0:T(8,128)S(1)} custom-call(f32[64,256]{1,0:T(8,128)S(1)} %shard_map.58.tail_ref), custom_call_target="tpu_custom_call" | custom-call | tf_op jit(solution)/shard_map/pallas_call | solution.py:359
  120.3 0.3 collective-permute-done.21.refs_5_
  120.6 3.0 %shard_map.63 = (f32[128,512]{1,0:T(8,128)}, f32[4,1024,128]{2,1,0:T(8,128)}, f32[4,512,128]{2,1,0:T(8,128)S(1)}, f32[128,128]{1,0:T(8,128)S(1)}) custom-call(f32[128,128]{1,0:T(8,128)S(1)} %shard_map.59.inverse_ref, f32[32,5632]{1,0:T(8,128)S(1)} %shard_map.48.mine_ref.refs_0_, f32[32,5632]{1,0:T(8,128)S(1)} %collective-permute-done.9.other_ref.refs_1_, ...), custom_call_target="tpu_custom_call" | custom-call | tf_op jit(solution)/shard_map/pallas_call | solution.py:462
  123.6 1.6 %collective-permute-done.23.came_ref = f32[512,256]{1,0:T(8,128)S(1)} collective-permute-done((f32[512,256]{1,0:T(8,128)S(1)}, f32[512,256]{1,0:T(8,128)S(1)}, u32[]{:S(2)}, u32[]{:S(2)}) %collective-permute-start.23) | collective-permute-done | bytes 524320 | tf_op jit(solution)/shard_map/ppermute | solution.py:65
  125.3 1.4 %shard_map.64 = f32[4,1024,128]{2,1,0:T(8,128)} custom-call(f32[128,128]{1,0:T(8,128)S(1)} %get-tuple-element.81.turned_ref, f32[4,512,128]{2,1,0:T(8,128)S(1)} %get-tuple-element.82.partial_ref, f32[512,256]{1,0:T(8,128)S(1)} %collective-permute-done.23.came_ref, f32[4,1024,128]{2,1,0:T(8,128)} %get-tuple-element.83._), custom_call_target="tpu_custom_call", output_to_operand_aliasing={{}: (3, {})} | custom-call | tf_op jit(solution)/shard_map/pallas_call | solution.py:490
  (10 shorter events, 0.3 us)
Async XLA Ops:
  13.9 4.2 %collective-permute-start = (f32[64,3072]{1,0:T(8,128)S(1)}, f32[64,3072]{1,0:T(8,128)S(1)}, u32[]{:S(2)}, u32[]{:S(2)}) collective-permute-start(f32[64,3072]{1,0:T(8,128)S(1)} %get-tuple-element.44), channel_id=1, source_target_pairs={{0,1},{1,0},{2,3},{3,2},{4,5},{5,4},{6,7},{7,6},{8,9},{9,8},{10,11... | collective-permute-start | bytes 2359304 | tf_op jit(solution)/shard_map/ppermute | solution.py:380
  17.5 2.4 %collective-permute-start.5 = (f32[64,2560]{1,0:T(8,128)S(1)}, f32[64,2560]{1,0:T(8,128)S(1)}, u32[]{:S(2)}, u32[]{:S(2)}) collective-permute-start(f32[64,2560]{1,0:T(8,128)S(1)} %get-tuple-element.54), channel_id=1, source_target_pairs={{0,1},{1,0},{2,3},{3,2},{4,5},{5,4},{6,7},{7,6},{8,9},{9,8},{10,11... | collective-permute-start | bytes 1966088 | tf_op jit(solution)/shard_map/ppermute | solution.py:381
  18.2 7.9 %collective-permute-start.1 = (f32[32,3072]{1,0:T(8,128)S(1)}, f32[32,3072]{1,0:T(8,128)S(1)}, u32[]{:S(2)}, u32[]{:S(2)}) collective-permute-start(f32[32,3072]{1,0:T(8,128)S(1)} %get-tuple-element.46), channel_id=1, source_target_pairs={{0,2},{1,7},{2,0},{3,5},{4,6},{5,3},{6,4},{7,1},{8,10},{9,15},{10,... | collective-permute-start | bytes 1179656 | tf_op jit(solution)/shard_map/ppermute | solution.py:65
  20.0 10.3 %collective-permute-start.6 = (f32[32,2560]{1,0:T(8,128)S(1)}, f32[32,2560]{1,0:T(8,128)S(1)}, u32[]{:S(2)}, u32[]{:S(2)}) collective-permute-start(f32[32,2560]{1,0:T(8,128)S(1)} %get-tuple-element.56), channel_id=1, source_target_pairs={{0,2},{1,7},{2,0},{3,5},{4,6},{5,3},{6,4},{7,1},{8,10},{9,15},{10,... | collective-permute-start | bytes 983048 | tf_op jit(solution)/shard_map/ppermute | solution.py:65
  26.1 9.1 %collective-permute-start.2 = (f32[32,3072]{1,0:T(8,128)S(1)}, f32[32,3072]{1,0:T(8,128)S(1)}, u32[]{:S(2)}, u32[]{:S(2)}) collective-permute-start(f32[32,3072]{1,0:T(8,128)S(1)} %shard_map.43.a_ref), channel_id=1, source_target_pairs={{0,6},{1,3},{2,4},{3,1},{4,2},{5,7},{6,0},{7,5},{8,14},{9,11},{10,... | collective-permute-start | bytes 1179656 | tf_op jit(solution)/shard_map/ppermute | solution.py:65
  30.3 10.8 %collective-permute-start.7 = (f32[32,2560]{1,0:T(8,128)S(1)}, f32[32,2560]{1,0:T(8,128)S(1)}, u32[]{:S(2)}, u32[]{:S(2)}) collective-permute-start(f32[32,2560]{1,0:T(8,128)S(1)} %shard_map.47.middle_ref), channel_id=1, source_target_pairs={{0,6},{1,3},{2,4},{3,1},{4,2},{5,7},{6,0},{7,5},{8,14},{9,11},{10,... | collective-permute-start | bytes 983048 | tf_op jit(solution)/shard_map/ppermute | solution.py:65
  35.2 7.7 %collective-permute-start.4 = (f32[32,1536]{1,0:T(8,128)S(1)}, f32[32,1536]{1,0:T(8,128)S(1)}, u32[]{:S(2)}, u32[]{:S(2)}) collective-permute-start(f32[32,1536]{1,0:T(8,128)S(1)} %get-tuple-element.47.left_ref), channel_id=1, source_target_pairs={{8,0},{9,1},{10,2},{11,3},{12,4},{13,5},{14,6},{15,7},{16,8},{17,9... | collective-permute-start | bytes 589832 | tf_op jit(solution)/shard_map/ppermute | solution.py:65
  36.5 7.7 %collective-permute-start.3 = (f32[32,1536]{1,0:T(8,128)S(1)}, f32[32,1536]{1,0:T(8,128)S(1)}, u32[]{:S(2)}, u32[]{:S(2)}) collective-permute-start(f32[32,1536]{1,0:T(8,128)S(1)} %get-tuple-element.48.right_ref), channel_id=1, source_target_pairs={{0,8},{1,9},{2,10},{3,11},{4,12},{5,13},{6,14},{7,15},{8,16},{9,17... | collective-permute-start | bytes 589832 | tf_op jit(solution)/shard_map/ppermute | solution.py:65
  44.3 2.3 %collective-permute-start.9 = (f32[32,5632]{1,0:T(8,128)S(1)}, f32[32,5632]{1,0:T(8,128)S(1)}, u32[]{:S(2)}, u32[]{:S(2)}) collective-permute-start(f32[32,5632]{1,0:T(8,128)S(1)} %shard_map.48.mine_ref.refs_0_), channel_id=1, source_target_pairs={{0,1},{1,0},{2,3},{3,2},{4,5},{5,4},{6,7},{7,6},{8,9},{9,8},{10,11... | collective-permute-start | bytes 2162696 | tf_op jit(solution)/shard_map/ppermute | solution.py:404
  44.4 11.4 %collective-permute-start.8 = (f32[32,5632]{1,0:T(8,128)S(1)}, f32[32,5632]{1,0:T(8,128)S(1)}, u32[]{:S(2)}, u32[]{:S(2)}) collective-permute-start(f32[32,5632]{1,0:T(8,128)S(1)} %shard_map.48.mine_ref.refs_0_), channel_id=1, source_target_pairs={{0,2},{1,7},{2,0},{3,5},{4,6},{5,3},{6,4},{7,1},{8,10},{9,15},{10,... | collective-permute-start | bytes 2162696 | tf_op jit(solution)/shard_map/ppermute | solution.py:65
  55.8 8.7 %collective-permute-start.11 = (f32[32,5632]{1,0:T(8,128)S(1)}, f32[32,5632]{1,0:T(8,128)S(1)}, u32[]{:S(2)}, u32[]{:S(2)}) collective-permute-start(f32[32,5632]{1,0:T(8,128)S(1)} %collective-permute-done.8.mine_ref.refs_2_), channel_id=1, source_target_pairs={{0,1},{1,0},{2,3},{3,2},{4,5},{5,4},{6,7},{7,6},{8,9},{9,8},{10,11... | collective-permute-start | bytes 2162696 | tf_op jit(solution)/shard_map/ppermute | solution.py:409
  56.4 15.9 %collective-permute-start.10 = (f32[512,256]{1,0:T(8,128)S(1)}, f32[512,256]{1,0:T(8,128)S(1)}, u32[]{:S(2)}, u32[]{:S(2)}) collective-permute-start(f32[512,256]{1,0:T(8,128)S(1)} %get-tuple-element.60), channel_id=1, source_target_pairs={{0,32},{1,97},{2,34},{3,99},{4,36},{5,101},{6,38},{7,103},{8,40},{... | collective-permute-start | bytes 1572872 | tf_op jit(solution)/shard_map/ppermute | solution.py:65
  72.2 9.3 %collective-permute-start.13 = (f32[512,256]{1,0:T(8,128)S(1)}, f32[512,256]{1,0:T(8,128)S(1)}, u32[]{:S(2)}, u32[]{:S(2)}) collective-permute-start(f32[512,256]{1,0:T(8,128)S(1)} %get-tuple-element.62), channel_id=1, source_target_pairs={{0,8},{1,25},{2,10},{3,27},{4,12},{5,29},{6,14},{7,31},{8,0},{9,17... | collective-permute-start | bytes 1572872 | tf_op jit(solution)/shard_map/ppermute | solution.py:65
  73.5 8.5 %collective-permute-start.12 = (f32[320,256]{1,0:T(8,128)S(1)}, f32[320,256]{1,0:T(8,128)S(1)}, u32[]{:S(2)}, u32[]{:S(2)}) collective-permute-start(f32[320,256]{1,0:T(8,128)S(1)} %get-tuple-element.65), channel_id=1, source_target_pairs={{0,96},{1,33},{2,98},{3,35},{4,100},{5,37},{6,102},{7,39},{8,104},... | collective-permute-start | bytes 983048 | tf_op jit(solution)/shard_map/ppermute | solution.py:65
  81.5 10.0 %collective-permute-start.15 = (f32[256,256]{1,0:T(8,128)S(1)}, f32[256,256]{1,0:T(8,128)S(1)}, u32[]{:S(2)}, u32[]{:S(2)}) collective-permute-start(f32[256,256]{1,0:T(8,128)S(1)} %get-tuple-element.68), channel_id=1, source_target_pairs={{0,24},{1,9},{2,26},{3,11},{4,28},{5,13},{6,30},{7,15},{8,16},{9,1... | collective-permute-start | bytes 786440 | tf_op jit(solution)/shard_map/ppermute | solution.py:65
  82.0 11.8 %collective-permute-start.14 = (f32[320,256]{1,0:T(8,128)S(1)}, f32[320,256]{1,0:T(8,128)S(1)}, u32[]{:S(2)}, u32[]{:S(2)}) collective-permute-start(f32[320,256]{1,0:T(8,128)S(1)} %shard_map.53.a_ref), channel_id=1, source_target_pairs={{0,8},{1,25},{2,10},{3,27},{4,12},{5,29},{6,14},{7,31},{8,0},{9,17... | collective-permute-start | bytes 983048 | tf_op jit(solution)/shard_map/ppermute | solution.py:65
  91.6 6.6 %collective-permute-start.17 = (f32[256,256]{1,0:T(8,128)S(1)}, f32[256,256]{1,0:T(8,128)S(1)}, u32[]{:S(2)}, u32[]{:S(2)}) collective-permute-start(f32[256,256]{1,0:T(8,128)S(1)} %shard_map.54.a_ref), channel_id=1, source_target_pairs={{0,32},{1,97},{2,34},{3,99},{4,36},{5,101},{6,38},{7,103},{8,40},{... | collective-permute-start | bytes 786440 | tf_op jit(solution)/shard_map/ppermute | solution.py:65
  93.9 8.4 %collective-permute-start.16 = (f32[320,256]{1,0:T(8,128)S(1)}, f32[320,256]{1,0:T(8,128)S(1)}, u32[]{:S(2)}, u32[]{:S(2)}) collective-permute-start(f32[320,256]{1,0:T(8,128)S(1)} %shard_map.55.a_ref), channel_id=1, source_target_pairs={{0,24},{1,9},{2,26},{3,11},{4,28},{5,13},{6,30},{7,15},{8,16},{9,1... | collective-permute-start | bytes 983048 | tf_op jit(solution)/shard_map/ppermute | solution.py:65
  98.2 8.4 %collective-permute-start.20 = (f32[256,256]{1,0:T(8,128)S(1)}, f32[256,256]{1,0:T(8,128)S(1)}, u32[]{:S(2)}, u32[]{:S(2)}) collective-permute-start(f32[256,256]{1,0:T(8,128)S(1)} %shard_map.56.a_ref), channel_id=1, source_target_pairs={{0,96},{1,33},{2,98},{3,35},{4,100},{5,37},{6,102},{7,39},{8,104},... | collective-permute-start | bytes 786440 | tf_op jit(solution)/shard_map/ppermute | solution.py:65
  102.3 13.8 %collective-permute-start.18 = (f32[64,256]{1,0:T(8,128)S(1)}, f32[64,256]{1,0:T(8,128)S(1)}, u32[]{:S(2)}, u32[]{:S(2)}) collective-permute-start(f32[64,256]{1,0:T(8,128)S(1)} %get-tuple-element.75.a_ref), channel_id=1, source_target_pairs={{0,32},{1,97},{2,34},{3,99},{4,36},{5,101},{6,38},{7,103},{8,40},{... | collective-permute-start | bytes 196616 | tf_op jit(solution)/shard_map/ppermute | solution.py:65
  102.4 8.9 %collective-permute-start.19 = (f32[256,256]{1,0:T(8,128)S(1)}, f32[256,256]{1,0:T(8,128)S(1)}, u32[]{:S(2)}, u32[]{:S(2)}) collective-permute-start(f32[256,256]{1,0:T(8,128)S(1)} %get-tuple-element.76.a_ref), channel_id=1, source_target_pairs={{0,96},{1,33},{2,98},{3,35},{4,100},{5,37},{6,102},{7,39},{8,104},... | collective-permute-start | bytes 786440 | tf_op jit(solution)/shard_map/ppermute | solution.py:65
  106.6 9.3 %collective-permute-start.22 = (f32[256,256]{1,0:T(8,128)S(1)}, f32[256,256]{1,0:T(8,128)S(1)}, u32[]{:S(2)}, u32[]{:S(2)}) collective-permute-start(f32[256,256]{1,0:T(8,128)S(1)} %shard_map.60.a_ref), channel_id=1, source_target_pairs={{0,24},{1,9},{2,26},{3,11},{4,28},{5,13},{6,30},{7,15},{8,16},{9,1... | collective-permute-start | bytes 786440 | tf_op jit(solution)/shard_map/ppermute | solution.py:65
  111.3 9.3 %collective-permute-start.21 = (f32[512,256]{1,0:T(8,128)S(1)}, f32[512,256]{1,0:T(8,128)S(1)}, u32[]{:S(2)}, u32[]{:S(2)}) collective-permute-start(f32[512,256]{1,0:T(8,128)S(1)} %shard_map.61.refs_4_), channel_id=1, source_target_pairs={{0,32},{1,97},{2,34},{3,99},{4,36},{5,101},{6,38},{7,103},{8,40},{... | collective-permute-start | bytes 1572872 | tf_op jit(solution)/shard_map/ppermute | solution.py:65
  116.0 9.3 %collective-permute-start.23 = (f32[512,256]{1,0:T(8,128)S(1)}, f32[512,256]{1,0:T(8,128)S(1)}, u32[]{:S(2)}, u32[]{:S(2)}) collective-permute-start(f32[512,256]{1,0:T(8,128)S(1)} %shard_map.62.refs_6_), channel_id=1, source_target_pairs={{0,8},{1,25},{2,10},{3,27},{4,12},{5,29},{6,14},{7,31},{8,0},{9,17... | collective-permute-start | bytes 1572872 | tf_op jit(solution)/shard_map/ppermute | solution.py:65

commit v6 on v5

--- a/solution.py
+++ b/solution.py
@@ -50,19 +50,25 @@
 SIDE = 4
 
 
-def along(axis, step, value, blocks=0):
+def along(axis, step, value):
     pairs = []
     for x in range(SIDE):
         for z in range(SIDE):
             for y in range(SIDE):
                 for core in range(2):
-                    flip = 0 if step is None else (1, 3)[step ^ core]
+                    flip = (1, 3)[step ^ core]
                     there = {"x": x, "z": z, "y": y}
                     there[axis] ^= flip
-                    time = there["x"] * SIDE + there["z"] + blocks
-                    if 0 <= time < SIDE * SIDE:
-                        pairs.append((index(x, z, y, core), index(time // SIDE, time % SIDE, there["y"], core)))
+                    pairs.append((index(x, z, y, core), index(there["x"], there["z"], there["y"], core)))
     return lax.ppermute(value, AXES, pairs)
+
+
+def paired(value, first):
+    count = SIDE * SIDE
+    pairs = []
+    for low in range(first, count - 1, 2):
+        pairs += [(low, low + 1), (low + 1, low)]
+    return lax.ppermute(value, ("x", "z"), pairs)
 
 
 def index(x, z, y, core):
@@ -99,14 +105,18 @@
             columns = pl.ds(pl.multiple_of(place(at) * LAG, LAG), LAG)
             return pltpu.make_async_copy(s_hbm.at[:, columns], s_ref.at[:, columns], s_sem.at[at])
 
-        fetch_omega = pltpu.make_async_copy(o_hbm, o_ref, o_sem)
-        fetch_omega.start()
+        def fetch_omega(d):
+            return pltpu.make_async_copy(o_hbm.at[d], o_ref.at[d], o_sem.at[d])
+
+        for d in range(delays):
+            fetch_omega(d).start()
         fetch(0).start()
         acc_ref[...] = jnp.zeros_like(acc_ref)
-        fetch_omega.wait()
-        for at in range(1, AHEAD):
-            fetch(at).start()
         for d in range(delays):
+            fetch_omega(d).wait()
+            if d == delays - 1:
+                for at in range(1, AHEAD):
+                    fetch(at).start()
             high, low = split(o_ref[d].T)
             high_ref[d * rank : (d + 1) * rank, :] = high
             low_ref[d * rank : (d + 1) * rank, :] = low
@@ -152,7 +162,7 @@
             pltpu.VMEM(omega.shape, F32),
             pltpu.VMEM((rank, margin + block), F32),
             pltpu.SemaphoreType.DMA((steps,)),
-            pltpu.SemaphoreType.DMA,
+            pltpu.SemaphoreType.DMA((delays,)),
         ],
         compiler_params=pltpu.CompilerParams(vmem_limit_bytes=20 * MIB),
         cost_estimate=pl.CostEstimate(flops=4 * WEIGHT, bytes_accessed=samples.size * 4, transcendentals=0),
@@ -386,21 +396,27 @@
     (middle,) = add(middle, middle_came)
     middle_came = along("y", 1, middle)
 
-    def add_ends(a_ref, b_ref, left_ref, right_ref):
+    def even():
+        return lax.rem(lax.axis_index("z"), 2) == 0
+
+    def add_ends(a_ref, b_ref, left_ref, right_ref, one_ref, two_ref):
         left_ref[...] = a_ref[:, :margin] + b_ref[:, :margin]
         right_ref[...] = a_ref[:, margin:] + b_ref[:, margin:]
-
-    left, right = call(add_ends, [(quarter, margin)] * 2, [ends, ends_came], 8)
-    left_came = along("y", None, right, 1)
-    right_came = along("y", None, left, -1)
-
-    def join(left_ref, left_came_ref, right_ref, right_came_ref, middle_ref, middle_came_ref, out_ref):
+        one_ref[...] = jnp.where(even(), right_ref[...], left_ref[...])
+        two_ref[...] = jnp.where(even(), left_ref[...], right_ref[...])
+
+    left, right, one, two = call(add_ends, [(quarter, margin)] * 4, [ends, ends_came], 8)
+    one, two = paired(one, 0), paired(two, 1)
+
+    def join(left_ref, right_ref, one_ref, two_ref, middle_ref, middle_came_ref, out_ref):
         inside = lax.axis_index("x") + lax.axis_index("z") > 0
-        out_ref[:, :margin] = jnp.where(inside, left_ref[...] + left_came_ref[...], 0.0)
+        left_came = jnp.where(even(), two_ref[...], one_ref[...])
+        right_came = jnp.where(even(), one_ref[...], two_ref[...])
+        out_ref[:, :margin] = jnp.where(inside, left_ref[...] + left_came, 0.0)
         out_ref[:, margin:block] = middle_ref[...] + middle_came_ref[...]
-        out_ref[:, block:] = right_ref[...] + right_came_ref[...]
-
-    (mine,) = call(join, [(quarter, width)], [left, left_came, right, right_came, middle, middle_came], 8)
+        out_ref[:, block:] = right_ref[...] + right_came
+
+    (mine,) = call(join, [(quarter, width)], [left, right, one, two, middle, middle_came], 8)
     sketches = [(mine, lax.ppermute(mine, "core", [(0, 1), (1, 0)]))]
     mine = along("y", 0, mine)
 

time: 128 us -> 125 us (0.977); the launches traced: 127 us -> 125 us
  waiting for transfers between devices: 40.4 us -> 38.6 us
    ppermute x20 -> x18, waiting for transfers between devices: 39.8 us -> 35.6 us  [along(): return lax.ppermute(value, AXES, pairs)]
    ppermute x0 -> x2, starting transfers between devices: none -> 2.74 us  [paired(): return lax.ppermute(value, ('x', 'z'), pairs)]
    ppermute x0 -> x2, waiting for transfers between devices: none -> 2.44 us  [paired(): return lax.ppermute(value, ('x', 'z'), pairs)]
    ppermute x20 -> x18, starting transfers between devices: 41.2 us -> 38.9 us  [along(): return lax.ppermute(value, AXES, pairs)]
  transfers between devices with their start and end apart: 24 -> 24, of which waited for: 17 -> 14; matrix products, arithmetic and copies ran while one was open for 0% -> 0% of each run, Pallas kernels for 22% -> 22%
where the time goes in v6:
time: 125 us
  Pallas kernels  42.9 us (34%)
  starting transfers between devices  42.9 us (34%)
  waiting for transfers between devices  38.6 us (31%)
    ppermute x18, starting transfers between devices, along(): return lax.ppermute(value, AXES, pairs)  38.9 us
    ppermute x18, waiting for transfers between devices, along(): return lax.ppermute(value, AXES, pairs)  35.6 us
    pallas_call x2, Pallas kernels, projection_partial(): pl.pallas_call(body, out_shape=[jax.ShapeDtypeStruct((channels // 2, lane...  15.4 us
    pallas_call x1, Pallas kernels, sketch_ends(): pl.pallas_call(body, out_shape=[ends, ends, jax.ShapeDtypeStruct((rank, b...  13.3 us
    pallas_call x18, Pallas kernels, call(): pl.pallas_call(body, out_shape=[jax.ShapeDtypeStruct(shape, F32) for shap...  5.48 us
    pallas_call x1, Pallas kernels, inverse_factor(): pl.pallas_call(body, out_shape=jax.ShapeDtypeStruct((rank, rank), F32), i...  4.23 us
    pallas_call x1, Pallas kernels, shards(): pl.pallas_call(finish_first, out_shape=outs, in_specs=whole(8), out_specs...  3.02 us
    ppermute x2, starting transfers between devices, paired(): return lax.ppermute(value, ('x', 'z'), pairs)  2.74 us
  transfers between devices with their start and end apart: 24, of which 14 were waited for; matrix products, arithmetic and copies ran while one was open for 0% of the time, Pallas kernels for 22%

profile of v6, /device:TPU:0, one launch (start us, length us, event | category | flops | bytes accessed | tf_op | source)
XLA Modules:
  0.0 125.3 jit_solution(2622319895736509328)
XLA Ops:
  0.6 13.3 %shard_map.41 = (f32[64,3072]{1,0:T(8,128)S(1)}, f32[64,3072]{1,0:T(8,128)S(1)}, f32[128,2560]{1,0:T(8,128)S(1)}, f32[1024,4096]{1,0:T(8,128)S(1)}, bf16[512,102...) custom-call(f32[1024,4096]{1,0:T(8,128)} %s_hbm.1, f32[4,1024,128]{2,1,0:T(8,128)} %o_hbm.1), custom_call_target="tpu_custom_call" | custom-call | flops 80000000000 | bytes 16777216 | tf_op jit(solution)/shard_map/pallas_call | solution.py:149
  13.9 0.1 collective-permute-start
  14.0 3.5 %shard_map.45 = (f32[64,2560]{1,0:T(8,128)S(1)}, f32[64,2560]{1,0:T(8,128)S(1)}) custom-call(f32[128,2560]{1,0:T(8,128)S(1)} %get-tuple-element.53.middle_ref, f32[1024,4096]{1,0:T(8,128)S(1)} %get-tuple-element.54.s_ref, bf16[512,1024]{1,0:T(8,128)(2,1)S(1)} %get-tuple-element.55.high_ref, bf16[512,1024]{1,0:T(8,128)(2,1)S(1)} %get-tuple-element.56.low_ref), custom_call_target="tpu_custom_call" | custom-call | flops 40000000000 | tf_op jit(solution)/shard_map/pallas_call | solution.py:38
  17.6 0.6 collective-permute-start.5
  18.1 0.0 collective-permute-done.b_ref
  18.2 0.1 shard_map.42
  18.2 1.7 %collective-permute-start.1 = (f32[32,3072]{1,0:T(8,128)S(1)}, f32[32,3072]{1,0:T(8,128)S(1)}, u32[]{:S(2)}, u32[]{:S(2)}) collective-permute-start(f32[32,3072]{1,0:T(8,128)S(1)} %get-tuple-element.48), channel_id=1, source_target_pairs={{0,2},{1,7},{2,0},{3,5},{4,6},{5,3},{6,4},{7,1},{8,10},{9,15},{10,... | collective-permute-start | bytes 1179656 | tf_op jit(solution)/shard_map/ppermute | solution.py:63
  20.0 0.0 collective-permute-done.5.b_ref
  20.0 0.1 shard_map.46
  20.1 1.6 %collective-permute-start.6 = (f32[32,2560]{1,0:T(8,128)S(1)}, f32[32,2560]{1,0:T(8,128)S(1)}, u32[]{:S(2)}, u32[]{:S(2)}) collective-permute-start(f32[32,2560]{1,0:T(8,128)S(1)} %get-tuple-element.60), channel_id=1, source_target_pairs={{0,2},{1,7},{2,0},{3,5},{4,6},{5,3},{6,4},{7,1},{8,10},{9,15},{10,... | collective-permute-start | bytes 983048 | tf_op jit(solution)/shard_map/ppermute | solution.py:63
  21.7 4.4 %collective-permute-done.1.b_ref = f32[32,3072]{1,0:T(8,128)S(1)} collective-permute-done((f32[32,3072]{1,0:T(8,128)S(1)}, f32[32,3072]{1,0:T(8,128)S(1)}, u32[]{:S(2)}, u32[]{:S(2)}) %collective-permute-start.1) | collective-permute-done | bytes 393248 | tf_op jit(solution)/shard_map/ppermute | solution.py:63
  26.1 3.2 %collective-permute-start.2 = (f32[32,3072]{1,0:T(8,128)S(1)}, f32[32,3072]{1,0:T(8,128)S(1)}, u32[]{:S(2)}, u32[]{:S(2)}) collective-permute-start(f32[32,3072]{1,0:T(8,128)S(1)} %shard_map.43.a_ref), channel_id=1, source_target_pairs={{0,6},{1,3},{2,4},{3,1},{4,2},{5,7},{6,0},{7,5},{8,14},{9,11},{10,... | collective-permute-start | bytes 1179656 | tf_op jit(solution)/shard_map/ppermute | solution.py:63
  29.3 1.0 collective-permute-done.6.b_ref
  30.4 3.1 %collective-permute-start.7 = (f32[32,2560]{1,0:T(8,128)S(1)}, f32[32,2560]{1,0:T(8,128)S(1)}, u32[]{:S(2)}, u32[]{:S(2)}) collective-permute-start(f32[32,2560]{1,0:T(8,128)S(1)} %shard_map.47.middle_ref), channel_id=1, source_target_pairs={{0,6},{1,3},{2,4},{3,1},{4,2},{5,7},{6,0},{7,5},{8,14},{9,11},{10,... | collective-permute-start | bytes 983048 | tf_op jit(solution)/shard_map/ppermute | solution.py:63
  33.4 1.8 %collective-permute-done.2.b_ref = f32[32,3072]{1,0:T(8,128)S(1)} collective-permute-done((f32[32,3072]{1,0:T(8,128)S(1)}, f32[32,3072]{1,0:T(8,128)S(1)}, u32[]{:S(2)}, u32[]{:S(2)}) %collective-permute-start.2) | collective-permute-done | bytes 393248 | tf_op jit(solution)/shard_map/ppermute | solution.py:63
  35.2 0.1 shard_map.44
  35.3 2.1 %collective-permute-start.3 = (f32[32,1536]{1,0:T(8,128)S(1)}, f32[32,1536]{1,0:T(8,128)S(1)}, u32[]{:S(2)}, u32[]{:S(2)}) collective-permute-start(f32[32,1536]{1,0:T(8,128)S(1)} %get-tuple-element.51), channel_id=1, source_target_pairs={{0,8},{8,0},{16,24},{24,16},{32,40},{40,32},{48,56},{56,48},{64,72... | collective-permute-start | bytes 589832 | tf_op jit(solution)/shard_map/ppermute | solution.py:71
  37.4 0.7 collective-permute-start.4
  38.0 0.7 collective-permute-done.7.middle_came_ref
  38.7 2.4 %collective-permute-done.3.one_ref = f32[32,1536]{1,0:T(8,128)S(1)} collective-permute-done((f32[32,1536]{1,0:T(8,128)S(1)}, f32[32,1536]{1,0:T(8,128)S(1)}, u32[]{:S(2)}, u32[]{:S(2)}) %collective-permute-start.3) | collective-permute-done | bytes 196640 | tf_op jit(solution)/shard_map/ppermute | solution.py:71
  41.2 0.0 collective-permute-done.4.two_ref
  41.2 0.1 shard_map.48.mine_ref.refs_0_
  41.3 0.1 collective-permute-start.9
  41.4 1.7 %collective-permute-start.8 = (f32[32,5632]{1,0:T(8,128)S(1)}, f32[32,5632]{1,0:T(8,128)S(1)}, u32[]{:S(2)}, u32[]{:S(2)}) collective-permute-start(f32[32,5632]{1,0:T(8,128)S(1)} %shard_map.48.mine_ref.refs_0_), channel_id=1, source_target_pairs={{0,2},{1,7},{2,0},{3,5},{4,6},{5,3},{6,4},{7,1},{8,10},{9,15},{10,... | collective-permute-start | bytes 2162696 | tf_op jit(solution)/shard_map/ppermute | solution.py:63
  43.0 0.5 collective-permute-done.9.other_ref.refs_1_
  43.5 7.7 %shard_map.49 = (f32[512,256]{1,0:T(8,128)S(1)}, f32[512,256]{1,0:T(8,128)S(1)}) custom-call(f32[1024,4096]{1,0:T(8,128)S(1)} %get-tuple-element.54.s_ref, f32[32,5632]{1,0:T(8,128)S(1)} %shard_map.48.mine_ref.refs_0_, f32[32,5632]{1,0:T(8,128)S(1)} %collective-permute-done.9.other_ref.refs_1_), custom_call_target="tpu_custom_call" | custom-call | flops 80000000000 | bytes 16777216 | tf_op jit(solution)/shard_map/pallas_call | solution.py:233
  51.3 1.5 %collective-permute-done.8.mine_ref.refs_2_ = f32[32,5632]{1,0:T(8,128)S(1)} collective-permute-done((f32[32,5632]{1,0:T(8,128)S(1)}, f32[32,5632]{1,0:T(8,128)S(1)}, u32[]{:S(2)}, u32[]{:S(2)}) %collective-permute-start.8) | collective-permute-done | bytes 720928 | tf_op jit(solution)/shard_map/ppermute | solution.py:63
  52.7 0.5 collective-permute-start.11
  53.3 7.4 %collective-permute-start.10 = (f32[512,256]{1,0:T(8,128)S(1)}, f32[512,256]{1,0:T(8,128)S(1)}, u32[]{:S(2)}, u32[]{:S(2)}) collective-permute-start(f32[512,256]{1,0:T(8,128)S(1)} %get-tuple-element.64), channel_id=1, source_target_pairs={{0,32},{1,97},{2,34},{3,99},{4,36},{5,101},{6,38},{7,103},{8,40},{... | collective-permute-start | bytes 1572872 | tf_op jit(solution)/shard_map/ppermute | solution.py:63
  60.6 0.0 collective-permute-done.11.other_ref.refs_3_
  60.6 7.7 %shard_map.50 = (f32[512,256]{1,0:T(8,128)S(1)}, f32[512,256]{1,0:T(8,128)S(1)}) custom-call(f32[1024,4096]{1,0:T(8,128)S(1)} %get-tuple-element.54.s_ref, f32[32,5632]{1,0:T(8,128)S(1)} %collective-permute-done.8.mine_ref.refs_2_, f32[32,5632]{1,0:T(8,128)S(1)} %collective-permute-done.11.other_ref.refs_3_), custom_call_target="tpu_custom_call" | custom-call | flops 80000000000 | bytes 16777216 | tf_op jit(solution)/shard_map/pallas_call | solution.py:233
  68.4 0.1 collective-permute-start.13
  68.4 0.0 collective-permute-done.10.b_ref
  68.5 1.2 shard_map.51
  69.6 3.2 %collective-permute-start.12 = (f32[320,256]{1,0:T(8,128)S(1)}, f32[320,256]{1,0:T(8,128)S(1)}, u32[]{:S(2)}, u32[]{:S(2)}) collective-permute-start(f32[320,256]{1,0:T(8,128)S(1)} %get-tuple-element.69), channel_id=1, source_target_pairs={{0,96},{1,33},{2,98},{3,35},{4,100},{5,37},{6,102},{7,39},{8,104},... | collective-permute-start | bytes 983048 | tf_op jit(solution)/shard_map/ppermute | solution.py:63
  72.8 4.8 %collective-permute-done.13.b_ref = f32[512,256]{1,0:T(8,128)S(1)} collective-permute-done((f32[512,256]{1,0:T(8,128)S(1)}, f32[512,256]{1,0:T(8,128)S(1)}, u32[]{:S(2)}, u32[]{:S(2)}) %collective-permute-start.13) | collective-permute-done | bytes 524320 | tf_op jit(solution)/shard_map/ppermute | solution.py:63
  77.6 0.1 shard_map.52
  77.7 2.9 %collective-permute-start.15 = (f32[256,256]{1,0:T(8,128)S(1)}, f32[256,256]{1,0:T(8,128)S(1)}, u32[]{:S(2)}, u32[]{:S(2)}) collective-permute-start(f32[256,256]{1,0:T(8,128)S(1)} %get-tuple-element.72), channel_id=1, source_target_pairs={{0,24},{1,9},{2,26},{3,11},{4,28},{5,13},{6,30},{7,15},{8,16},{9,1... | collective-permute-start | bytes 786440 | tf_op jit(solution)/shard_map/ppermute | solution.py:63
  80.6 0.0 collective-permute-done.12.b_ref
  80.6 0.1 collective-permute-start.14
  80.7 7.2 %collective-permute-done.15.b_ref = f32[256,256]{1,0:T(8,128)S(1)} collective-permute-done((f32[256,256]{1,0:T(8,128)S(1)}, f32[256,256]{1,0:T(8,128)S(1)}, u32[]{:S(2)}, u32[]{:S(2)}) %collective-permute-start.15) | collective-permute-done | bytes 262176 | tf_op jit(solution)/shard_map/ppermute | solution.py:63
  87.9 2.0 %collective-permute-start.17 = (f32[256,256]{1,0:T(8,128)S(1)}, f32[256,256]{1,0:T(8,128)S(1)}, u32[]{:S(2)}, u32[]{:S(2)}) collective-permute-start(f32[256,256]{1,0:T(8,128)S(1)} %shard_map.54.a_ref), channel_id=1, source_target_pairs={{0,32},{1,97},{2,34},{3,99},{4,36},{5,101},{6,38},{7,103},{8,40},{... | collective-permute-start | bytes 786440 | tf_op jit(solution)/shard_map/ppermute | solution.py:63
  90.0 0.0 collective-permute-done.14.b_ref
  90.0 2.6 %collective-permute-start.16 = (f32[320,256]{1,0:T(8,128)S(1)}, f32[320,256]{1,0:T(8,128)S(1)}, u32[]{:S(2)}, u32[]{:S(2)}) collective-permute-start(f32[320,256]{1,0:T(8,128)S(1)} %shard_map.55.a_ref), channel_id=1, source_target_pairs={{0,24},{1,9},{2,26},{3,11},{4,28},{5,13},{6,30},{7,15},{8,16},{9,1... | collective-permute-start | bytes 983048 | tf_op jit(solution)/shard_map/ppermute | solution.py:63
  92.6 3.6 %collective-permute-done.17.b_ref = f32[256,256]{1,0:T(8,128)S(1)} collective-permute-done((f32[256,256]{1,0:T(8,128)S(1)}, f32[256,256]{1,0:T(8,128)S(1)}, u32[]{:S(2)}, u32[]{:S(2)}) %collective-permute-start.17) | collective-permute-done | bytes 262176 | tf_op jit(solution)/shard_map/ppermute | solution.py:63
  96.3 2.5 %collective-permute-start.20 = (f32[256,256]{1,0:T(8,128)S(1)}, f32[256,256]{1,0:T(8,128)S(1)}, u32[]{:S(2)}, u32[]{:S(2)}) collective-permute-start(f32[256,256]{1,0:T(8,128)S(1)} %shard_map.56.a_ref), channel_id=1, source_target_pairs={{0,96},{1,33},{2,98},{3,35},{4,100},{5,37},{6,102},{7,39},{8,104},... | collective-permute-start | bytes 786440 | tf_op jit(solution)/shard_map/ppermute | solution.py:63
  98.8 0.0 collective-permute-done.16.b_ref
  98.8 0.7 collective-permute-start.18
  99.5 2.4 %collective-permute-start.19 = (f32[256,256]{1,0:T(8,128)S(1)}, f32[256,256]{1,0:T(8,128)S(1)}, u32[]{:S(2)}, u32[]{:S(2)}) collective-permute-start(f32[256,256]{1,0:T(8,128)S(1)} %get-tuple-element.80.a_ref), channel_id=1, source_target_pairs={{0,96},{1,33},{2,98},{3,35},{4,100},{5,37},{6,102},{7,39},{8,104},... | collective-permute-start | bytes 786440 | tf_op jit(solution)/shard_map/ppermute | solution.py:63
  101.9 2.0 %collective-permute-done.20.b_ref = f32[256,256]{1,0:T(8,128)S(1)} collective-permute-done((f32[256,256]{1,0:T(8,128)S(1)}, f32[256,256]{1,0:T(8,128)S(1)}, u32[]{:S(2)}, u32[]{:S(2)}) %collective-permute-start.20) | collective-permute-done | bytes 262176 | tf_op jit(solution)/shard_map/ppermute | solution.py:63
  104.0 1.3 %collective-permute-start.22 = (f32[256,256]{1,0:T(8,128)S(1)}, f32[256,256]{1,0:T(8,128)S(1)}, u32[]{:S(2)}, u32[]{:S(2)}) collective-permute-start(f32[256,256]{1,0:T(8,128)S(1)} %shard_map.60.a_ref), channel_id=1, source_target_pairs={{0,24},{1,9},{2,26},{3,11},{4,28},{5,13},{6,30},{7,15},{8,16},{9,1... | collective-permute-start | bytes 786440 | tf_op jit(solution)/shard_map/ppermute | solution.py:63
  105.3 2.1 %collective-permute-done.19.b_ref = f32[256,256]{1,0:T(8,128)S(1)} collective-permute-done((f32[256,256]{1,0:T(8,128)S(1)}, f32[256,256]{1,0:T(8,128)S(1)}, u32[]{:S(2)}, u32[]{:S(2)}) %collective-permute-start.19) | collective-permute-done | bytes 262176 | tf_op jit(solution)/shard_map/ppermute | solution.py:63
  107.4 0.1 shard_map.61.refs_4_
  107.4 2.3 %collective-permute-start.21 = (f32[512,256]{1,0:T(8,128)S(1)}, f32[512,256]{1,0:T(8,128)S(1)}, u32[]{:S(2)}, u32[]{:S(2)}) collective-permute-start(f32[512,256]{1,0:T(8,128)S(1)} %shard_map.61.refs_4_), channel_id=1, source_target_pairs={{0,32},{1,97},{2,34},{3,99},{4,36},{5,101},{6,38},{7,103},{8,40},{... | collective-permute-start | bytes 1572872 | tf_op jit(solution)/shard_map/ppermute | solution.py:63
  109.8 4.7 %collective-permute-done.22.b_ref = f32[256,256]{1,0:T(8,128)S(1)} collective-permute-done((f32[256,256]{1,0:T(8,128)S(1)}, f32[256,256]{1,0:T(8,128)S(1)}, u32[]{:S(2)}, u32[]{:S(2)}) %collective-permute-start.22) | collective-permute-done | bytes 262176 | tf_op jit(solution)/shard_map/ppermute | solution.py:63
  114.4 0.1 shard_map.62.refs_6_
  114.5 0.1 collective-permute-start.23
  114.6 0.0 collective-permute-done.18.b_ref
  114.6 4.2 %shard_map.59.inverse_ref = f32[128,128]{1,0:T(8,128)S(1)} custom-call(f32[64,256]{1,0:T(8,128)S(1)} %shard_map.58.tail_ref), custom_call_target="tpu_custom_call" | custom-call | tf_op jit(solution)/shard_map/pallas_call | solution.py:369
  118.9 0.0 collective-permute-done.21.refs_5_
  118.9 3.0 %shard_map.63 = (f32[128,512]{1,0:T(8,128)}, f32[4,1024,128]{2,1,0:T(8,128)}, f32[4,512,128]{2,1,0:T(8,128)S(1)}, f32[128,128]{1,0:T(8,128)S(1)}) custom-call(f32[128,128]{1,0:T(8,128)S(1)} %shard_map.59.inverse_ref, f32[32,5632]{1,0:T(8,128)S(1)} %shard_map.48.mine_ref.refs_0_, f32[32,5632]{1,0:T(8,128)S(1)} %collective-permute-done.9.other_ref.refs_1_, ...), custom_call_target="tpu_custom_call" | custom-call | tf_op jit(solution)/shard_map/pallas_call | solution.py:478
  121.9 1.9 %collective-permute-done.23.came_ref = f32[512,256]{1,0:T(8,128)S(1)} collective-permute-done((f32[512,256]{1,0:T(8,128)S(1)}, f32[512,256]{1,0:T(8,128)S(1)}, u32[]{:S(2)}, u32[]{:S(2)}) %collective-permute-start.23) | collective-permute-done | bytes 524320 | tf_op jit(solution)/shard_map/ppermute | solution.py:63
  123.8 1.4 %shard_map.64 = f32[4,1024,128]{2,1,0:T(8,128)} custom-call(f32[128,128]{1,0:T(8,128)S(1)} %get-tuple-element.85.turned_ref, f32[4,512,128]{2,1,0:T(8,128)S(1)} %get-tuple-element.86.partial_ref, f32[512,256]{1,0:T(8,128)S(1)} %collective-permute-done.23.came_ref, f32[4,1024,128]{2,1,0:T(8,128)} %get-tuple-element.87._), custom_call_target="tpu_custom_call", output_to_operand_aliasing={{}: (3, {})} | custom-call | tf_op jit(solution)/shard_map/pallas_call | solution.py:506
  (9 shorter events, 0.3 us)
Async XLA Ops:
  13.9 4.2 %collective-permute-start = (f32[64,3072]{1,0:T(8,128)S(1)}, f32[64,3072]{1,0:T(8,128)S(1)}, u32[]{:S(2)}, u32[]{:S(2)}) collective-permute-start(f32[64,3072]{1,0:T(8,128)S(1)} %get-tuple-element.46), channel_id=1, source_target_pairs={{0,1},{1,0},{2,3},{3,2},{4,5},{5,4},{6,7},{7,6},{8,9},{9,8},{10,11... | collective-permute-start | bytes 2359304 | tf_op jit(solution)/shard_map/ppermute | solution.py:390
  17.6 2.4 %collective-permute-start.5 = (f32[64,2560]{1,0:T(8,128)S(1)}, f32[64,2560]{1,0:T(8,128)S(1)}, u32[]{:S(2)}, u32[]{:S(2)}) collective-permute-start(f32[64,2560]{1,0:T(8,128)S(1)} %get-tuple-element.58), channel_id=1, source_target_pairs={{0,1},{1,0},{2,3},{3,2},{4,5},{5,4},{6,7},{7,6},{8,9},{9,8},{10,11... | collective-permute-start | bytes 1966088 | tf_op jit(solution)/shard_map/ppermute | solution.py:391
  18.2 7.9 %collective-permute-start.1 = (f32[32,3072]{1,0:T(8,128)S(1)}, f32[32,3072]{1,0:T(8,128)S(1)}, u32[]{:S(2)}, u32[]{:S(2)}) collective-permute-start(f32[32,3072]{1,0:T(8,128)S(1)} %get-tuple-element.48), channel_id=1, source_target_pairs={{0,2},{1,7},{2,0},{3,5},{4,6},{5,3},{6,4},{7,1},{8,10},{9,15},{10,... | collective-permute-start | bytes 1179656 | tf_op jit(solution)/shard_map/ppermute | solution.py:63
  20.1 10.3 %collective-permute-start.6 = (f32[32,2560]{1,0:T(8,128)S(1)}, f32[32,2560]{1,0:T(8,128)S(1)}, u32[]{:S(2)}, u32[]{:S(2)}) collective-permute-start(f32[32,2560]{1,0:T(8,128)S(1)} %get-tuple-element.60), channel_id=1, source_target_pairs={{0,2},{1,7},{2,0},{3,5},{4,6},{5,3},{6,4},{7,1},{8,10},{9,15},{10,... | collective-permute-start | bytes 983048 | tf_op jit(solution)/shard_map/ppermute | solution.py:63
  26.1 9.1 %collective-permute-start.2 = (f32[32,3072]{1,0:T(8,128)S(1)}, f32[32,3072]{1,0:T(8,128)S(1)}, u32[]{:S(2)}, u32[]{:S(2)}) collective-permute-start(f32[32,3072]{1,0:T(8,128)S(1)} %shard_map.43.a_ref), channel_id=1, source_target_pairs={{0,6},{1,3},{2,4},{3,1},{4,2},{5,7},{6,0},{7,5},{8,14},{9,11},{10,... | collective-permute-start | bytes 1179656 | tf_op jit(solution)/shard_map/ppermute | solution.py:63
  30.4 8.4 %collective-permute-start.7 = (f32[32,2560]{1,0:T(8,128)S(1)}, f32[32,2560]{1,0:T(8,128)S(1)}, u32[]{:S(2)}, u32[]{:S(2)}) collective-permute-start(f32[32,2560]{1,0:T(8,128)S(1)} %shard_map.47.middle_ref), channel_id=1, source_target_pairs={{0,6},{1,3},{2,4},{3,1},{4,2},{5,7},{6,0},{7,5},{8,14},{9,11},{10,... | collective-permute-start | bytes 983048 | tf_op jit(solution)/shard_map/ppermute | solution.py:63
  35.3 5.9 %collective-permute-start.3 = (f32[32,1536]{1,0:T(8,128)S(1)}, f32[32,1536]{1,0:T(8,128)S(1)}, u32[]{:S(2)}, u32[]{:S(2)}) collective-permute-start(f32[32,1536]{1,0:T(8,128)S(1)} %get-tuple-element.51), channel_id=1, source_target_pairs={{0,8},{8,0},{16,24},{24,16},{32,40},{40,32},{48,56},{56,48},{64,72... | collective-permute-start | bytes 589832 | tf_op jit(solution)/shard_map/ppermute | solution.py:71
  37.4 3.8 %collective-permute-start.4 = (f32[32,1536]{1,0:T(8,128)S(1)}, f32[32,1536]{1,0:T(8,128)S(1)}, u32[]{:S(2)}, u32[]{:S(2)}) collective-permute-start(f32[32,1536]{1,0:T(8,128)S(1)} %get-tuple-element.52), channel_id=1, source_target_pairs={{8,16},{16,8},{24,32},{32,24},{40,48},{48,40},{56,64},{64,56},{72,... | collective-permute-start | bytes 589832 | tf_op jit(solution)/shard_map/ppermute | solution.py:71
  41.3 2.3 %collective-permute-start.9 = (f32[32,5632]{1,0:T(8,128)S(1)}, f32[32,5632]{1,0:T(8,128)S(1)}, u32[]{:S(2)}, u32[]{:S(2)}) collective-permute-start(f32[32,5632]{1,0:T(8,128)S(1)} %shard_map.48.mine_ref.refs_0_), channel_id=1, source_target_pairs={{0,1},{1,0},{2,3},{3,2},{4,5},{5,4},{6,7},{7,6},{8,9},{9,8},{10,11... | collective-permute-start | bytes 2162696 | tf_op jit(solution)/shard_map/ppermute | solution.py:420
  41.4 11.4 %collective-permute-start.8 = (f32[32,5632]{1,0:T(8,128)S(1)}, f32[32,5632]{1,0:T(8,128)S(1)}, u32[]{:S(2)}, u32[]{:S(2)}) collective-permute-start(f32[32,5632]{1,0:T(8,128)S(1)} %shard_map.48.mine_ref.refs_0_), channel_id=1, source_target_pairs={{0,2},{1,7},{2,0},{3,5},{4,6},{5,3},{6,4},{7,1},{8,10},{9,15},{10,... | collective-permute-start | bytes 2162696 | tf_op jit(solution)/shard_map/ppermute | solution.py:63
  52.7 7.9 %collective-permute-start.11 = (f32[32,5632]{1,0:T(8,128)S(1)}, f32[32,5632]{1,0:T(8,128)S(1)}, u32[]{:S(2)}, u32[]{:S(2)}) collective-permute-start(f32[32,5632]{1,0:T(8,128)S(1)} %collective-permute-done.8.mine_ref.refs_2_), channel_id=1, source_target_pairs={{0,1},{1,0},{2,3},{3,2},{4,5},{5,4},{6,7},{7,6},{8,9},{9,8},{10,11... | collective-permute-start | bytes 2162696 | tf_op jit(solution)/shard_map/ppermute | solution.py:425
  53.3 15.2 %collective-permute-start.10 = (f32[512,256]{1,0:T(8,128)S(1)}, f32[512,256]{1,0:T(8,128)S(1)}, u32[]{:S(2)}, u32[]{:S(2)}) collective-permute-start(f32[512,256]{1,0:T(8,128)S(1)} %get-tuple-element.64), channel_id=1, source_target_pairs={{0,32},{1,97},{2,34},{3,99},{4,36},{5,101},{6,38},{7,103},{8,40},{... | collective-permute-start | bytes 1572872 | tf_op jit(solution)/shard_map/ppermute | solution.py:63
  68.4 9.3 %collective-permute-start.13 = (f32[512,256]{1,0:T(8,128)S(1)}, f32[512,256]{1,0:T(8,128)S(1)}, u32[]{:S(2)}, u32[]{:S(2)}) collective-permute-start(f32[512,256]{1,0:T(8,128)S(1)} %get-tuple-element.66), channel_id=1, source_target_pairs={{0,8},{1,25},{2,10},{3,27},{4,12},{5,29},{6,14},{7,31},{8,0},{9,17... | collective-permute-start | bytes 1572872 | tf_op jit(solution)/shard_map/ppermute | solution.py:63
  69.6 11.0 %collective-permute-start.12 = (f32[320,256]{1,0:T(8,128)S(1)}, f32[320,256]{1,0:T(8,128)S(1)}, u32[]{:S(2)}, u32[]{:S(2)}) collective-permute-start(f32[320,256]{1,0:T(8,128)S(1)} %get-tuple-element.69), channel_id=1, source_target_pairs={{0,96},{1,33},{2,98},{3,35},{4,100},{5,37},{6,102},{7,39},{8,104},... | collective-permute-start | bytes 983048 | tf_op jit(solution)/shard_map/ppermute | solution.py:63
  77.7 10.2 %collective-permute-start.15 = (f32[256,256]{1,0:T(8,128)S(1)}, f32[256,256]{1,0:T(8,128)S(1)}, u32[]{:S(2)}, u32[]{:S(2)}) collective-permute-start(f32[256,256]{1,0:T(8,128)S(1)} %get-tuple-element.72), channel_id=1, source_target_pairs={{0,24},{1,9},{2,26},{3,11},{4,28},{5,13},{6,30},{7,15},{8,16},{9,1... | collective-permute-start | bytes 786440 | tf_op jit(solution)/shard_map/ppermute | solution.py:63
  80.6 9.3 %collective-permute-start.14 = (f32[320,256]{1,0:T(8,128)S(1)}, f32[320,256]{1,0:T(8,128)S(1)}, u32[]{:S(2)}, u32[]{:S(2)}) collective-permute-start(f32[320,256]{1,0:T(8,128)S(1)} %shard_map.53.a_ref), channel_id=1, source_target_pairs={{0,8},{1,25},{2,10},{3,27},{4,12},{5,29},{6,14},{7,31},{8,0},{9,17... | collective-permute-start | bytes 983048 | tf_op jit(solution)/shard_map/ppermute | solution.py:63
  87.9 8.3 %collective-permute-start.17 = (f32[256,256]{1,0:T(8,128)S(1)}, f32[256,256]{1,0:T(8,128)S(1)}, u32[]{:S(2)}, u32[]{:S(2)}) collective-permute-start(f32[256,256]{1,0:T(8,128)S(1)} %shard_map.54.a_ref), channel_id=1, source_target_pairs={{0,32},{1,97},{2,34},{3,99},{4,36},{5,101},{6,38},{7,103},{8,40},{... | collective-permute-start | bytes 786440 | tf_op jit(solution)/shard_map/ppermute | solution.py:63
  90.0 8.7 %collective-permute-start.16 = (f32[320,256]{1,0:T(8,128)S(1)}, f32[320,256]{1,0:T(8,128)S(1)}, u32[]{:S(2)}, u32[]{:S(2)}) collective-permute-start(f32[320,256]{1,0:T(8,128)S(1)} %shard_map.55.a_ref), channel_id=1, source_target_pairs={{0,24},{1,9},{2,26},{3,11},{4,28},{5,13},{6,30},{7,15},{8,16},{9,1... | collective-permute-start | bytes 983048 | tf_op jit(solution)/shard_map/ppermute | solution.py:63
  96.3 7.7 %collective-permute-start.20 = (f32[256,256]{1,0:T(8,128)S(1)}, f32[256,256]{1,0:T(8,128)S(1)}, u32[]{:S(2)}, u32[]{:S(2)}) collective-permute-start(f32[256,256]{1,0:T(8,128)S(1)} %shard_map.56.a_ref), channel_id=1, source_target_pairs={{0,96},{1,33},{2,98},{3,35},{4,100},{5,37},{6,102},{7,39},{8,104},... | collective-permute-start | bytes 786440 | tf_op jit(solution)/shard_map/ppermute | solution.py:63
  98.8 15.8 %collective-permute-start.18 = (f32[64,256]{1,0:T(8,128)S(1)}, f32[64,256]{1,0:T(8,128)S(1)}, u32[]{:S(2)}, u32[]{:S(2)}) collective-permute-start(f32[64,256]{1,0:T(8,128)S(1)} %get-tuple-element.79.a_ref), channel_id=1, source_target_pairs={{0,32},{1,97},{2,34},{3,99},{4,36},{5,101},{6,38},{7,103},{8,40},{... | collective-permute-start | bytes 196616 | tf_op jit(solution)/shard_map/ppermute | solution.py:63
  99.5 7.9 %collective-permute-start.19 = (f32[256,256]{1,0:T(8,128)S(1)}, f32[256,256]{1,0:T(8,128)S(1)}, u32[]{:S(2)}, u32[]{:S(2)}) collective-permute-start(f32[256,256]{1,0:T(8,128)S(1)} %get-tuple-element.80.a_ref), channel_id=1, source_target_pairs={{0,96},{1,33},{2,98},{3,35},{4,100},{5,37},{6,102},{7,39},{8,104},... | collective-permute-start | bytes 786440 | tf_op jit(solution)/shard_map/ppermute | solution.py:63
  104.0 10.5 %collective-permute-start.22 = (f32[256,256]{1,0:T(8,128)S(1)}, f32[256,256]{1,0:T(8,128)S(1)}, u32[]{:S(2)}, u32[]{:S(2)}) collective-permute-start(f32[256,256]{1,0:T(8,128)S(1)} %shard_map.60.a_ref), channel_id=1, source_target_pairs={{0,24},{1,9},{2,26},{3,11},{4,28},{5,13},{6,30},{7,15},{8,16},{9,1... | collective-permute-start | bytes 786440 | tf_op jit(solution)/shard_map/ppermute | solution.py:63
  107.4 11.4 %collective-permute-start.21 = (f32[512,256]{1,0:T(8,128)S(1)}, f32[512,256]{1,0:T(8,128)S(1)}, u32[]{:S(2)}, u32[]{:S(2)}) collective-permute-start(f32[512,256]{1,0:T(8,128)S(1)} %shard_map.61.refs_4_), channel_id=1, source_target_pairs={{0,32},{1,97},{2,34},{3,99},{4,36},{5,101},{6,38},{7,103},{8,40},{... | collective-permute-start | bytes 1572872 | tf_op jit(solution)/shard_map/ppermute | solution.py:63
  114.5 9.3 %collective-permute-start.23 = (f32[512,256]{1,0:T(8,128)S(1)}, f32[512,256]{1,0:T(8,128)S(1)}, u32[]{:S(2)}, u32[]{:S(2)}) collective-permute-start(f32[512,256]{1,0:T(8,128)S(1)} %shard_map.62.refs_6_), channel_id=1, source_target_pairs={{0,8},{1,25},{2,10},{3,27},{4,12},{5,29},{6,14},{7,31},{8,0},{9,17... | collective-permute-start | bytes 1572872 | tf_op jit(solution)/shard_map/ppermute | solution.py:63

commit v7 on v6

--- a/solution.py
+++ b/solution.py
@@ -201,7 +201,7 @@
     return jnp.minimum(*places), jnp.maximum(*places)
 
 
-def projection_partial(samples, sketch, delays, axis):
+def projection_partial(samples, sketch, delays):
     channels, block = samples.shape
     quarter, width = sketch[0].shape
     count = 2 * quarter
@@ -226,7 +226,7 @@
                 lows.append(low_ref[:, at])
             acc_ref[...] += dot3(s_high, s_low, jnp.concatenate(highs, 0), jnp.concatenate(lows, 0), NT)
 
-        which = side(axis, 0)
+        which = side(*ROUTE[0])
         for place, ref in ((which, keep_ref), (1 - which, send_ref)):
             ref[...] = acc_ref[rows_at(place, channels // 2), :]
 
@@ -302,9 +302,12 @@
     return call(body, [(2 * count, mine.shape[1])], [mine, came], 8, weight=WEIGHT)[0]
 
 
-def advanced(at, keep, came, one, tail):
+ROUTE = (("z", 0), ("x", 0), ("x", 1), ("z", 1), ("x", 0), ("z", 0))
+
+
+def advanced(at, keep, came, tail):
     if at == 4:
-        value = unfold(keep, came, one, 1)
+        value = unfold(keep, came, *ROUTE[at])
         return value, value, None
     value, *rest = add(keep, came, tail if at == 3 else 0)
     return value, value, *(rest or [None])
@@ -312,22 +315,20 @@
 
 def summed_both(first, second, sketches, margin):
     states = [first, second]
-    axes = (("x", "z"), ("z", "x"))
-    came = [along(axes[i][0], 0, states[i][1]) for i in range(2)]
+    came = [along(*ROUTE[0], state[1]) for state in states]
     for at in range(5):
         for i in range(2):
             arrived, _ = lax.optimization_barrier((came[i], states[1 - i][1]))
-            one, two = axes[i]
             if at > 0:
                 tail = 0 if i else states[i][0].shape[0] - first[0].shape[0] // 2
-                *states[i], rest = advanced(at, states[i][0], arrived, one, tail)
+                *states[i], rest = advanced(at, states[i][0], arrived, tail)
                 if rest is not None:
-                    gram = add(rest, along(one, 0, rest))[0]
+                    gram = add(rest, along(*ROUTE[0], rest))[0]
             elif i == 0:
-                states[i] = fold_with_gram(states[i][0], arrived, one, 1, sketches, margin)
+                states[i] = fold_with_gram(states[i][0], arrived, *ROUTE[1], sketches, margin)
             else:
-                states[i] = fold(states[i][0], arrived, one, 1)
-            came[i] = along(*((one, 1), (two, 0), (two, 1), (one, 1), (one, 0))[at], states[i][1])
+                states[i] = fold(states[i][0], arrived, *ROUTE[1])
+            came[i] = along(*ROUTE[at + 1], states[i][1])
     return (states[0][0], came[0]), (states[1][0], came[1]), gram
 
 
@@ -420,10 +421,10 @@
     sketches = [(mine, lax.ppermute(mine, "core", [(0, 1), (1, 0)]))]
     mine = along("y", 0, mine)
 
-    first = projection_partial(samples, sketches[0], delays, "x")
+    first = projection_partial(samples, sketches[0], delays)
     mine, *first = lax.optimization_barrier((mine, *first))
     sketches.append((mine, lax.ppermute(mine, "core", [(0, 1), (1, 0)])))
-    second = projection_partial(samples, sketches[1], delays, "z")
+    second = projection_partial(samples, sketches[1], delays)
     first, second, gram = summed_both(first, second, sketches, margin)
     inverse = inverse_factor(gram, rank)
 
@@ -440,8 +441,7 @@
         rows, ins, outs, (mine_ref, sketch_ref, sem, both_ref) = refs[:4], refs[4:7], refs[7:11], refs[11:]
         basis_ref, out_ref, partial_ref, turned_ref = outs
         turned_ref[...] = inverse_ref[...].T
-        which = side("z", 0)
-        here = side("x", 0)
+        which = side(*ROUTE[0])
 
         def put_first(place):
             def put(d, value):
@@ -449,8 +449,8 @@
 
             return put
 
-        multiplied(turned_ref, 0, ins[0], put_first(here))
-        multiplied(turned_ref, 0, ins[1], put_first(1 - here))
+        multiplied(turned_ref, 0, ins[0], put_first(which))
+        multiplied(turned_ref, 0, ins[1], put_first(1 - which))
 
         def copy(d):
             return pltpu.make_async_copy(mine_ref.at[d], out_ref.at[d, rows_at(which, channels // 2), :], sem.at[d])
@@ -490,7 +490,7 @@
     )(inverse, *sketches[0], *sketches[1], *first, second[0])
 
     def finish_second(turned_ref, partial_ref, came_ref, _, out_ref, mine_ref, sem):
-        which = 1 - side("z", 0)
+        which = 1 - side(*ROUTE[0])
 
         def copy(d):
             return pltpu.make_async_copy(mine_ref.at[d], out_ref.at[d, rows_at(which, channels // 2), :], sem.at[d])

time: 125 us -> 122 us (0.976)
  waiting for transfers between devices: 38.6 us -> 34 us
  starting transfers between devices: 42.9 us -> 44.3 us
    ppermute x18, waiting for transfers between devices: 35.6 us -> 31 us  [along(): return lax.ppermute(value, AXES, pairs)]
    ppermute x18, starting transfers between devices: 38.9 us -> 40.3 us  [along(): return lax.ppermute(value, AXES, pairs)]
  transfers between devices with their start and end apart: 24 -> 24, of which waited for: 14 -> 16; matrix products, arithmetic and copies ran while one was open for 0% -> 0% of each run, Pallas kernels for 22% -> 23%
where the time goes in v7:
time: 122 us
  starting transfers between devices  44.3 us (36%)
  Pallas kernels  42.9 us (35%)
  waiting for transfers between devices  34 us (28%)
    ppermute x18, starting transfers between devices, along(): return lax.ppermute(value, AXES, pairs)  40.3 us
    ppermute x18, waiting for transfers between devices, along(): return lax.ppermute(value, AXES, pairs)  31 us
    pallas_call x2, Pallas kernels, projection_partial(): pl.pallas_call(body, out_shape=[jax.ShapeDtypeStruct((channels // 2, lane...  15.4 us
    pallas_call x1, Pallas kernels, sketch_ends(): pl.pallas_call(body, out_shape=[ends, ends, jax.ShapeDtypeStruct((rank, b...  13.3 us
    pallas_call x18, Pallas kernels, call(): pl.pallas_call(body, out_shape=[jax.ShapeDtypeStruct(shape, F32) for shap...  5.48 us
    pallas_call x1, Pallas kernels, inverse_factor(): pl.pallas_call(body, out_shape=jax.ShapeDtypeStruct((rank, rank), F32), i...  4.23 us
    pallas_call x1, Pallas kernels, shards(): pl.pallas_call(finish_first, out_shape=outs, in_specs=whole(8), out_specs...  3.09 us
    ppermute x2, starting transfers between devices, paired(): return lax.ppermute(value, ('x', 'z'), pairs)  2.74 us
  transfers between devices with their start and end apart: 24, of which 16 were waited for; matrix products, arithmetic and copies ran while one was open for 0% of the time, Pallas kernels for 23%

profile of v7, /device:TPU:0, one launch (start us, length us, event | category | flops | bytes accessed | tf_op | source)
XLA Modules:
  0.0 122.2 jit_solution(1823644263497449632)
XLA Ops:
  0.6 13.3 %shard_map.41 = (f32[64,3072]{1,0:T(8,128)S(1)}, f32[64,3072]{1,0:T(8,128)S(1)}, f32[128,2560]{1,0:T(8,128)S(1)}, f32[1024,4096]{1,0:T(8,128)S(1)}, bf16[512,102...) custom-call(f32[1024,4096]{1,0:T(8,128)} %s_hbm.1, f32[4,1024,128]{2,1,0:T(8,128)} %o_hbm.1), custom_call_target="tpu_custom_call" | custom-call | flops 80000000000 | bytes 16777216 | tf_op jit(solution)/shard_map/pallas_call | solution.py:149
  13.9 0.1 collective-permute-start
  14.0 3.5 %shard_map.45 = (f32[64,2560]{1,0:T(8,128)S(1)}, f32[64,2560]{1,0:T(8,128)S(1)}) custom-call(f32[128,2560]{1,0:T(8,128)S(1)} %get-tuple-element.53.middle_ref, f32[1024,4096]{1,0:T(8,128)S(1)} %get-tuple-element.54.s_ref, bf16[512,1024]{1,0:T(8,128)(2,1)S(1)} %get-tuple-element.55.high_ref, bf16[512,1024]{1,0:T(8,128)(2,1)S(1)} %get-tuple-element.56.low_ref), custom_call_target="tpu_custom_call" | custom-call | flops 40000000000 | tf_op jit(solution)/shard_map/pallas_call | solution.py:38
  17.6 0.6 collective-permute-start.5
  18.1 0.0 collective-permute-done.b_ref
  18.2 0.1 shard_map.42
  18.2 1.7 %collective-permute-start.1 = (f32[32,3072]{1,0:T(8,128)S(1)}, f32[32,3072]{1,0:T(8,128)S(1)}, u32[]{:S(2)}, u32[]{:S(2)}) collective-permute-start(f32[32,3072]{1,0:T(8,128)S(1)} %get-tuple-element.48), channel_id=1, source_target_pairs={{0,2},{1,7},{2,0},{3,5},{4,6},{5,3},{6,4},{7,1},{8,10},{9,15},{10,... | collective-permute-start | bytes 1179656 | tf_op jit(solution)/shard_map/ppermute | solution.py:63
  20.0 0.0 collective-permute-done.5.b_ref
  20.0 0.1 shard_map.46
  20.1 1.6 %collective-permute-start.6 = (f32[32,2560]{1,0:T(8,128)S(1)}, f32[32,2560]{1,0:T(8,128)S(1)}, u32[]{:S(2)}, u32[]{:S(2)}) collective-permute-start(f32[32,2560]{1,0:T(8,128)S(1)} %get-tuple-element.60), channel_id=1, source_target_pairs={{0,2},{1,7},{2,0},{3,5},{4,6},{5,3},{6,4},{7,1},{8,10},{9,15},{10,... | collective-permute-start | bytes 983048 | tf_op jit(solution)/shard_map/ppermute | solution.py:63
  21.7 4.4 %collective-permute-done.1.b_ref = f32[32,3072]{1,0:T(8,128)S(1)} collective-permute-done((f32[32,3072]{1,0:T(8,128)S(1)}, f32[32,3072]{1,0:T(8,128)S(1)}, u32[]{:S(2)}, u32[]{:S(2)}) %collective-permute-start.1) | collective-permute-done | bytes 393248 | tf_op jit(solution)/shard_map/ppermute | solution.py:63
  26.1 3.2 %collective-permute-start.2 = (f32[32,3072]{1,0:T(8,128)S(1)}, f32[32,3072]{1,0:T(8,128)S(1)}, u32[]{:S(2)}, u32[]{:S(2)}) collective-permute-start(f32[32,3072]{1,0:T(8,128)S(1)} %shard_map.43.a_ref), channel_id=1, source_target_pairs={{0,6},{1,3},{2,4},{3,1},{4,2},{5,7},{6,0},{7,5},{8,14},{9,11},{10,... | collective-permute-start | bytes 1179656 | tf_op jit(solution)/shard_map/ppermute | solution.py:63
  29.3 1.0 collective-permute-done.6.b_ref
  30.4 3.1 %collective-permute-start.7 = (f32[32,2560]{1,0:T(8,128)S(1)}, f32[32,2560]{1,0:T(8,128)S(1)}, u32[]{:S(2)}, u32[]{:S(2)}) collective-permute-start(f32[32,2560]{1,0:T(8,128)S(1)} %shard_map.47.middle_ref), channel_id=1, source_target_pairs={{0,6},{1,3},{2,4},{3,1},{4,2},{5,7},{6,0},{7,5},{8,14},{9,11},{10,... | collective-permute-start | bytes 983048 | tf_op jit(solution)/shard_map/ppermute | solution.py:63
  33.4 1.8 %collective-permute-done.2.b_ref = f32[32,3072]{1,0:T(8,128)S(1)} collective-permute-done((f32[32,3072]{1,0:T(8,128)S(1)}, f32[32,3072]{1,0:T(8,128)S(1)}, u32[]{:S(2)}, u32[]{:S(2)}) %collective-permute-start.2) | collective-permute-done | bytes 393248 | tf_op jit(solution)/shard_map/ppermute | solution.py:63
  35.2 0.1 shard_map.44
  35.3 2.1 %collective-permute-start.3 = (f32[32,1536]{1,0:T(8,128)S(1)}, f32[32,1536]{1,0:T(8,128)S(1)}, u32[]{:S(2)}, u32[]{:S(2)}) collective-permute-start(f32[32,1536]{1,0:T(8,128)S(1)} %get-tuple-element.51), channel_id=1, source_target_pairs={{0,8},{8,0},{16,24},{24,16},{32,40},{40,32},{48,56},{56,48},{64,72... | collective-permute-start | bytes 589832 | tf_op jit(solution)/shard_map/ppermute | solution.py:71
  37.4 0.7 collective-permute-start.4
  38.0 0.7 collective-permute-done.7.middle_came_ref
  38.7 2.4 %collective-permute-done.3.one_ref = f32[32,1536]{1,0:T(8,128)S(1)} collective-permute-done((f32[32,1536]{1,0:T(8,128)S(1)}, f32[32,1536]{1,0:T(8,128)S(1)}, u32[]{:S(2)}, u32[]{:S(2)}) %collective-permute-start.3) | collective-permute-done | bytes 196640 | tf_op jit(solution)/shard_map/ppermute | solution.py:71
  41.2 0.0 collective-permute-done.4.two_ref
  41.2 0.1 shard_map.48.mine_ref.refs_0_
  41.3 0.1 collective-permute-start.9
  41.4 1.7 %collective-permute-start.8 = (f32[32,5632]{1,0:T(8,128)S(1)}, f32[32,5632]{1,0:T(8,128)S(1)}, u32[]{:S(2)}, u32[]{:S(2)}) collective-permute-start(f32[32,5632]{1,0:T(8,128)S(1)} %shard_map.48.mine_ref.refs_0_), channel_id=1, source_target_pairs={{0,2},{1,7},{2,0},{3,5},{4,6},{5,3},{6,4},{7,1},{8,10},{9,15},{10,... | collective-permute-start | bytes 2162696 | tf_op jit(solution)/shard_map/ppermute | solution.py:63
  43.0 0.5 collective-permute-done.9.other_ref.refs_1_
  43.5 7.7 %shard_map.49 = (f32[512,256]{1,0:T(8,128)S(1)}, f32[512,256]{1,0:T(8,128)S(1)}) custom-call(f32[1024,4096]{1,0:T(8,128)S(1)} %get-tuple-element.54.s_ref, f32[32,5632]{1,0:T(8,128)S(1)} %shard_map.48.mine_ref.refs_0_, f32[32,5632]{1,0:T(8,128)S(1)} %collective-permute-done.9.other_ref.refs_1_), custom_call_target="tpu_custom_call" | custom-call | flops 80000000000 | bytes 16777216 | tf_op jit(solution)/shard_map/pallas_call | solution.py:233
  51.3 1.5 %collective-permute-done.8.mine_ref.refs_2_ = f32[32,5632]{1,0:T(8,128)S(1)} collective-permute-done((f32[32,5632]{1,0:T(8,128)S(1)}, f32[32,5632]{1,0:T(8,128)S(1)}, u32[]{:S(2)}, u32[]{:S(2)}) %collective-permute-start.8) | collective-permute-done | bytes 720928 | tf_op jit(solution)/shard_map/ppermute | solution.py:63
  52.7 0.5 collective-permute-start.11
  53.3 5.3 %collective-permute-start.10 = (f32[512,256]{1,0:T(8,128)S(1)}, f32[512,256]{1,0:T(8,128)S(1)}, u32[]{:S(2)}, u32[]{:S(2)}) collective-permute-start(f32[512,256]{1,0:T(8,128)S(1)} %get-tuple-element.64), channel_id=1, source_target_pairs={{0,8},{1,25},{2,10},{3,27},{4,12},{5,29},{6,14},{7,31},{8,0},{9,17... | collective-permute-start | bytes 1572872 | tf_op jit(solution)/shard_map/ppermute | solution.py:63
  58.6 0.0 collective-permute-done.11.other_ref.refs_3_
  58.6 7.7 %shard_map.50 = (f32[512,256]{1,0:T(8,128)S(1)}, f32[512,256]{1,0:T(8,128)S(1)}) custom-call(f32[1024,4096]{1,0:T(8,128)S(1)} %get-tuple-element.54.s_ref, f32[32,5632]{1,0:T(8,128)S(1)} %collective-permute-done.8.mine_ref.refs_2_, f32[32,5632]{1,0:T(8,128)S(1)} %collective-permute-done.11.other_ref.refs_3_), custom_call_target="tpu_custom_call" | custom-call | flops 80000000000 | bytes 16777216 | tf_op jit(solution)/shard_map/pallas_call | solution.py:233
  66.3 1.9 %collective-permute-start.13 = (f32[512,256]{1,0:T(8,128)S(1)}, f32[512,256]{1,0:T(8,128)S(1)}, u32[]{:S(2)}, u32[]{:S(2)}) collective-permute-start(f32[512,256]{1,0:T(8,128)S(1)} %get-tuple-element.66), channel_id=1, source_target_pairs={{0,8},{1,25},{2,10},{3,27},{4,12},{5,29},{6,14},{7,31},{8,0},{9,17... | collective-permute-start | bytes 1572872 | tf_op jit(solution)/shard_map/ppermute | solution.py:63
  68.2 0.0 collective-permute-done.10.b_ref
  68.2 1.2 shard_map.51
  69.3 2.4 %collective-permute-start.12 = (f32[320,256]{1,0:T(8,128)S(1)}, f32[320,256]{1,0:T(8,128)S(1)}, u32[]{:S(2)}, u32[]{:S(2)}) collective-permute-start(f32[320,256]{1,0:T(8,128)S(1)} %get-tuple-element.69), channel_id=1, source_target_pairs={{0,32},{1,97},{2,34},{3,99},{4,36},{5,101},{6,38},{7,103},{8,40},{... | collective-permute-start | bytes 983048 | tf_op jit(solution)/shard_map/ppermute | solution.py:63
  71.7 3.8 %collective-permute-done.13.b_ref = f32[512,256]{1,0:T(8,128)S(1)} collective-permute-done((f32[512,256]{1,0:T(8,128)S(1)}, f32[512,256]{1,0:T(8,128)S(1)}, u32[]{:S(2)}, u32[]{:S(2)}) %collective-permute-start.13) | collective-permute-done | bytes 524320 | tf_op jit(solution)/shard_map/ppermute | solution.py:63
  75.5 0.1 shard_map.52
  75.6 4.0 %collective-permute-start.15 = (f32[256,256]{1,0:T(8,128)S(1)}, f32[256,256]{1,0:T(8,128)S(1)}, u32[]{:S(2)}, u32[]{:S(2)}) collective-permute-start(f32[256,256]{1,0:T(8,128)S(1)} %get-tuple-element.72), channel_id=1, source_target_pairs={{0,32},{1,97},{2,34},{3,99},{4,36},{5,101},{6,38},{7,103},{8,40},{... | collective-permute-start | bytes 786440 | tf_op jit(solution)/shard_map/ppermute | solution.py:63
  79.6 0.0 collective-permute-done.12.b_ref
  79.6 2.2 %collective-permute-start.14 = (f32[320,256]{1,0:T(8,128)S(1)}, f32[320,256]{1,0:T(8,128)S(1)}, u32[]{:S(2)}, u32[]{:S(2)}) collective-permute-start(f32[320,256]{1,0:T(8,128)S(1)} %shard_map.53.a_ref), channel_id=1, source_target_pairs={{0,96},{1,33},{2,98},{3,35},{4,100},{5,37},{6,102},{7,39},{8,104},... | collective-permute-start | bytes 983048 | tf_op jit(solution)/shard_map/ppermute | solution.py:63
  81.8 3.6 %collective-permute-done.15.b_ref = f32[256,256]{1,0:T(8,128)S(1)} collective-permute-done((f32[256,256]{1,0:T(8,128)S(1)}, f32[256,256]{1,0:T(8,128)S(1)}, u32[]{:S(2)}, u32[]{:S(2)}) %collective-permute-start.15) | collective-permute-done | bytes 262176 | tf_op jit(solution)/shard_map/ppermute | solution.py:63
  85.5 4.7 %collective-permute-start.17 = (f32[256,256]{1,0:T(8,128)S(1)}, f32[256,256]{1,0:T(8,128)S(1)}, u32[]{:S(2)}, u32[]{:S(2)}) collective-permute-start(f32[256,256]{1,0:T(8,128)S(1)} %shard_map.54.a_ref), channel_id=1, source_target_pairs={{0,96},{1,33},{2,98},{3,35},{4,100},{5,37},{6,102},{7,39},{8,104},... | collective-permute-start | bytes 786440 | tf_op jit(solution)/shard_map/ppermute | solution.py:63
  90.1 0.0 collective-permute-done.14.b_ref
  90.2 1.1 collective-permute-start.16
  91.3 3.2 %collective-permute-done.17.b_ref = f32[256,256]{1,0:T(8,128)S(1)} collective-permute-done((f32[256,256]{1,0:T(8,128)S(1)}, f32[256,256]{1,0:T(8,128)S(1)}, u32[]{:S(2)}, u32[]{:S(2)}) %collective-permute-start.17) | collective-permute-done | bytes 262176 | tf_op jit(solution)/shard_map/ppermute | solution.py:63
  94.5 2.6 %collective-permute-start.20 = (f32[256,256]{1,0:T(8,128)S(1)}, f32[256,256]{1,0:T(8,128)S(1)}, u32[]{:S(2)}, u32[]{:S(2)}) collective-permute-start(f32[256,256]{1,0:T(8,128)S(1)} %shard_map.56.a_ref), channel_id=1, source_target_pairs={{0,24},{1,9},{2,26},{3,11},{4,28},{5,13},{6,30},{7,15},{8,16},{9,1... | collective-permute-start | bytes 786440 | tf_op jit(solution)/shard_map/ppermute | solution.py:63
  97.1 2.0 %collective-permute-done.16.b_ref = f32[320,256]{1,0:T(8,128)S(1)} collective-permute-done((f32[320,256]{1,0:T(8,128)S(1)}, f32[320,256]{1,0:T(8,128)S(1)}, u32[]{:S(2)}, u32[]{:S(2)}) %collective-permute-start.16) | collective-permute-done | bytes 327712 | tf_op jit(solution)/shard_map/ppermute | solution.py:63
  99.1 0.1 collective-permute-start.18
  99.2 0.1 collective-permute-start.19
  99.3 2.9 %collective-permute-done.20.b_ref = f32[256,256]{1,0:T(8,128)S(1)} collective-permute-done((f32[256,256]{1,0:T(8,128)S(1)}, f32[256,256]{1,0:T(8,128)S(1)}, u32[]{:S(2)}, u32[]{:S(2)}) %collective-permute-start.20) | collective-permute-done | bytes 262176 | tf_op jit(solution)/shard_map/ppermute | solution.py:63
  102.2 0.9 collective-permute-start.22
  103.2 2.5 %collective-permute-done.19.b_ref = f32[256,256]{1,0:T(8,128)S(1)} collective-permute-done((f32[256,256]{1,0:T(8,128)S(1)}, f32[256,256]{1,0:T(8,128)S(1)}, u32[]{:S(2)}, u32[]{:S(2)}) %collective-permute-start.19) | collective-permute-done | bytes 262176 | tf_op jit(solution)/shard_map/ppermute | solution.py:63
  105.7 0.1 shard_map.61.refs_4_
  105.7 2.0 %collective-permute-start.21 = (f32[512,256]{1,0:T(8,128)S(1)}, f32[512,256]{1,0:T(8,128)S(1)}, u32[]{:S(2)}, u32[]{:S(2)}) collective-permute-start(f32[512,256]{1,0:T(8,128)S(1)} %shard_map.61.refs_4_), channel_id=1, source_target_pairs={{0,8},{1,25},{2,10},{3,27},{4,12},{5,29},{6,14},{7,31},{8,0},{9,17... | collective-permute-start | bytes 1572872 | tf_op jit(solution)/shard_map/ppermute | solution.py:63
  107.8 0.9 collective-permute-done.22.b_ref
  108.7 0.1 shard_map.62.refs_6_
  108.7 1.8 %collective-permute-start.23 = (f32[512,256]{1,0:T(8,128)S(1)}, f32[512,256]{1,0:T(8,128)S(1)}, u32[]{:S(2)}, u32[]{:S(2)}) collective-permute-start(f32[512,256]{1,0:T(8,128)S(1)} %shard_map.62.refs_6_), channel_id=1, source_target_pairs={{0,8},{1,25},{2,10},{3,27},{4,12},{5,29},{6,14},{7,31},{8,0},{9,17... | collective-permute-start | bytes 1572872 | tf_op jit(solution)/shard_map/ppermute | solution.py:63
  110.6 0.0 collective-permute-done.18.b_ref
  110.6 4.2 %shard_map.59.inverse_ref = f32[128,128]{1,0:T(8,128)S(1)} custom-call(f32[64,256]{1,0:T(8,128)S(1)} %shard_map.58.tail_ref), custom_call_target="tpu_custom_call" | custom-call | tf_op jit(solution)/shard_map/pallas_call | solution.py:370
  114.8 0.2 collective-permute-done.21.refs_5_
  115.0 3.1 %shard_map.63 = (f32[128,512]{1,0:T(8,128)}, f32[4,1024,128]{2,1,0:T(8,128)}, f32[4,512,128]{2,1,0:T(8,128)S(1)}, f32[128,128]{1,0:T(8,128)S(1)}) custom-call(f32[128,128]{1,0:T(8,128)S(1)} %shard_map.59.inverse_ref, f32[32,5632]{1,0:T(8,128)S(1)} %shard_map.48.mine_ref.refs_0_, f32[32,5632]{1,0:T(8,128)S(1)} %collective-permute-done.9.other_ref.refs_1_, ...), custom_call_target="tpu_custom_call" | custom-call | tf_op jit(solution)/shard_map/pallas_call | solution.py:478
  118.1 2.5 %collective-permute-done.23.came_ref = f32[512,256]{1,0:T(8,128)S(1)} collective-permute-done((f32[512,256]{1,0:T(8,128)S(1)}, f32[512,256]{1,0:T(8,128)S(1)}, u32[]{:S(2)}, u32[]{:S(2)}) %collective-permute-start.23) | collective-permute-done | bytes 524320 | tf_op jit(solution)/shard_map/ppermute | solution.py:63
  120.6 1.4 %shard_map.64 = f32[4,1024,128]{2,1,0:T(8,128)} custom-call(f32[128,128]{1,0:T(8,128)S(1)} %get-tuple-element.85.turned_ref, f32[4,512,128]{2,1,0:T(8,128)S(1)} %get-tuple-element.86.partial_ref, f32[512,256]{1,0:T(8,128)S(1)} %collective-permute-done.23.came_ref, f32[4,1024,128]{2,1,0:T(8,128)} %get-tuple-element.87._), custom_call_target="tpu_custom_call", output_to_operand_aliasing={{}: (3, {})} | custom-call | tf_op jit(solution)/shard_map/pallas_call | solution.py:506
  (9 shorter events, 0.3 us)
Async XLA Ops:
  13.9 4.2 %collective-permute-start = (f32[64,3072]{1,0:T(8,128)S(1)}, f32[64,3072]{1,0:T(8,128)S(1)}, u32[]{:S(2)}, u32[]{:S(2)}) collective-permute-start(f32[64,3072]{1,0:T(8,128)S(1)} %get-tuple-element.46), channel_id=1, source_target_pairs={{0,1},{1,0},{2,3},{3,2},{4,5},{5,4},{6,7},{7,6},{8,9},{9,8},{10,11... | collective-permute-start | bytes 2359304 | tf_op jit(solution)/shard_map/ppermute | solution.py:391
  17.6 2.4 %collective-permute-start.5 = (f32[64,2560]{1,0:T(8,128)S(1)}, f32[64,2560]{1,0:T(8,128)S(1)}, u32[]{:S(2)}, u32[]{:S(2)}) collective-permute-start(f32[64,2560]{1,0:T(8,128)S(1)} %get-tuple-element.58), channel_id=1, source_target_pairs={{0,1},{1,0},{2,3},{3,2},{4,5},{5,4},{6,7},{7,6},{8,9},{9,8},{10,11... | collective-permute-start | bytes 1966088 | tf_op jit(solution)/shard_map/ppermute | solution.py:392
  18.2 7.9 %collective-permute-start.1 = (f32[32,3072]{1,0:T(8,128)S(1)}, f32[32,3072]{1,0:T(8,128)S(1)}, u32[]{:S(2)}, u32[]{:S(2)}) collective-permute-start(f32[32,3072]{1,0:T(8,128)S(1)} %get-tuple-element.48), channel_id=1, source_target_pairs={{0,2},{1,7},{2,0},{3,5},{4,6},{5,3},{6,4},{7,1},{8,10},{9,15},{10,... | collective-permute-start | bytes 1179656 | tf_op jit(solution)/shard_map/ppermute | solution.py:63
  20.1 10.3 %collective-permute-start.6 = (f32[32,2560]{1,0:T(8,128)S(1)}, f32[32,2560]{1,0:T(8,128)S(1)}, u32[]{:S(2)}, u32[]{:S(2)}) collective-permute-start(f32[32,2560]{1,0:T(8,128)S(1)} %get-tuple-element.60), channel_id=1, source_target_pairs={{0,2},{1,7},{2,0},{3,5},{4,6},{5,3},{6,4},{7,1},{8,10},{9,15},{10,... | collective-permute-start | bytes 983048 | tf_op jit(solution)/shard_map/ppermute | solution.py:63
  26.1 9.1 %collective-permute-start.2 = (f32[32,3072]{1,0:T(8,128)S(1)}, f32[32,3072]{1,0:T(8,128)S(1)}, u32[]{:S(2)}, u32[]{:S(2)}) collective-permute-start(f32[32,3072]{1,0:T(8,128)S(1)} %shard_map.43.a_ref), channel_id=1, source_target_pairs={{0,6},{1,3},{2,4},{3,1},{4,2},{5,7},{6,0},{7,5},{8,14},{9,11},{10,... | collective-permute-start | bytes 1179656 | tf_op jit(solution)/shard_map/ppermute | solution.py:63
  30.4 8.4 %collective-permute-start.7 = (f32[32,2560]{1,0:T(8,128)S(1)}, f32[32,2560]{1,0:T(8,128)S(1)}, u32[]{:S(2)}, u32[]{:S(2)}) collective-permute-start(f32[32,2560]{1,0:T(8,128)S(1)} %shard_map.47.middle_ref), channel_id=1, source_target_pairs={{0,6},{1,3},{2,4},{3,1},{4,2},{5,7},{6,0},{7,5},{8,14},{9,11},{10,... | collective-permute-start | bytes 983048 | tf_op jit(solution)/shard_map/ppermute | solution.py:63
  35.3 5.9 %collective-permute-start.3 = (f32[32,1536]{1,0:T(8,128)S(1)}, f32[32,1536]{1,0:T(8,128)S(1)}, u32[]{:S(2)}, u32[]{:S(2)}) collective-permute-start(f32[32,1536]{1,0:T(8,128)S(1)} %get-tuple-element.51), channel_id=1, source_target_pairs={{0,8},{8,0},{16,24},{24,16},{32,40},{40,32},{48,56},{56,48},{64,72... | collective-permute-start | bytes 589832 | tf_op jit(solution)/shard_map/ppermute | solution.py:71
  37.4 3.8 %collective-permute-start.4 = (f32[32,1536]{1,0:T(8,128)S(1)}, f32[32,1536]{1,0:T(8,128)S(1)}, u32[]{:S(2)}, u32[]{:S(2)}) collective-permute-start(f32[32,1536]{1,0:T(8,128)S(1)} %get-tuple-element.52), channel_id=1, source_target_pairs={{8,16},{16,8},{24,32},{32,24},{40,48},{48,40},{56,64},{64,56},{72,... | collective-permute-start | bytes 589832 | tf_op jit(solution)/shard_map/ppermute | solution.py:71
  41.3 2.3 %collective-permute-start.9 = (f32[32,5632]{1,0:T(8,128)S(1)}, f32[32,5632]{1,0:T(8,128)S(1)}, u32[]{:S(2)}, u32[]{:S(2)}) collective-permute-start(f32[32,5632]{1,0:T(8,128)S(1)} %shard_map.48.mine_ref.refs_0_), channel_id=1, source_target_pairs={{0,1},{1,0},{2,3},{3,2},{4,5},{5,4},{6,7},{7,6},{8,9},{9,8},{10,11... | collective-permute-start | bytes 2162696 | tf_op jit(solution)/shard_map/ppermute | solution.py:421
  41.4 11.4 %collective-permute-start.8 = (f32[32,5632]{1,0:T(8,128)S(1)}, f32[32,5632]{1,0:T(8,128)S(1)}, u32[]{:S(2)}, u32[]{:S(2)}) collective-permute-start(f32[32,5632]{1,0:T(8,128)S(1)} %shard_map.48.mine_ref.refs_0_), channel_id=1, source_target_pairs={{0,2},{1,7},{2,0},{3,5},{4,6},{5,3},{6,4},{7,1},{8,10},{9,15},{10,... | collective-permute-start | bytes 2162696 | tf_op jit(solution)/shard_map/ppermute | solution.py:63
  52.7 5.8 %collective-permute-start.11 = (f32[32,5632]{1,0:T(8,128)S(1)}, f32[32,5632]{1,0:T(8,128)S(1)}, u32[]{:S(2)}, u32[]{:S(2)}) collective-permute-start(f32[32,5632]{1,0:T(8,128)S(1)} %collective-permute-done.8.mine_ref.refs_2_), channel_id=1, source_target_pairs={{0,1},{1,0},{2,3},{3,2},{4,5},{5,4},{6,7},{7,6},{8,9},{9,8},{10,11... | collective-permute-start | bytes 2162696 | tf_op jit(solution)/shard_map/ppermute | solution.py:426
  53.3 14.9 %collective-permute-start.10 = (f32[512,256]{1,0:T(8,128)S(1)}, f32[512,256]{1,0:T(8,128)S(1)}, u32[]{:S(2)}, u32[]{:S(2)}) collective-permute-start(f32[512,256]{1,0:T(8,128)S(1)} %get-tuple-element.64), channel_id=1, source_target_pairs={{0,8},{1,25},{2,10},{3,27},{4,12},{5,29},{6,14},{7,31},{8,0},{9,17... | collective-permute-start | bytes 1572872 | tf_op jit(solution)/shard_map/ppermute | solution.py:63
  66.3 9.3 %collective-permute-start.13 = (f32[512,256]{1,0:T(8,128)S(1)}, f32[512,256]{1,0:T(8,128)S(1)}, u32[]{:S(2)}, u32[]{:S(2)}) collective-permute-start(f32[512,256]{1,0:T(8,128)S(1)} %get-tuple-element.66), channel_id=1, source_target_pairs={{0,8},{1,25},{2,10},{3,27},{4,12},{5,29},{6,14},{7,31},{8,0},{9,17... | collective-permute-start | bytes 1572872 | tf_op jit(solution)/shard_map/ppermute | solution.py:63
  69.3 10.2 %collective-permute-start.12 = (f32[320,256]{1,0:T(8,128)S(1)}, f32[320,256]{1,0:T(8,128)S(1)}, u32[]{:S(2)}, u32[]{:S(2)}) collective-permute-start(f32[320,256]{1,0:T(8,128)S(1)} %get-tuple-element.69), channel_id=1, source_target_pairs={{0,32},{1,97},{2,34},{3,99},{4,36},{5,101},{6,38},{7,103},{8,40},{... | collective-permute-start | bytes 983048 | tf_op jit(solution)/shard_map/ppermute | solution.py:63
  75.6 9.8 %collective-permute-start.15 = (f32[256,256]{1,0:T(8,128)S(1)}, f32[256,256]{1,0:T(8,128)S(1)}, u32[]{:S(2)}, u32[]{:S(2)}) collective-permute-start(f32[256,256]{1,0:T(8,128)S(1)} %get-tuple-element.72), channel_id=1, source_target_pairs={{0,32},{1,97},{2,34},{3,99},{4,36},{5,101},{6,38},{7,103},{8,40},{... | collective-permute-start | bytes 786440 | tf_op jit(solution)/shard_map/ppermute | solution.py:63
  79.6 10.5 %collective-permute-start.14 = (f32[320,256]{1,0:T(8,128)S(1)}, f32[320,256]{1,0:T(8,128)S(1)}, u32[]{:S(2)}, u32[]{:S(2)}) collective-permute-start(f32[320,256]{1,0:T(8,128)S(1)} %shard_map.53.a_ref), channel_id=1, source_target_pairs={{0,96},{1,33},{2,98},{3,35},{4,100},{5,37},{6,102},{7,39},{8,104},... | collective-permute-start | bytes 983048 | tf_op jit(solution)/shard_map/ppermute | solution.py:63
  85.5 9.0 %collective-permute-start.17 = (f32[256,256]{1,0:T(8,128)S(1)}, f32[256,256]{1,0:T(8,128)S(1)}, u32[]{:S(2)}, u32[]{:S(2)}) collective-permute-start(f32[256,256]{1,0:T(8,128)S(1)} %shard_map.54.a_ref), channel_id=1, source_target_pairs={{0,96},{1,33},{2,98},{3,35},{4,100},{5,37},{6,102},{7,39},{8,104},... | collective-permute-start | bytes 786440 | tf_op jit(solution)/shard_map/ppermute | solution.py:63
  90.2 8.9 %collective-permute-start.16 = (f32[320,256]{1,0:T(8,128)S(1)}, f32[320,256]{1,0:T(8,128)S(1)}, u32[]{:S(2)}, u32[]{:S(2)}) collective-permute-start(f32[320,256]{1,0:T(8,128)S(1)} %shard_map.55.a_ref), channel_id=1, source_target_pairs={{0,24},{1,9},{2,26},{3,11},{4,28},{5,13},{6,30},{7,15},{8,16},{9,1... | collective-permute-start | bytes 983048 | tf_op jit(solution)/shard_map/ppermute | solution.py:63
  94.5 7.7 %collective-permute-start.20 = (f32[256,256]{1,0:T(8,128)S(1)}, f32[256,256]{1,0:T(8,128)S(1)}, u32[]{:S(2)}, u32[]{:S(2)}) collective-permute-start(f32[256,256]{1,0:T(8,128)S(1)} %shard_map.56.a_ref), channel_id=1, source_target_pairs={{0,24},{1,9},{2,26},{3,11},{4,28},{5,13},{6,30},{7,15},{8,16},{9,1... | collective-permute-start | bytes 786440 | tf_op jit(solution)/shard_map/ppermute | solution.py:63
  99.1 11.4 %collective-permute-start.18 = (f32[64,256]{1,0:T(8,128)S(1)}, f32[64,256]{1,0:T(8,128)S(1)}, u32[]{:S(2)}, u32[]{:S(2)}) collective-permute-start(f32[64,256]{1,0:T(8,128)S(1)} %get-tuple-element.79.a_ref), channel_id=1, source_target_pairs={{0,8},{1,25},{2,10},{3,27},{4,12},{5,29},{6,14},{7,31},{8,0},{9,17... | collective-permute-start | bytes 196616 | tf_op jit(solution)/shard_map/ppermute | solution.py:63
  99.2 6.5 %collective-permute-start.19 = (f32[256,256]{1,0:T(8,128)S(1)}, f32[256,256]{1,0:T(8,128)S(1)}, u32[]{:S(2)}, u32[]{:S(2)}) collective-permute-start(f32[256,256]{1,0:T(8,128)S(1)} %get-tuple-element.80.a_ref), channel_id=1, source_target_pairs={{0,32},{1,97},{2,34},{3,99},{4,36},{5,101},{6,38},{7,103},{8,40},{... | collective-permute-start | bytes 786440 | tf_op jit(solution)/shard_map/ppermute | solution.py:63
  102.2 6.5 %collective-permute-start.22 = (f32[256,256]{1,0:T(8,128)S(1)}, f32[256,256]{1,0:T(8,128)S(1)}, u32[]{:S(2)}, u32[]{:S(2)}) collective-permute-start(f32[256,256]{1,0:T(8,128)S(1)} %shard_map.60.a_ref), channel_id=1, source_target_pairs={{0,32},{1,97},{2,34},{3,99},{4,36},{5,101},{6,38},{7,103},{8,40},{... | collective-permute-start | bytes 786440 | tf_op jit(solution)/shard_map/ppermute | solution.py:63
  105.7 9.3 %collective-permute-start.21 = (f32[512,256]{1,0:T(8,128)S(1)}, f32[512,256]{1,0:T(8,128)S(1)}, u32[]{:S(2)}, u32[]{:S(2)}) collective-permute-start(f32[512,256]{1,0:T(8,128)S(1)} %shard_map.61.refs_4_), channel_id=1, source_target_pairs={{0,8},{1,25},{2,10},{3,27},{4,12},{5,29},{6,14},{7,31},{8,0},{9,17... | collective-permute-start | bytes 1572872 | tf_op jit(solution)/shard_map/ppermute | solution.py:63
  108.7 11.9 %collective-permute-start.23 = (f32[512,256]{1,0:T(8,128)S(1)}, f32[512,256]{1,0:T(8,128)S(1)}, u32[]{:S(2)}, u32[]{:S(2)}) collective-permute-start(f32[512,256]{1,0:T(8,128)S(1)} %shard_map.62.refs_6_), channel_id=1, source_target_pairs={{0,8},{1,25},{2,10},{3,27},{4,12},{5,29},{6,14},{7,31},{8,0},{9,17... | collective-permute-start | bytes 1572872 | tf_op jit(solution)/shard_map/ppermute | solution.py:63

commit v8 on v7

--- a/solution.py
+++ b/solution.py
@@ -10,8 +10,8 @@
 from jax.sharding import PartitionSpec as P
 
 LAG = 512
-WIDE = 1024
-AHEAD = 3
+WIDE = 2048
+AHEAD = 4
 F32 = jnp.float32
 BF16 = jnp.bfloat16
 NT = (((1,), (1,)), ((), ()))
@@ -302,7 +302,7 @@
     return call(body, [(2 * count, mine.shape[1])], [mine, came], 8, weight=WEIGHT)[0]
 
 
-ROUTE = (("z", 0), ("x", 0), ("x", 1), ("z", 1), ("x", 0), ("z", 0))
+ROUTE = (("x", 0), ("z", 0), ("z", 1), ("x", 1), ("z", 0), ("x", 0))
 
 
 def advanced(at, keep, came, tail):

time: 122 us -> 121 us (level)
  waiting for transfers between devices: 34 us -> 37.1 us
  starting transfers between devices: 44.3 us -> 41.2 us
    ppermute x18, starting transfers between devices: 40.3 us -> 37.1 us  [along(): return lax.ppermute(value, AXES, pairs)]
    ppermute x18, waiting for transfers between devices: 31 us -> 34.1 us  [along(): return lax.ppermute(value, AXES, pairs)]
  transfers between devices with their start and end apart: 24 -> 24, of which waited for: 16 -> 17; matrix products, arithmetic and copies ran while one was open for 0% -> 0% of each run, Pallas kernels for 23% -> 23%
where the time goes in v8:
time: 121 us
  Pallas kernels  42.1 us (35%)
  starting transfers between devices  41.2 us (34%)
  waiting for transfers between devices  37.1 us (31%)
    ppermute x18, starting transfers between devices, along(): return lax.ppermute(value, AXES, pairs)  37.1 us
    ppermute x18, waiting for transfers between devices, along(): return lax.ppermute(value, AXES, pairs)  34.1 us
    pallas_call x2, Pallas kernels, projection_partial(): pl.pallas_call(body, out_shape=[jax.ShapeDtypeStruct((channels // 2, lane...  14.6 us
    pallas_call x1, Pallas kernels, sketch_ends(): pl.pallas_call(body, out_shape=[ends, ends, jax.ShapeDtypeStruct((rank, b...  13.3 us
    pallas_call x18, Pallas kernels, call(): pl.pallas_call(body, out_shape=[jax.ShapeDtypeStruct(shape, F32) for shap...  5.47 us
    pallas_call x1, Pallas kernels, inverse_factor(): pl.pallas_call(body, out_shape=jax.ShapeDtypeStruct((rank, rank), F32), i...  4.23 us
    pallas_call x1, Pallas kernels, shards(): pl.pallas_call(finish_first, out_shape=outs, in_specs=whole(8), out_specs...  3.08 us
    ppermute x2, starting transfers between devices, paired(): return lax.ppermute(value, ('x', 'z'), pairs)  2.74 us
  transfers between devices with their start and end apart: 24, of which 17 were waited for; matrix products, arithmetic and copies ran while one was open for 0% of the time, Pallas kernels for 23%

profile of v8, /device:TPU:0, one launch (start us, length us, event | category | flops | bytes accessed | tf_op | source)
XLA Modules:
  0.0 121.3 jit_solution(18083796163440263368)
XLA Ops:
  0.6 13.3 %shard_map.41 = (f32[64,3072]{1,0:T(8,128)S(1)}, f32[64,3072]{1,0:T(8,128)S(1)}, f32[128,2560]{1,0:T(8,128)S(1)}, f32[1024,4096]{1,0:T(8,128)S(1)}, bf16[512,102...) custom-call(f32[1024,4096]{1,0:T(8,128)} %s_hbm.1, f32[4,1024,128]{2,1,0:T(8,128)} %o_hbm.1), custom_call_target="tpu_custom_call" | custom-call | flops 80000000000 | bytes 16777216 | tf_op jit(solution)/shard_map/pallas_call | solution.py:149
  13.9 0.1 collective-permute-start
  14.0 3.5 %shard_map.45 = (f32[64,2560]{1,0:T(8,128)S(1)}, f32[64,2560]{1,0:T(8,128)S(1)}) custom-call(f32[128,2560]{1,0:T(8,128)S(1)} %get-tuple-element.53.middle_ref, f32[1024,4096]{1,0:T(8,128)S(1)} %get-tuple-element.54.s_ref, bf16[512,1024]{1,0:T(8,128)(2,1)S(1)} %get-tuple-element.55.high_ref, bf16[512,1024]{1,0:T(8,128)(2,1)S(1)} %get-tuple-element.56.low_ref), custom_call_target="tpu_custom_call" | custom-call | flops 40000000000 | tf_op jit(solution)/shard_map/pallas_call | solution.py:38
  17.6 0.6 collective-permute-start.5
  18.1 0.0 collective-permute-done.b_ref
  18.2 0.1 shard_map.42
  18.2 1.7 %collective-permute-start.1 = (f32[32,3072]{1,0:T(8,128)S(1)}, f32[32,3072]{1,0:T(8,128)S(1)}, u32[]{:S(2)}, u32[]{:S(2)}) collective-permute-start(f32[32,3072]{1,0:T(8,128)S(1)} %get-tuple-element.48), channel_id=1, source_target_pairs={{0,2},{1,7},{2,0},{3,5},{4,6},{5,3},{6,4},{7,1},{8,10},{9,15},{10,... | collective-permute-start | bytes 1179656 | tf_op jit(solution)/shard_map/ppermute | solution.py:63
  20.0 0.0 collective-permute-done.5.b_ref
  20.0 0.1 shard_map.46
  20.1 1.6 %collective-permute-start.6 = (f32[32,2560]{1,0:T(8,128)S(1)}, f32[32,2560]{1,0:T(8,128)S(1)}, u32[]{:S(2)}, u32[]{:S(2)}) collective-permute-start(f32[32,2560]{1,0:T(8,128)S(1)} %get-tuple-element.60), channel_id=1, source_target_pairs={{0,2},{1,7},{2,0},{3,5},{4,6},{5,3},{6,4},{7,1},{8,10},{9,15},{10,... | collective-permute-start | bytes 983048 | tf_op jit(solution)/shard_map/ppermute | solution.py:63
  21.7 4.4 %collective-permute-done.1.b_ref = f32[32,3072]{1,0:T(8,128)S(1)} collective-permute-done((f32[32,3072]{1,0:T(8,128)S(1)}, f32[32,3072]{1,0:T(8,128)S(1)}, u32[]{:S(2)}, u32[]{:S(2)}) %collective-permute-start.1) | collective-permute-done | bytes 393248 | tf_op jit(solution)/shard_map/ppermute | solution.py:63
  26.1 3.2 %collective-permute-start.2 = (f32[32,3072]{1,0:T(8,128)S(1)}, f32[32,3072]{1,0:T(8,128)S(1)}, u32[]{:S(2)}, u32[]{:S(2)}) collective-permute-start(f32[32,3072]{1,0:T(8,128)S(1)} %shard_map.43.a_ref), channel_id=1, source_target_pairs={{0,6},{1,3},{2,4},{3,1},{4,2},{5,7},{6,0},{7,5},{8,14},{9,11},{10,... | collective-permute-start | bytes 1179656 | tf_op jit(solution)/shard_map/ppermute | solution.py:63
  29.3 1.0 collective-permute-done.6.b_ref
  30.4 3.1 %collective-permute-start.7 = (f32[32,2560]{1,0:T(8,128)S(1)}, f32[32,2560]{1,0:T(8,128)S(1)}, u32[]{:S(2)}, u32[]{:S(2)}) collective-permute-start(f32[32,2560]{1,0:T(8,128)S(1)} %shard_map.47.middle_ref), channel_id=1, source_target_pairs={{0,6},{1,3},{2,4},{3,1},{4,2},{5,7},{6,0},{7,5},{8,14},{9,11},{10,... | collective-permute-start | bytes 983048 | tf_op jit(solution)/shard_map/ppermute | solution.py:63
  33.4 1.8 %collective-permute-done.2.b_ref = f32[32,3072]{1,0:T(8,128)S(1)} collective-permute-done((f32[32,3072]{1,0:T(8,128)S(1)}, f32[32,3072]{1,0:T(8,128)S(1)}, u32[]{:S(2)}, u32[]{:S(2)}) %collective-permute-start.2) | collective-permute-done | bytes 393248 | tf_op jit(solution)/shard_map/ppermute | solution.py:63
  35.2 0.1 shard_map.44
  35.3 2.1 %collective-permute-start.3 = (f32[32,1536]{1,0:T(8,128)S(1)}, f32[32,1536]{1,0:T(8,128)S(1)}, u32[]{:S(2)}, u32[]{:S(2)}) collective-permute-start(f32[32,1536]{1,0:T(8,128)S(1)} %get-tuple-element.51), channel_id=1, source_target_pairs={{0,8},{8,0},{16,24},{24,16},{32,40},{40,32},{48,56},{56,48},{64,72... | collective-permute-start | bytes 589832 | tf_op jit(solution)/shard_map/ppermute | solution.py:71
  37.4 0.7 collective-permute-start.4
  38.0 0.7 collective-permute-done.7.middle_came_ref
  38.7 2.4 %collective-permute-done.3.one_ref = f32[32,1536]{1,0:T(8,128)S(1)} collective-permute-done((f32[32,1536]{1,0:T(8,128)S(1)}, f32[32,1536]{1,0:T(8,128)S(1)}, u32[]{:S(2)}, u32[]{:S(2)}) %collective-permute-start.3) | collective-permute-done | bytes 196640 | tf_op jit(solution)/shard_map/ppermute | solution.py:71
  41.2 0.0 collective-permute-done.4.two_ref
  41.2 0.1 shard_map.48.mine_ref.refs_0_
  41.3 0.1 collective-permute-start.9
  41.4 1.7 %collective-permute-start.8 = (f32[32,5632]{1,0:T(8,128)S(1)}, f32[32,5632]{1,0:T(8,128)S(1)}, u32[]{:S(2)}, u32[]{:S(2)}) collective-permute-start(f32[32,5632]{1,0:T(8,128)S(1)} %shard_map.48.mine_ref.refs_0_), channel_id=1, source_target_pairs={{0,2},{1,7},{2,0},{3,5},{4,6},{5,3},{6,4},{7,1},{8,10},{9,15},{10,... | collective-permute-start | bytes 2162696 | tf_op jit(solution)/shard_map/ppermute | solution.py:63
  43.0 0.5 collective-permute-done.9.other_ref.refs_1_
  43.5 7.3 %shard_map.49 = (f32[512,256]{1,0:T(8,128)S(1)}, f32[512,256]{1,0:T(8,128)S(1)}) custom-call(f32[1024,4096]{1,0:T(8,128)S(1)} %get-tuple-element.54.s_ref, f32[32,5632]{1,0:T(8,128)S(1)} %shard_map.48.mine_ref.refs_0_, f32[32,5632]{1,0:T(8,128)S(1)} %collective-permute-done.9.other_ref.refs_1_), custom_call_target="tpu_custom_call" | custom-call | flops 80000000000 | bytes 16777216 | tf_op jit(solution)/shard_map/pallas_call | solution.py:233
  50.8 1.9 %collective-permute-done.8.mine_ref.refs_2_ = f32[32,5632]{1,0:T(8,128)S(1)} collective-permute-done((f32[32,5632]{1,0:T(8,128)S(1)}, f32[32,5632]{1,0:T(8,128)S(1)}, u32[]{:S(2)}, u32[]{:S(2)}) %collective-permute-start.8) | collective-permute-done | bytes 720928 | tf_op jit(solution)/shard_map/ppermute | solution.py:63
  52.7 0.5 collective-permute-start.11
  53.3 7.4 %collective-permute-start.10 = (f32[512,256]{1,0:T(8,128)S(1)}, f32[512,256]{1,0:T(8,128)S(1)}, u32[]{:S(2)}, u32[]{:S(2)}) collective-permute-start(f32[512,256]{1,0:T(8,128)S(1)} %get-tuple-element.64), channel_id=1, source_target_pairs={{0,32},{1,97},{2,34},{3,99},{4,36},{5,101},{6,38},{7,103},{8,40},{... | collective-permute-start | bytes 1572872 | tf_op jit(solution)/shard_map/ppermute | solution.py:63
  60.6 0.0 collective-permute-done.11.other_ref.refs_3_
  60.6 7.3 %shard_map.50 = (f32[512,256]{1,0:T(8,128)S(1)}, f32[512,256]{1,0:T(8,128)S(1)}) custom-call(f32[1024,4096]{1,0:T(8,128)S(1)} %get-tuple-element.54.s_ref, f32[32,5632]{1,0:T(8,128)S(1)} %collective-permute-done.8.mine_ref.refs_2_, f32[32,5632]{1,0:T(8,128)S(1)} %collective-permute-done.11.other_ref.refs_3_), custom_call_target="tpu_custom_call" | custom-call | flops 80000000000 | bytes 16777216 | tf_op jit(solution)/shard_map/pallas_call | solution.py:233
  67.9 1.9 %collective-permute-start.13 = (f32[512,256]{1,0:T(8,128)S(1)}, f32[512,256]{1,0:T(8,128)S(1)}, u32[]{:S(2)}, u32[]{:S(2)}) collective-permute-start(f32[512,256]{1,0:T(8,128)S(1)} %get-tuple-element.66), channel_id=1, source_target_pairs={{0,32},{1,97},{2,34},{3,99},{4,36},{5,101},{6,38},{7,103},{8,40},{... | collective-permute-start | bytes 1572872 | tf_op jit(solution)/shard_map/ppermute | solution.py:63
  69.8 0.0 collective-permute-done.10.b_ref
  69.8 1.2 shard_map.51
  71.0 0.1 collective-permute-start.12
  71.1 6.1 %collective-permute-done.13.b_ref = f32[512,256]{1,0:T(8,128)S(1)} collective-permute-done((f32[512,256]{1,0:T(8,128)S(1)}, f32[512,256]{1,0:T(8,128)S(1)}, u32[]{:S(2)}, u32[]{:S(2)}) %collective-permute-start.13) | collective-permute-done | bytes 524320 | tf_op jit(solution)/shard_map/ppermute | solution.py:63
  77.2 0.1 shard_map.52
  77.3 0.1 collective-permute-start.15
  77.4 0.8 collective-permute-done.12.b_ref
  78.2 2.6 %collective-permute-start.14 = (f32[320,256]{1,0:T(8,128)S(1)}, f32[320,256]{1,0:T(8,128)S(1)}, u32[]{:S(2)}, u32[]{:S(2)}) collective-permute-start(f32[320,256]{1,0:T(8,128)S(1)} %shard_map.53.a_ref), channel_id=1, source_target_pairs={{0,24},{1,9},{2,26},{3,11},{4,28},{5,13},{6,30},{7,15},{8,16},{9,1... | collective-permute-start | bytes 983048 | tf_op jit(solution)/shard_map/ppermute | solution.py:63
  80.8 3.5 %collective-permute-done.15.b_ref = f32[256,256]{1,0:T(8,128)S(1)} collective-permute-done((f32[256,256]{1,0:T(8,128)S(1)}, f32[256,256]{1,0:T(8,128)S(1)}, u32[]{:S(2)}, u32[]{:S(2)}) %collective-permute-start.15) | collective-permute-done | bytes 262176 | tf_op jit(solution)/shard_map/ppermute | solution.py:63
  84.3 4.8 %collective-permute-start.17 = (f32[256,256]{1,0:T(8,128)S(1)}, f32[256,256]{1,0:T(8,128)S(1)}, u32[]{:S(2)}, u32[]{:S(2)}) collective-permute-start(f32[256,256]{1,0:T(8,128)S(1)} %shard_map.54.a_ref), channel_id=1, source_target_pairs={{0,24},{1,9},{2,26},{3,11},{4,28},{5,13},{6,30},{7,15},{8,16},{9,1... | collective-permute-start | bytes 786440 | tf_op jit(solution)/shard_map/ppermute | solution.py:63
  89.2 0.0 collective-permute-done.14.b_ref
  89.2 1.9 %collective-permute-start.16 = (f32[320,256]{1,0:T(8,128)S(1)}, f32[320,256]{1,0:T(8,128)S(1)}, u32[]{:S(2)}, u32[]{:S(2)}) collective-permute-start(f32[320,256]{1,0:T(8,128)S(1)} %shard_map.55.a_ref), channel_id=1, source_target_pairs={{0,96},{1,33},{2,98},{3,35},{4,100},{5,37},{6,102},{7,39},{8,104},... | collective-permute-start | bytes 983048 | tf_op jit(solution)/shard_map/ppermute | solution.py:63
  91.1 2.4 %collective-permute-done.17.b_ref = f32[256,256]{1,0:T(8,128)S(1)} collective-permute-done((f32[256,256]{1,0:T(8,128)S(1)}, f32[256,256]{1,0:T(8,128)S(1)}, u32[]{:S(2)}, u32[]{:S(2)}) %collective-permute-start.17) | collective-permute-done | bytes 262176 | tf_op jit(solution)/shard_map/ppermute | solution.py:63
  93.5 3.9 %collective-permute-start.20 = (f32[256,256]{1,0:T(8,128)S(1)}, f32[256,256]{1,0:T(8,128)S(1)}, u32[]{:S(2)}, u32[]{:S(2)}) collective-permute-start(f32[256,256]{1,0:T(8,128)S(1)} %shard_map.56.a_ref), channel_id=1, source_target_pairs={{0,96},{1,33},{2,98},{3,35},{4,100},{5,37},{6,102},{7,39},{8,104},... | collective-permute-start | bytes 786440 | tf_op jit(solution)/shard_map/ppermute | solution.py:63
  97.4 0.1 collective-permute-done.16.b_ref
  97.6 0.8 collective-permute-start.18
  98.4 0.0 collective-permute-start.19
  98.4 3.3 %collective-permute-done.20.b_ref = f32[256,256]{1,0:T(8,128)S(1)} collective-permute-done((f32[256,256]{1,0:T(8,128)S(1)}, f32[256,256]{1,0:T(8,128)S(1)}, u32[]{:S(2)}, u32[]{:S(2)}) %collective-permute-start.20) | collective-permute-done | bytes 262176 | tf_op jit(solution)/shard_map/ppermute | solution.py:63
  101.8 0.1 collective-permute-start.22
  101.9 2.9 %collective-permute-done.19.b_ref = f32[256,256]{1,0:T(8,128)S(1)} collective-permute-done((f32[256,256]{1,0:T(8,128)S(1)}, f32[256,256]{1,0:T(8,128)S(1)}, u32[]{:S(2)}, u32[]{:S(2)}) %collective-permute-start.19) | collective-permute-done | bytes 262176 | tf_op jit(solution)/shard_map/ppermute | solution.py:63
  104.8 0.1 shard_map.61.refs_4_
  104.9 1.4 %collective-permute-start.21 = (f32[512,256]{1,0:T(8,128)S(1)}, f32[512,256]{1,0:T(8,128)S(1)}, u32[]{:S(2)}, u32[]{:S(2)}) collective-permute-start(f32[512,256]{1,0:T(8,128)S(1)} %shard_map.61.refs_4_), channel_id=1, source_target_pairs={{0,32},{1,97},{2,34},{3,99},{4,36},{5,101},{6,38},{7,103},{8,40},{... | collective-permute-start | bytes 1572872 | tf_op jit(solution)/shard_map/ppermute | solution.py:63
  106.2 2.0 %collective-permute-done.22.b_ref = f32[256,256]{1,0:T(8,128)S(1)} collective-permute-done((f32[256,256]{1,0:T(8,128)S(1)}, f32[256,256]{1,0:T(8,128)S(1)}, u32[]{:S(2)}, u32[]{:S(2)}) %collective-permute-start.22) | collective-permute-done | bytes 262176 | tf_op jit(solution)/shard_map/ppermute | solution.py:63
  108.3 0.1 shard_map.62.refs_6_
  108.3 0.9 collective-permute-start.23
  109.3 0.0 collective-permute-done.18.b_ref
  109.3 4.2 %shard_map.59.inverse_ref = f32[128,128]{1,0:T(8,128)S(1)} custom-call(f32[64,256]{1,0:T(8,128)S(1)} %shard_map.58.tail_ref), custom_call_target="tpu_custom_call" | custom-call | tf_op jit(solution)/shard_map/pallas_call | solution.py:370
  113.5 0.6 collective-permute-done.21.refs_5_
  114.1 3.1 %shard_map.63 = (f32[128,512]{1,0:T(8,128)}, f32[4,1024,128]{2,1,0:T(8,128)}, f32[4,512,128]{2,1,0:T(8,128)S(1)}, f32[128,128]{1,0:T(8,128)S(1)}) custom-call(f32[128,128]{1,0:T(8,128)S(1)} %shard_map.59.inverse_ref, f32[32,5632]{1,0:T(8,128)S(1)} %shard_map.48.mine_ref.refs_0_, f32[32,5632]{1,0:T(8,128)S(1)} %collective-permute-done.9.other_ref.refs_1_, ...), custom_call_target="tpu_custom_call" | custom-call | tf_op jit(solution)/shard_map/pallas_call | solution.py:478
  117.2 2.5 %collective-permute-done.23.came_ref = f32[512,256]{1,0:T(8,128)S(1)} collective-permute-done((f32[512,256]{1,0:T(8,128)S(1)}, f32[512,256]{1,0:T(8,128)S(1)}, u32[]{:S(2)}, u32[]{:S(2)}) %collective-permute-start.23) | collective-permute-done | bytes 524320 | tf_op jit(solution)/shard_map/ppermute | solution.py:63
  119.7 1.4 %shard_map.64 = f32[4,1024,128]{2,1,0:T(8,128)} custom-call(f32[128,128]{1,0:T(8,128)S(1)} %get-tuple-element.85.turned_ref, f32[4,512,128]{2,1,0:T(8,128)S(1)} %get-tuple-element.86.partial_ref, f32[512,256]{1,0:T(8,128)S(1)} %collective-permute-done.23.came_ref, f32[4,1024,128]{2,1,0:T(8,128)} %get-tuple-element.87._), custom_call_target="tpu_custom_call", output_to_operand_aliasing={{}: (3, {})} | custom-call | tf_op jit(solution)/shard_map/pallas_call | solution.py:506
  (9 shorter events, 0.3 us)
Async XLA Ops:
  13.9 4.2 %collective-permute-start = (f32[64,3072]{1,0:T(8,128)S(1)}, f32[64,3072]{1,0:T(8,128)S(1)}, u32[]{:S(2)}, u32[]{:S(2)}) collective-permute-start(f32[64,3072]{1,0:T(8,128)S(1)} %get-tuple-element.46), channel_id=1, source_target_pairs={{0,1},{1,0},{2,3},{3,2},{4,5},{5,4},{6,7},{7,6},{8,9},{9,8},{10,11... | collective-permute-start | bytes 2359304 | tf_op jit(solution)/shard_map/ppermute | solution.py:391
  17.6 2.4 %collective-permute-start.5 = (f32[64,2560]{1,0:T(8,128)S(1)}, f32[64,2560]{1,0:T(8,128)S(1)}, u32[]{:S(2)}, u32[]{:S(2)}) collective-permute-start(f32[64,2560]{1,0:T(8,128)S(1)} %get-tuple-element.58), channel_id=1, source_target_pairs={{0,1},{1,0},{2,3},{3,2},{4,5},{5,4},{6,7},{7,6},{8,9},{9,8},{10,11... | collective-permute-start | bytes 1966088 | tf_op jit(solution)/shard_map/ppermute | solution.py:392
  18.2 7.9 %collective-permute-start.1 = (f32[32,3072]{1,0:T(8,128)S(1)}, f32[32,3072]{1,0:T(8,128)S(1)}, u32[]{:S(2)}, u32[]{:S(2)}) collective-permute-start(f32[32,3072]{1,0:T(8,128)S(1)} %get-tuple-element.48), channel_id=1, source_target_pairs={{0,2},{1,7},{2,0},{3,5},{4,6},{5,3},{6,4},{7,1},{8,10},{9,15},{10,... | collective-permute-start | bytes 1179656 | tf_op jit(solution)/shard_map/ppermute | solution.py:63
  20.1 10.3 %collective-permute-start.6 = (f32[32,2560]{1,0:T(8,128)S(1)}, f32[32,2560]{1,0:T(8,128)S(1)}, u32[]{:S(2)}, u32[]{:S(2)}) collective-permute-start(f32[32,2560]{1,0:T(8,128)S(1)} %get-tuple-element.60), channel_id=1, source_target_pairs={{0,2},{1,7},{2,0},{3,5},{4,6},{5,3},{6,4},{7,1},{8,10},{9,15},{10,... | collective-permute-start | bytes 983048 | tf_op jit(solution)/shard_map/ppermute | solution.py:63
  26.1 9.1 %collective-permute-start.2 = (f32[32,3072]{1,0:T(8,128)S(1)}, f32[32,3072]{1,0:T(8,128)S(1)}, u32[]{:S(2)}, u32[]{:S(2)}) collective-permute-start(f32[32,3072]{1,0:T(8,128)S(1)} %shard_map.43.a_ref), channel_id=1, source_target_pairs={{0,6},{1,3},{2,4},{3,1},{4,2},{5,7},{6,0},{7,5},{8,14},{9,11},{10,... | collective-permute-start | bytes 1179656 | tf_op jit(solution)/shard_map/ppermute | solution.py:63
  30.4 8.4 %collective-permute-start.7 = (f32[32,2560]{1,0:T(8,128)S(1)}, f32[32,2560]{1,0:T(8,128)S(1)}, u32[]{:S(2)}, u32[]{:S(2)}) collective-permute-start(f32[32,2560]{1,0:T(8,128)S(1)} %shard_map.47.middle_ref), channel_id=1, source_target_pairs={{0,6},{1,3},{2,4},{3,1},{4,2},{5,7},{6,0},{7,5},{8,14},{9,11},{10,... | collective-permute-start | bytes 983048 | tf_op jit(solution)/shard_map/ppermute | solution.py:63
  35.3 5.9 %collective-permute-start.3 = (f32[32,1536]{1,0:T(8,128)S(1)}, f32[32,1536]{1,0:T(8,128)S(1)}, u32[]{:S(2)}, u32[]{:S(2)}) collective-permute-start(f32[32,1536]{1,0:T(8,128)S(1)} %get-tuple-element.51), channel_id=1, source_target_pairs={{0,8},{8,0},{16,24},{24,16},{32,40},{40,32},{48,56},{56,48},{64,72... | collective-permute-start | bytes 589832 | tf_op jit(solution)/shard_map/ppermute | solution.py:71
  37.4 3.8 %collective-permute-start.4 = (f32[32,1536]{1,0:T(8,128)S(1)}, f32[32,1536]{1,0:T(8,128)S(1)}, u32[]{:S(2)}, u32[]{:S(2)}) collective-permute-start(f32[32,1536]{1,0:T(8,128)S(1)} %get-tuple-element.52), channel_id=1, source_target_pairs={{8,16},{16,8},{24,32},{32,24},{40,48},{48,40},{56,64},{64,56},{72,... | collective-permute-start | bytes 589832 | tf_op jit(solution)/shard_map/ppermute | solution.py:71
  41.3 2.3 %collective-permute-start.9 = (f32[32,5632]{1,0:T(8,128)S(1)}, f32[32,5632]{1,0:T(8,128)S(1)}, u32[]{:S(2)}, u32[]{:S(2)}) collective-permute-start(f32[32,5632]{1,0:T(8,128)S(1)} %shard_map.48.mine_ref.refs_0_), channel_id=1, source_target_pairs={{0,1},{1,0},{2,3},{3,2},{4,5},{5,4},{6,7},{7,6},{8,9},{9,8},{10,11... | collective-permute-start | bytes 2162696 | tf_op jit(solution)/shard_map/ppermute | solution.py:421
  41.4 11.4 %collective-permute-start.8 = (f32[32,5632]{1,0:T(8,128)S(1)}, f32[32,5632]{1,0:T(8,128)S(1)}, u32[]{:S(2)}, u32[]{:S(2)}) collective-permute-start(f32[32,5632]{1,0:T(8,128)S(1)} %shard_map.48.mine_ref.refs_0_), channel_id=1, source_target_pairs={{0,2},{1,7},{2,0},{3,5},{4,6},{5,3},{6,4},{7,1},{8,10},{9,15},{10,... | collective-permute-start | bytes 2162696 | tf_op jit(solution)/shard_map/ppermute | solution.py:63
  52.7 7.9 %collective-permute-start.11 = (f32[32,5632]{1,0:T(8,128)S(1)}, f32[32,5632]{1,0:T(8,128)S(1)}, u32[]{:S(2)}, u32[]{:S(2)}) collective-permute-start(f32[32,5632]{1,0:T(8,128)S(1)} %collective-permute-done.8.mine_ref.refs_2_), channel_id=1, source_target_pairs={{0,1},{1,0},{2,3},{3,2},{4,5},{5,4},{6,7},{7,6},{8,9},{9,8},{10,11... | collective-permute-start | bytes 2162696 | tf_op jit(solution)/shard_map/ppermute | solution.py:426
  53.3 16.6 %collective-permute-start.10 = (f32[512,256]{1,0:T(8,128)S(1)}, f32[512,256]{1,0:T(8,128)S(1)}, u32[]{:S(2)}, u32[]{:S(2)}) collective-permute-start(f32[512,256]{1,0:T(8,128)S(1)} %get-tuple-element.64), channel_id=1, source_target_pairs={{0,32},{1,97},{2,34},{3,99},{4,36},{5,101},{6,38},{7,103},{8,40},{... | collective-permute-start | bytes 1572872 | tf_op jit(solution)/shard_map/ppermute | solution.py:63
  67.9 9.3 %collective-permute-start.13 = (f32[512,256]{1,0:T(8,128)S(1)}, f32[512,256]{1,0:T(8,128)S(1)}, u32[]{:S(2)}, u32[]{:S(2)}) collective-permute-start(f32[512,256]{1,0:T(8,128)S(1)} %get-tuple-element.66), channel_id=1, source_target_pairs={{0,32},{1,97},{2,34},{3,99},{4,36},{5,101},{6,38},{7,103},{8,40},{... | collective-permute-start | bytes 1572872 | tf_op jit(solution)/shard_map/ppermute | solution.py:63
  71.0 7.2 %collective-permute-start.12 = (f32[320,256]{1,0:T(8,128)S(1)}, f32[320,256]{1,0:T(8,128)S(1)}, u32[]{:S(2)}, u32[]{:S(2)}) collective-permute-start(f32[320,256]{1,0:T(8,128)S(1)} %get-tuple-element.69), channel_id=1, source_target_pairs={{0,8},{1,25},{2,10},{3,27},{4,12},{5,29},{6,14},{7,31},{8,0},{9,17... | collective-permute-start | bytes 983048 | tf_op jit(solution)/shard_map/ppermute | solution.py:63
  77.3 7.0 %collective-permute-start.15 = (f32[256,256]{1,0:T(8,128)S(1)}, f32[256,256]{1,0:T(8,128)S(1)}, u32[]{:S(2)}, u32[]{:S(2)}) collective-permute-start(f32[256,256]{1,0:T(8,128)S(1)} %get-tuple-element.72), channel_id=1, source_target_pairs={{0,8},{1,25},{2,10},{3,27},{4,12},{5,29},{6,14},{7,31},{8,0},{9,17... | collective-permute-start | bytes 786440 | tf_op jit(solution)/shard_map/ppermute | solution.py:63
  78.2 11.0 %collective-permute-start.14 = (f32[320,256]{1,0:T(8,128)S(1)}, f32[320,256]{1,0:T(8,128)S(1)}, u32[]{:S(2)}, u32[]{:S(2)}) collective-permute-start(f32[320,256]{1,0:T(8,128)S(1)} %shard_map.53.a_ref), channel_id=1, source_target_pairs={{0,24},{1,9},{2,26},{3,11},{4,28},{5,13},{6,30},{7,15},{8,16},{9,1... | collective-permute-start | bytes 983048 | tf_op jit(solution)/shard_map/ppermute | solution.py:63
  84.3 9.2 %collective-permute-start.17 = (f32[256,256]{1,0:T(8,128)S(1)}, f32[256,256]{1,0:T(8,128)S(1)}, u32[]{:S(2)}, u32[]{:S(2)}) collective-permute-start(f32[256,256]{1,0:T(8,128)S(1)} %shard_map.54.a_ref), channel_id=1, source_target_pairs={{0,24},{1,9},{2,26},{3,11},{4,28},{5,13},{6,30},{7,15},{8,16},{9,1... | collective-permute-start | bytes 786440 | tf_op jit(solution)/shard_map/ppermute | solution.py:63
  89.2 8.4 %collective-permute-start.16 = (f32[320,256]{1,0:T(8,128)S(1)}, f32[320,256]{1,0:T(8,128)S(1)}, u32[]{:S(2)}, u32[]{:S(2)}) collective-permute-start(f32[320,256]{1,0:T(8,128)S(1)} %shard_map.55.a_ref), channel_id=1, source_target_pairs={{0,96},{1,33},{2,98},{3,35},{4,100},{5,37},{6,102},{7,39},{8,104},... | collective-permute-start | bytes 983048 | tf_op jit(solution)/shard_map/ppermute | solution.py:63
  93.5 8.2 %collective-permute-start.20 = (f32[256,256]{1,0:T(8,128)S(1)}, f32[256,256]{1,0:T(8,128)S(1)}, u32[]{:S(2)}, u32[]{:S(2)}) collective-permute-start(f32[256,256]{1,0:T(8,128)S(1)} %shard_map.56.a_ref), channel_id=1, source_target_pairs={{0,96},{1,33},{2,98},{3,35},{4,100},{5,37},{6,102},{7,39},{8,104},... | collective-permute-start | bytes 786440 | tf_op jit(solution)/shard_map/ppermute | solution.py:63
  97.6 11.7 %collective-permute-start.18 = (f32[64,256]{1,0:T(8,128)S(1)}, f32[64,256]{1,0:T(8,128)S(1)}, u32[]{:S(2)}, u32[]{:S(2)}) collective-permute-start(f32[64,256]{1,0:T(8,128)S(1)} %get-tuple-element.79.a_ref), channel_id=1, source_target_pairs={{0,32},{1,97},{2,34},{3,99},{4,36},{5,101},{6,38},{7,103},{8,40},{... | collective-permute-start | bytes 196616 | tf_op jit(solution)/shard_map/ppermute | solution.py:63
  98.4 6.4 %collective-permute-start.19 = (f32[256,256]{1,0:T(8,128)S(1)}, f32[256,256]{1,0:T(8,128)S(1)}, u32[]{:S(2)}, u32[]{:S(2)}) collective-permute-start(f32[256,256]{1,0:T(8,128)S(1)} %get-tuple-element.80.a_ref), channel_id=1, source_target_pairs={{0,8},{1,25},{2,10},{3,27},{4,12},{5,29},{6,14},{7,31},{8,0},{9,17... | collective-permute-start | bytes 786440 | tf_op jit(solution)/shard_map/ppermute | solution.py:63
  101.8 6.5 %collective-permute-start.22 = (f32[256,256]{1,0:T(8,128)S(1)}, f32[256,256]{1,0:T(8,128)S(1)}, u32[]{:S(2)}, u32[]{:S(2)}) collective-permute-start(f32[256,256]{1,0:T(8,128)S(1)} %shard_map.60.a_ref), channel_id=1, source_target_pairs={{0,8},{1,25},{2,10},{3,27},{4,12},{5,29},{6,14},{7,31},{8,0},{9,17... | collective-permute-start | bytes 786440 | tf_op jit(solution)/shard_map/ppermute | solution.py:63
  104.9 9.3 %collective-permute-start.21 = (f32[512,256]{1,0:T(8,128)S(1)}, f32[512,256]{1,0:T(8,128)S(1)}, u32[]{:S(2)}, u32[]{:S(2)}) collective-permute-start(f32[512,256]{1,0:T(8,128)S(1)} %shard_map.61.refs_4_), channel_id=1, source_target_pairs={{0,32},{1,97},{2,34},{3,99},{4,36},{5,101},{6,38},{7,103},{8,40},{... | collective-permute-start | bytes 1572872 | tf_op jit(solution)/shard_map/ppermute | solution.py:63
  108.3 11.4 %collective-permute-start.23 = (f32[512,256]{1,0:T(8,128)S(1)}, f32[512,256]{1,0:T(8,128)S(1)}, u32[]{:S(2)}, u32[]{:S(2)}) collective-permute-start(f32[512,256]{1,0:T(8,128)S(1)} %shard_map.62.refs_6_), channel_id=1, source_target_pairs={{0,32},{1,97},{2,34},{3,99},{4,36},{5,101},{6,38},{7,103},{8,40},{... | collective-permute-start | bytes 1572872 | tf_op jit(solution)/shard_map/ppermute | solution.py:63
